TPU v7x, 32 devices: a whole 2x2x4 slice. The times are simulated.
32 devices in a mesh: dp: 8 (over z, y), mp: 4 (over x, core).
Axes of the slice: x: 2, y: 2, z: 4, core: 2. Of those that a mesh axis runs over, the one named last changes fastest.
Arguments:
- features: bfloat16 [32768, 512], P('dp', 'mp'), may hold values from -6 to 6
- lengths: int32 [8, 16], P('dp'), may hold values from 1 to 2048, 4096 in all within a row
- enc_conv3: bfloat16 [3, 512, 512], P(None, None, 'mp'), may hold values from -0.15625 to 0.15625
- enc_bias3: bfloat16 [512], P('mp'), may hold values from -3 to 3
- enc_conv1: bfloat16 [512, 512], P(None, 'mp'), may hold values from -0.5 to 0.5
- enc_bias1: bfloat16 [512], P('mp'), may hold values from -3 to 3
- codebooks: bfloat16 [2, 2, 1024, 256], replicated, may hold values from -3 to 3
- dec_conv3: bfloat16 [3, 512, 512], P(None, None, 'mp'), may hold values from -0.15625 to 0.15625
- dec_bias3: bfloat16 [512], P('mp'), may hold values from -3 to 3
- dec_conv1: bfloat16 [512, 512], P(None, 'mp'), may hold values from -0.5 to 0.5
- code_buffer: bfloat16 [1024, 512], replicated, may hold values from -6 to 6
- buffer_index: int32 [2, 2, 1024], replicated, may hold values from 0 to 1023
- out_cotangent: bfloat16 [32768, 512], P('dp', 'mp'), may hold values from -6 to 6
Outputs:
- grad_features: float32 [32768, 512], P('dp', 'mp')
- grad_enc_conv3: float32 [3, 512, 512], P(None, None, 'mp')
- grad_enc_bias3: float32 [512], P('mp')
- grad_enc_conv1: float32 [512, 512], P(None, 'mp')
- grad_enc_bias1: float32 [512], P('mp')
- grad_dec_conv3: float32 [3, 512, 512], P(None, None, 'mp')
- grad_dec_bias3: float32 [512], P('mp')
- grad_dec_conv1: float32 [512, 512], P(None, 'mp')
- grad_dec_bias1: float32 [512], P('mp')
- new_codebooks: float32 [2, 2, 1024, 256], replicated
All inputs are finite; a program needn't handle non-finite values.
Results may differ from a plain program's by a relative error of at most 0.015.
The roundings to bfloat16 on the way count: a program that leaves them out, or rounds other values in their place, can miss the bound.
Values may be sent and summed in bfloat16 or wider, within the bound.
No kernel may reach another device: no remote copies, remote signals or barrier semaphores. Data moves between devices by JAX's collectives and lax.ppermute only.
A program may use at most 192 MiB of HBM per device.

v0:
```python
import jax
import jax.numpy as jnp
from jax import lax
from jax.sharding import PartitionSpec as P

SOFTMAX_WARMTH = 8.0
THRESHOLD = 0.7
SHARPNESS = 4.0
STEP_SCALE = 0.5


def elu_fn(values):
    return jnp.where(values > 0, values, jnp.expm1(jnp.minimum(values, 0.0)))


def elu_slope(values):
    return jnp.where(values > 0, 1.0, jnp.exp(jnp.minimum(values, 0.0)))


def matrix_product(left_side, right_side):
    return jnp.dot(left_side, right_side, preferred_element_type=jnp.float32)


def shifted_taps(values, prev_ok, next_ok):
    zero_row = jnp.zeros((1, values.shape[1]), values.dtype)
    before = jnp.where(prev_ok[:, None] > 0, jnp.concatenate([zero_row, values[:-1]], 0), zero_row)
    after_tap = jnp.where(
        next_ok[:, None] > 0, jnp.concatenate([values[1:], zero_row], 0), zero_row
    )
    return (before, after_tap)


def conv_forward(values, weight, bias_row, prev_ok, next_ok):
    before, after_tap = shifted_taps(values, prev_ok, next_ok)
    return (
        matrix_product(before, weight[0])
        + matrix_product(values, weight[1])
        + matrix_product(after_tap, weight[2])
        + bias_row.astype(jnp.float32)
    )


def taps_weight_grad(before, values, after_tap, grad_out):
    return jnp.stack(
        [
            jnp.einsum("fd,fc->dc", before, grad_out, preferred_element_type=jnp.float32),
            jnp.einsum("fd,fc->dc", values, grad_out, preferred_element_type=jnp.float32),
            jnp.einsum("fd,fc->dc", after_tap, grad_out, preferred_element_type=jnp.float32),
        ]
    )


def conv_weight_grad(values, grad_out, prev_ok, next_ok):
    before, after_tap = shifted_taps(values, prev_ok, next_ok)
    return taps_weight_grad(before, values, after_tap, grad_out)


def conv_input_grad(grad_out, weight, prev_ok, next_ok):
    through_before = (
        jnp.einsum("fc,dc->fd", grad_out, weight[0], preferred_element_type=jnp.float32)
        * prev_ok[:, None]
    )
    through_middle = jnp.einsum(
        "fc,dc->fd", grad_out, weight[1], preferred_element_type=jnp.float32
    )
    through_after = (
        jnp.einsum("fc,dc->fd", grad_out, weight[2], preferred_element_type=jnp.float32)
        * next_ok[:, None]
    )
    zero_row = jnp.zeros((1, through_middle.shape[1]), jnp.float32)
    return (
        through_middle
        + jnp.concatenate([through_before[1:], zero_row], 0)
        + jnp.concatenate([zero_row, through_after[:-1]], 0)
    )


def softmax_rows(distance_scores):
    row_peak = jnp.max(distance_scores, axis=1, keepdims=True)
    exp_terms = jnp.exp(distance_scores - row_peak)
    return exp_terms / jnp.sum(exp_terms, axis=1, keepdims=True)


def quantize_forward(latent_frames, codebooks):
    groups, levels, num_codes, group_dim = codebooks.shape
    saved = []
    usage_rows = []
    quant_parts = []
    for group_idx in range(groups):
        remain = latent_frames[:, group_idx * group_dim : (group_idx + 1) * group_dim].astype(
            jnp.float32
        )
        summed = jnp.zeros_like(remain)
        for level_idx in range(levels):
            code_table_entries = codebooks[group_idx, level_idx]
            book_f = code_table_entries.astype(jnp.float32)
            current_residual = remain.astype(jnp.bfloat16)
            distance_scores = (
                2.0
                * jnp.einsum(
                    "nd,kd->nk",
                    current_residual,
                    code_table_entries,
                    preferred_element_type=jnp.float32,
                )
                - jnp.sum(book_f * book_f, axis=1)[None, :]
            ) / SOFTMAX_WARMTH
            probab = softmax_rows(distance_scores)
            probab_low = probab.astype(jnp.bfloat16)
            picked = matrix_product(probab_low, code_table_entries)
            usage_rows.append(jnp.sum(probab, axis=0))
            saved.append((current_residual, probab, probab_low))
            remain = remain - picked
            summed = summed + picked
        quant_parts.append(summed)
    quant = jnp.concatenate(quant_parts, axis=1).astype(jnp.bfloat16)
    usage_stack = jnp.stack(usage_rows).reshape(groups, levels, num_codes)
    return (quant, saved, usage_stack)


def quantize_backward(grad_quant, saved, codebooks):
    groups, levels, num_codes, group_dim = codebooks.shape
    grad_parts = []
    book_grads = []
    for group_idx in range(groups):
        grad_group = grad_quant[:, group_idx * group_dim : (group_idx + 1) * group_dim]
        grad_remain = jnp.zeros_like(grad_group)
        level_grads = []
        for level_idx in reversed(range(levels)):
            current_residual, probab, probab_low = saved[group_idx * levels + level_idx]
            code_table_entries = codebooks[group_idx, level_idx]
            book_f = code_table_entries.astype(jnp.float32)
            grad_picked = (grad_group - grad_remain).astype(jnp.bfloat16)
            grad_probab = jnp.einsum(
                "nd,kd->nk", grad_picked, code_table_entries, preferred_element_type=jnp.float32
            )
            grad_scores = probab * (
                grad_probab - jnp.sum(probab * grad_probab, axis=1, keepdims=True)
            )
            scores_reduced = grad_scores.astype(jnp.bfloat16)
            grad_current = matrix_product(scores_reduced, code_table_entries) * (
                2.0 / SOFTMAX_WARMTH
            )
            grad_table = jnp.einsum(
                "nk,nd->kd", probab_low, grad_picked, preferred_element_type=jnp.float32
            )
            grad_table = grad_table + 2.0 / SOFTMAX_WARMTH * jnp.einsum(
                "nk,nd->kd", scores_reduced, current_residual, preferred_element_type=jnp.float32
            )
            grad_table = (
                grad_table
                - 2.0
                / SOFTMAX_WARMTH
                * jnp.sum(scores_reduced.astype(jnp.float32), axis=0)[:, None]
                * book_f
            )
            level_grads.append(grad_table)
            grad_remain = grad_remain + grad_current
        grad_parts.append(grad_remain)
        book_grads.append(jnp.stack(level_grads[::-1]))
    return (jnp.concatenate(grad_parts, axis=1).astype(jnp.bfloat16), jnp.stack(book_grads))


def refresh_codes(
    books_f, code_grads, usage_sum, table_rows, group_ids, frames_all, num_codes, groups, group_dim
):
    ratio = usage_sum * (num_codes / frames_all)
    refresh = jax.nn.sigmoid(SHARPNESS * (THRESHOLD - ratio))[:, None]
    stepped = books_f - STEP_SCALE * (num_codes / frames_all) * code_grads
    halves = table_rows.reshape(table_rows.shape[0], groups, group_dim)
    select = (group_ids[:, None] == jnp.arange(groups, dtype=jnp.int32)[None, :]).astype(
        jnp.float32
    )
    chosen = jnp.sum(select[:, :, None] * halves, axis=1)
    return (1.0 - refresh) * stepped + refresh * chosen


def body(
    features,
    lengths,
    enc_conv3,
    enc_bias3,
    enc_conv1,
    enc_bias1,
    codebooks,
    dec_conv3,
    dec_bias3,
    dec_conv1,
    code_buffer,
    buffer_index,
    out_cotangent,
):
    frames = features.shape[0]
    shard_width = features.shape[1]
    groups, levels, num_codes, group_dim = codebooks.shape
    mp_index = lax.axis_index("mp")
    clip_ends = jnp.cumsum(lengths[0])
    starts = clip_ends - lengths[0]
    positions = jnp.arange(frames, dtype=jnp.int32)
    is_start = jnp.any(positions[:, None] == starts[None, :], axis=1)
    prev_ok = jnp.where(is_start, 0.0, 1.0).astype(jnp.float32)
    next_ok = jnp.concatenate([prev_ok[1:], jnp.zeros((1,), jnp.float32)])
    feat_f = features.astype(jnp.float32)
    act_in = elu_fn(feat_f).astype(jnp.bfloat16)
    act_in_all = lax.all_gather(act_in, "mp", axis=1, tiled=True)
    hidden_enc = conv_forward(act_in_all, enc_conv3, enc_bias3, prev_ok, next_ok)
    act_mid = elu_fn(hidden_enc).astype(jnp.bfloat16)
    act_mid_all = lax.all_gather(act_mid, "mp", axis=1, tiled=True)
    latent = feat_f + matrix_product(act_mid_all, enc_conv1) + enc_bias1.astype(jnp.float32)
    latent_frames = lax.all_to_all(
        latent.astype(jnp.bfloat16), "mp", split_axis=0, concat_axis=1, tiled=True
    )
    quant, saved, usage_stack = quantize_forward(latent_frames, codebooks)
    quant_all = lax.all_gather(quant, "mp", axis=0, tiled=True)
    quant_f = quant_all.astype(jnp.float32)
    act_dec = elu_fn(quant_f).astype(jnp.bfloat16)
    hidden_dec = conv_forward(act_dec, dec_conv3, dec_bias3, prev_ok, next_ok)
    act_dec_mid = elu_fn(hidden_dec).astype(jnp.bfloat16)
    act_dec_mid_all = lax.all_gather(act_dec_mid, "mp", axis=1, tiled=True)
    cot_f = out_cotangent.astype(jnp.float32)
    grad_dec_conv1 = jnp.einsum(
        "fd,fc->dc", act_dec_mid_all, out_cotangent, preferred_element_type=jnp.float32
    )
    grad_dec_bias1 = jnp.sum(cot_f, axis=0)
    partial_dec_mid = jnp.einsum(
        "fc,dc->fd", out_cotangent, dec_conv1, preferred_element_type=jnp.float32
    )
    grad_dec_mid = lax.psum_scatter(partial_dec_mid, "mp", scatter_dimension=1, tiled=True)
    grad_hidden_dec = (grad_dec_mid * elu_slope(hidden_dec)).astype(jnp.bfloat16)
    grad_dec_conv3 = conv_weight_grad(act_dec, grad_hidden_dec, prev_ok, next_ok)
    grad_dec_bias3 = jnp.sum(grad_hidden_dec.astype(jnp.float32), axis=0)
    partial_quant = conv_input_grad(grad_hidden_dec, dec_conv3, prev_ok, next_ok) * elu_slope(
        quant_f
    )
    own_cot = lax.dynamic_update_slice(
        jnp.zeros_like(partial_quant), cot_f, (jnp.int32(0), mp_index * shard_width)
    )
    grad_quant = lax.psum_scatter(partial_quant + own_cot, "mp", scatter_dimension=0, tiled=True)
    grad_latent_frames, grad_books = quantize_backward(grad_quant, saved, codebooks)
    grad_latent = lax.all_to_all(grad_latent_frames, "mp", split_axis=1, concat_axis=0, tiled=True)
    grad_enc_conv1 = jnp.einsum(
        "fd,fc->dc", act_mid_all, grad_latent, preferred_element_type=jnp.float32
    )
    grad_enc_bias1 = jnp.sum(grad_latent.astype(jnp.float32), axis=0)
    partial_enc_mid = jnp.einsum(
        "fc,dc->fd", grad_latent, enc_conv1, preferred_element_type=jnp.float32
    )
    grad_act_mid = lax.psum_scatter(partial_enc_mid, "mp", scatter_dimension=1, tiled=True)
    grad_hidden_enc = (grad_act_mid * elu_slope(hidden_enc)).astype(jnp.bfloat16)
    grad_enc_conv3 = conv_weight_grad(act_in_all, grad_hidden_enc, prev_ok, next_ok)
    grad_enc_bias3 = jnp.sum(grad_hidden_enc.astype(jnp.float32), axis=0)
    partial_enc_in = conv_input_grad(grad_hidden_enc, enc_conv3, prev_ok, next_ok)
    grad_act_in = lax.psum_scatter(
        partial_enc_in.astype(jnp.bfloat16), "mp", scatter_dimension=1, tiled=True
    ).astype(jnp.float32)
    grad_features = grad_latent.astype(jnp.float32) + grad_act_in * elu_slope(feat_f)
    summed_grads = lax.psum(
        (
            grad_enc_conv3,
            grad_enc_bias3,
            grad_enc_conv1,
            grad_enc_bias1,
            grad_dec_conv3,
            grad_dec_bias3,
            grad_dec_conv1,
            grad_dec_bias1,
        ),
        "dp",
    )
    total_rows = groups * levels * num_codes
    frames_all = frames * lax.axis_size("dp")
    flat_books = codebooks.reshape(total_rows, group_dim)
    flat_index = buffer_index.reshape(total_rows)
    code_grads, usage_all = lax.psum((grad_books, usage_stack), ("dp", "mp"))
    group_ids = jnp.arange(total_rows, dtype=jnp.int32) // (levels * num_codes)
    table_rows = code_buffer[flat_index].astype(jnp.float32)
    fresh = refresh_codes(
        flat_books.astype(jnp.float32),
        code_grads.reshape(total_rows, group_dim),
        usage_all.reshape(total_rows),
        table_rows,
        group_ids,
        frames_all,
        num_codes,
        groups,
        group_dim,
    )
    new_codebooks = fresh.reshape(groups, levels, num_codes, group_dim)
    return (
        grad_features,
        summed_grads[0],
        summed_grads[1],
        summed_grads[2],
        summed_grads[3],
        summed_grads[4],
        summed_grads[5],
        summed_grads[6],
        summed_grads[7],
        new_codebooks,
    )


def solution(mesh):
    return jax.shard_map(
        body,
        mesh=mesh,
        in_specs=(
            P("dp", "mp"),
            P("dp", None),
            P(None, None, "mp"),
            P("mp"),
            P(None, "mp"),
            P("mp"),
            P(),
            P(None, None, "mp"),
            P("mp"),
            P(None, "mp"),
            P(),
            P(),
            P("dp", "mp"),
        ),
        out_specs=(
            P("dp", "mp"),
            P(None, None, "mp"),
            P("mp"),
            P(None, "mp"),
            P("mp"),
            P(None, None, "mp"),
            P("mp"),
            P(None, "mp"),
            P("mp"),
            P(),
        ),
        check_vma=False,
    )
```

profile of v0, /device:TPU:0, one launch (start us, length us, event | category | flops | bytes accessed | tf_op | source)
XLA Modules:
  0.0 830.0 jit_solution(14503458661189977418)
XLA Ops:
  14.1 34.2 %all-gather.5.cloned.1.call-done = bf16[4096,512]{1,0:T(8,128)(2,1)} async-done(((bf16[4096,128]{1,0:T(8,128)(2,1)}), bf16[4096,512]{1,0:T(8,128)(2,1)}) %all-gather.5.cloned.1.call-update) | async-done | bytes 4194320 | tf_op jit(solution)/shard_map/all_gather | solution.py:205
  48.3 4.1 fusion.176
  63.0 34.5 %all-gather.7.cloned.1.call-done = bf16[4096,512]{1,0:T(8,128)(2,1)} async-done(((bf16[4096,128]{1,0:T(8,128)(2,1)}), bf16[4096,512]{1,0:T(8,128)(2,1)}) %all-gather.7.cloned.1.call-update) | async-done | bytes 4194320 | tf_op jit(solution)/shard_map/all_gather | solution.py:208
  97.5 4.8 fusion.8
  102.3 4.2 all-to-all-start
  107.3 13.8 %all-to-all-done = bf16[4,1024,128]{2,1,0:T(8,128)(2,1)} async-done(((bf16[4,1024,128]{2,1,0:T(8,128)(2,1)}), bf16[4,1024,128]{2,1,0:T(8,128)(2,1)}, u32[]{:S(2)}, u32[]{:S(2)}) %all-to-all-start) | async-done | bytes 1048608 | tf_op jit(solution)/shard_map/all_to_all | solution.py:210
  153.6 5.8 fusion.177
  161.2 27.0 %all-gather.9.cloned.1.call-done = bf16[4096,512]{1,0:T(8,128)(2,1)} async-done(((bf16[1024,512]{1,0:T(8,128)(2,1)}), bf16[4096,512]{1,0:T(8,128)(2,1)}) %all-gather.9.cloned.1.call-update) | async-done | bytes 4194320 | tf_op jit(solution)/shard_map/all_gather | solution.py:214
  188.2 5.6 fusion.4
  193.8 11.5 %fusion.175 = (bf16[4095,512]{1,0:T(8,128)(2,1)}, bf16[4095,512]{1,0:T(8,128)(2,1)S(1)}) fusion(bf16[4096,512]{1,0:T(8,128)(2,1)S(1)} %fusion.4), kind=kLoop, calls=%fused_computation.278 | loop fusion | bytes 16773120 | tf_op jit(solution)/shard_map/slice | solution.py:28
  209.1 5.0 convolution_add_fusion.1
  214.1 48.3 %reduce-scatter.7.cloned.1.call-done = f32[4096,128]{1,0:T(8,128)} async-done(((f32[4096,512]{1,0:T(8,128)}), f32[4096,128]{1,0:T(8,128)}) %reduce-scatter.7.cloned.1.call-update) | async-done | bytes 2097168 | tf_op jit(solution)/shard_map/reduce_scatter | solution.py:228
  262.3 6.0 convert_reduce_fusion.5
  272.7 7.7 fusion.3
  280.4 4.0 convert_reduce_fusion.4
  284.6 71.8 %reduce-scatter.9.cloned.1.call-done = f32[1024,512]{1,0:T(8,128)} async-done(((f32[4096,512]{1,0:T(8,128)}), f32[1024,512]{1,0:T(8,128)}) %reduce-scatter.9.cloned.1.call-update) | async-done | bytes 2097168 | tf_op jit(solution)/shard_map/reduce_scatter | solution.py:238
  356.4 4.1 fusion.172
  381.9 16.9 %all_to_all.35 = bf16[1024,4,128]{2,0,1:T(8,128)(2,1)S(1)} all-to-all(bf16[1024,4,128]{2,0,1:T(8,128)(2,1)S(1)} %pad_maximum_fusion.2), channel_id=1, replica_groups=mesh['dp'=8,'mp'=4] {'mp'}, dimensions={1} | all-to-all | bytes 2097152 | tf_op jit(solution)/shard_map/all_to_all | solution.py:240
  399.7 4.5 fusion.178
  425.2 51.0 %reduce-scatter.11.cloned.1.call-done = f32[4096,128]{1,0:T(8,128)} async-done(((f32[4096,512]{1,0:T(8,128)}), f32[4096,128]{1,0:T(8,128)}) %reduce-scatter.11.cloned.1.call-update) | async-done | bytes 2097168 | tf_op jit(solution)/shard_map/reduce_scatter | solution.py:248
  486.8 6.4 copy.90
  494.0 17.3 %gather_fusion = bf16[4096,512]{1,0:T(8,128)(2,1)} fusion(bf16[1024,512]{1,0:T(8,128)(2,1)S(1)} %copy-done, s32[4096]{0:T(1024)S(1)} %broadcast_clamp_fusion), kind=kCustom, calls=%fused_computation | custom fusion | bytes 8404992 | tf_op jit(solution)/shard_map/gather | solution.py:276
  511.3 9.7 %reshape.197 = f32[4096,2,256]{2,1,0:T(2,128)} reshape(bf16[4096,512]{1,0:T(8,128)(2,1)} %gather_fusion) | data formatting | bytes 12582912 | tf_op jit(solution)/shard_map/convert_element_type | solution.py:276
  521.7 25.9 %multiply_reduce_fusion = f32[4096,256]{1,0:T(8,128)} fusion(f32[4096,2,256]{2,1,0:T(2,128)} %reshape.197, f32[4096,2]{1,0:T(8,128)S(1)} %fusion.34), kind=kLoop, calls=%fused_computation.13 | loop fusion | flops 3145728 | bytes 12615680 | tf_op jit(solution)/shard_map/reduce_sum | solution.py:174
  556.7 4.9 fusion.180
  561.6 4.2 fusion.179
  573.0 39.7 %psum.78 = f32[2,2,1024]{2,1,0:T(2,128)S(1)} all-reduce(f32[2,2,1024]{2,1,0:T(2,128)S(1)} %reshape.195), channel_id=1, replica_groups=mesh['dp'=8,'mp'=4] {'dp','mp'}, use_global_device_ids=true, to_apply=%region_38.39 | all-reduce | flops 4096 | bytes 32768 | tf_op jit(solution)/shard_map/psum | solution.py:274
  614.5 46.5 %all-reduce.13.cloned.1.call-done = f32[2,2,1024,256]{3,2,1,0:T(8,128)} async-done(((f32[2,2,1024,256]{3,2,1,0:T(8,128)}), f32[2,2,1024,256]{3,2,1,0:T(8,128)}) %all-reduce.13.cloned.1.call-update) | async-done | bytes 4194320 | tf_op jit(solution)/shard_map/psum | solution.py:274
  661.0 5.4 multiply_add_fusion
  666.5 20.1 %all-reduce.8 = (f32[128]{0:T(128)}, f32[128]{0:T(128)}, f32[128]{0:T(128)}, f32[128]{0:T(128)}) all-reduce(f32[128]{0:T(128)S(1)} %copy-done.85, f32[128]{0:T(128)S(1)} %convert_reduce_fusion.6, f32[128]{0:T(128)S(1)} %copy-done.86, f32[128]{0:T(128)S(1)} %copy-done.84), channel_id=1, replica_groups=mesh['dp'=8,'mp'=4] {'dp'}, use_global_device_ids=true, to_apply=%region_24.25 | all-reduce | flops 512 | bytes 4096 | tf_op jit(solution)/shard_map/psum | solution.py:257
  686.5 20.6 %reduce-scatter.13.cloned.1.call-done = bf16[128,4096]{1,0:T(8,128)(2,1)} async-done(((bf16[512,4096]{1,0:T(8,128)(2,1)}), bf16[128,4096]{1,0:T(8,128)(2,1)}) %reduce-scatter.13.cloned.1.call-update) | async-done | bytes 1048592
  712.3 102.9 %all-reduce.15.cloned.1.call-done = (f32[3,512,128]{2,1,0:T(8,128)}, f32[512,128]{1,0:T(8,128)}, f32[3,512,128]{2,1,0:T(8,128)}, f32[512,128]{1,0:T(8,128)}) async-done(((f32[3,512,128]{2,1,0:T(8,128)}, f32[512,128]{1,0:T(8,128)}, f32[3,512,128]{2,1,0:T(8,128)}, f32[512,128]{1,0:T(8,128)}), (f32[3,512,128]{2,1,0:T(8,128)}, f32[512,128]{1,0:T(8,128)}, f32[3,512,128]{2,1,0:T(8,128)}, ...) | async-done | bytes 2097168 | tf_op jit(solution)/shard_map/psum | solution.py:257
  (297 shorter events, 145.6 us)
Async XLA Ops:
  7.2 486.8 %copy-start = (bf16[1024,512]{1,0:T(8,128)(2,1)S(1)}, bf16[1024,512]{1,0:T(8,128)(2,1)}, u32[]{:S(2)}) copy-start(bf16[1024,512]{1,0:T(8,128)(2,1)} %param.23) | copy-start | bytes 3145732
  7.2 41.1 %all-gather.5.cloned.1.call-start = ((), (), s32[]{:S(2)}) async-start(), calls=%async_computation.6 | async-start | bytes 5242880 | tf_op jit(solution)/shard_map/all_gather | solution.py:205
  10.4 87.1 %all-gather.7.cloned.1.call-start = ((), (), s32[]{:S(2)}) async-start(), calls=%async_computation.7 | async-start | bytes 5242880 | tf_op jit(solution)/shard_map/all_gather | solution.py:208
  14.0 38.3 %copy-start.79 = (pred[4096]{0:T(1024)(128)(4,1)}, pred[4096]{0:T(1024)(128)(4,1)S(1)}, u32[]{:S(2)}) copy-start(pred[4096]{0:T(1024)(128)(4,1)S(1)} %broadcast_compare_fusion.1) | copy-start | bytes 12292
  14.0 38.3 %copy-start.55 = (bf16[3,512,128]{2,1,0:T(8,128)(2,1)S(1)}, bf16[3,512,128]{2,1,0:T(8,128)(2,1)}, u32[]{:S(2)}) copy-start(bf16[3,512,128]{2,1,0:T(8,128)(2,1)} %param.15) | copy-start | bytes 1179652
  52.4 6.4 copy-start.50
  63.0 43.6 %copy-start.13 = (bf16[2,2,1024,256]{3,2,1,0:T(8,128)(2,1)S(1)}, bf16[2,2,1024,256]{3,2,1,0:T(8,128)(2,1)}, u32[]{:S(2)}) copy-start(bf16[2,2,1024,256]{3,2,1,0:T(8,128)(2,1)} %param.19) | copy-start | bytes 6291460
  102.3 18.8 %all-to-all-start = ((bf16[4,1024,128]{2,1,0:T(8,128)(2,1)}), bf16[4,1024,128]{2,1,0:T(8,128)(2,1)}, u32[]{:S(2)}, u32[]{:S(2)}) async-start(bf16[4,1024,128]{2,1,0:T(8,128)(2,1)} %bitcast.197), calls=%async_computation | async-start | bytes 2097152 | tf_op jit(solution)/shard_map/all_to_all | solution.py:210
  106.6 81.6 %all-gather.9.cloned.1.call-start = ((), (), s32[]{:S(2)}) async-start(), calls=%async_computation.9 | async-start | bytes 5242880 | tf_op jit(solution)/shard_map/all_gather | solution.py:214
  107.3 37.2 %copy-start.64 = (f32[1024]{0:T(1024)}, f32[1024]{0:T(1024)S(1)}, u32[]{:S(2)}) copy-start(f32[1024]{0:T(1024)S(1)} %get-tuple-element.21) | copy-start | bytes 12292
  107.3 40.9 %copy-start.62 = (f32[1024]{0:T(1024)}, f32[1024]{0:T(1024)S(1)}, u32[]{:S(2)}) copy-start(f32[1024]{0:T(1024)S(1)} %get-tuple-element.18) | copy-start | bytes 12292
  153.5 108.8 %reduce-scatter.7.cloned.1.call-start = ((), (), s32[]{:S(2)}) async-start(), calls=%async_computation.8 | async-start | bytes 10485760 | tf_op jit(solution)/shard_map/reduce_scatter | solution.py:228
  159.4 197.0 %reduce-scatter.9.cloned.1.call-start = ((), (), s32[]{:S(2)}) async-start(), calls=%async_computation.10 | async-start | bytes 10485760 | tf_op jit(solution)/shard_map/reduce_scatter | solution.py:238
  193.8 11.6 %copy-start.58 = (bf16[3,512,128]{2,1,0:T(8,128)(2,1)S(1)}, bf16[3,512,128]{2,1,0:T(8,128)(2,1)}, u32[]{:S(2)}) copy-start(bf16[3,512,128]{2,1,0:T(8,128)(2,1)} %param.20) | copy-start | bytes 1179652
  193.8 11.5 %copy-start.80 = (pred[4096]{0:T(1024)(128)(4,1)S(1)}, pred[4096]{0:T(1024)(128)(4,1)}, u32[]{:S(2)}) copy-start(pred[4096]{0:T(1024)(128)(4,1)} %copy-done.79) | copy-start | bytes 12292
  272.6 7.8 copy-start.30
  284.5 76.0 %copy-start.65 = (f32[1024]{0:T(1024)S(1)}, f32[1024]{0:T(1024)}, u32[]{:S(2)}) copy-start(f32[1024]{0:T(1024)} %copy-done.64) | copy-start | bytes 12292
  284.5 75.9 %copy-start.71 = (f32[1024]{0:T(1024)S(1)}, f32[1024]{0:T(1024)}, u32[]{:S(2)}) copy-start(f32[1024]{0:T(1024)} %copy-done.70) | copy-start | bytes 12292
  284.5 75.9 %copy-start.73 = (f32[1024]{0:T(1024)S(1)}, f32[1024]{0:T(1024)}, u32[]{:S(2)}) copy-start(f32[1024]{0:T(1024)} %copy-done.72) | copy-start | bytes 12292
  284.5 191.6 %reduce-scatter.11.cloned.1.call-start = ((), (), s32[]{:S(2)}) async-start(), calls=%async_computation.11 | async-start | bytes 10485760 | tf_op jit(solution)/shard_map/reduce_scatter | solution.py:248
  370.9 5.9 copy-start.43
  381.2 18.5 %copy-start.57 = (bf16[512,128]{1,0:T(8,128)(2,1)S(1)}, bf16[512,128]{1,0:T(8,128)(2,1)}, u32[]{:S(2)}) copy-start(bf16[512,128]{1,0:T(8,128)(2,1)} %param.17) | copy-start | bytes 393220
  404.3 152.4 %all-gather.11.cloned.1.call-start = ((), (), s32[]{:S(2)}) async-start(), calls=%async_computation.12 | async-start | bytes 5242880 | tf_op jit(solution)/shard_map/all_gather | solution.py:219
  405.0 256.0 %all-reduce.13.cloned.1.call-start = ((), (), s32[]{:S(2)}) async-start(), calls=%async_computation.13 | async-start | bytes 8388608 | tf_op jit(solution)/shard_map/psum | solution.py:274
  425.1 54.4 %copy-start.56 = (bf16[3,512,128]{2,1,0:T(8,128)(2,1)S(1)}, bf16[3,512,128]{2,1,0:T(8,128)(2,1)}, u32[]{:S(2)}) copy-start(bf16[3,512,128]{2,1,0:T(8,128)(2,1)} %param.15) | copy-start | bytes 1179652
  425.1 282.0 %reduce-scatter.13.cloned.1.call-start = ((), (), s32[]{:S(2)}) async-start(), calls=%async_computation.14 | async-start | bytes 5242880
  493.2 322.0 %all-reduce.15.cloned.1.call-start = ((), (), s32[]{:S(2)}) async-start(), calls=%async_computation.15 | async-start | bytes 4194304 | tf_op jit(solution)/shard_map/psum | solution.py:257
  521.7 26.0 %copy-start.27 = (bf16[4096,128]{1,0:T(8,128)(2,1)S(1)}, bf16[4096,128]{1,0:T(8,128)(2,1)}, u32[]{:S(2)}) copy-start(bf16[4096,128]{1,0:T(8,128)(2,1)} %copy-done.26) | copy-start | bytes 3145732
  521.7 26.0 %copy-start.54 = (bf16[4095,512]{1,0:T(8,128)(2,1)S(1)}, bf16[4095,512]{1,0:T(8,128)(2,1)}, u32[]{:S(2)}) copy-start(bf16[4095,512]{1,0:T(8,128)(2,1)} %get-tuple-element.44) | copy-start | bytes 12579844
  521.7 26.0 %copy-start.83 = (pred[4096]{0:T(1024)(128)(4,1)S(1)}, pred[4096]{0:T(1024)(128)(4,1)}, u32[]{:S(2)}) copy-start(pred[4096]{0:T(1024)(128)(4,1)} %broadcast_compare_fusion) | copy-start | bytes 12292
  556.7 9.1 %copy-start.19 = (bf16[4096,128]{1,0:T(8,128)(2,1)S(1)}, bf16[4096,128]{1,0:T(8,128)(2,1)}, u32[]{:S(2)}) copy-start(bf16[4096,128]{1,0:T(8,128)(2,1)} %copy-done.18) | copy-start | bytes 3145732
  556.7 9.1 %copy-start.51 = (bf16[4095,512]{1,0:T(8,128)(2,1)S(1)}, bf16[4095,512]{1,0:T(8,128)(2,1)}, u32[]{:S(2)}) copy-start(bf16[4095,512]{1,0:T(8,128)(2,1)} %copy-done.50) | copy-start | bytes 12579844
  (68 other events, 181.3 us)
Sparse Core Ops, SparseCore 0:
  10.5 37.7 all-gather.4
  62.5 35.0 all-gather.6
  153.7 34.4 all-gather.8
  190.6 71.6 reduce-scatter.6
  284.6 71.7 reduce-scatter.8
  404.4 71.7 reduce-scatter.10
  477.8 35.0 all-gather.10
  519.3 141.6 all-reduce.12
  663.7 43.3 reduce-scatter.12
  711.5 103.6 all-reduce.14
where the time goes:
time: 840 us; the launch traced here: 830 us
  waiting for transfers between devices  452 us (54%)
  matrix products  102 us (12%)
  local copies, waits for them, and re-layouts  96 us (11%)
  other arithmetic  82.8 us (10%)
  blocking collectives  76.6 us (9%)
  between operations  15.8 us (2%)
    psum x1, waiting for transfers between devices, body(): lax.psum((grad_enc_conv3, grad_enc_bias3, grad_enc_conv1, grad_enc_bias1,...  103 us
    reduce_scatter x1, waiting for transfers between devices, body(): lax.psum_scatter(partial_quant + own_cot, 'mp', scatter_dimension=0, tile...  71.8 us
    reduce_scatter x1, waiting for transfers between devices, body(): lax.psum_scatter(partial_enc_mid, 'mp', scatter_dimension=1, tiled=True)  51 us
    reduce_scatter x1, waiting for transfers between devices, body(): lax.psum_scatter(partial_dec_mid, 'mp', scatter_dimension=1, tiled=True)  48.3 us
    psum x1, waiting for transfers between devices, body(): code_grads, usage_all = lax.psum((grad_books, usage_stack), ('dp', 'mp'))  46.5 us
    unnamed x184, local copies, waits for them, and re-layouts  45.7 us
    psum x1, blocking collectives, body(): code_grads, usage_all = lax.psum((grad_books, usage_stack), ('dp', 'mp'))  39.7 us
    all_gather x1, waiting for transfers between devices, body(): act_mid_all = lax.all_gather(act_mid, 'mp', axis=1, tiled=True)  34.5 us
  transfers between devices with their start and end apart: 11, of which 10 were waited for; matrix products, arithmetic and copies ran while one was open for 19% of the time, Pallas kernels for 0%

commit v1 on v0

v1 whole, which is shorter than its diff:
```python
import jax
import jax.numpy as jnp
from jax import lax
from jax.sharding import PartitionSpec as P

SOFTMAX_WARMTH = 8.0
THRESHOLD = 0.7
SHARPNESS = 4.0
STEP_SCALE = 0.5
HALO = 16
BF16 = jnp.bfloat16
F32 = jnp.float32


def elu_fn(values):
    return jnp.where(values > 0, values, jnp.expm1(jnp.minimum(values, 0.0)))


def elu_slope(values):
    return jnp.where(values > 0, 1.0, jnp.exp(jnp.minimum(values, 0.0)))


def dot_nn(left, right):
    return jnp.dot(left, right, preferred_element_type=F32)


def dot_nt(left, right):
    return lax.dot_general(left, right, (((1,), (1,)), ((), ())), preferred_element_type=F32)


def dot_tn(left, right):
    return lax.dot_general(left, right, (((0,), (0,)), ((), ())), preferred_element_type=F32)


def swap(values, axis, bits):
    size = lax.axis_size(axis)
    return lax.ppermute(values, axis, [(i, i ^ bits) for i in range(size)])


def in_order(pieces, place, dim):
    stacked = jnp.stack(pieces)
    return jnp.concatenate(
        [
            lax.dynamic_index_in_dim(stacked, place ^ j, 0, keepdims=False)
            for j in range(len(pieces))
        ],
        dim,
    )


def to_frames(values, me, width, own):
    padded = jnp.pad(values, ((HALO, HALO), (0, 0)))
    pieces = []
    for k in range(width):
        piece = lax.dynamic_slice_in_dim(padded, (me ^ k) * own, own + 2 * HALO, 0)
        pieces.append(swap(piece, "mp", k) if k else piece)
    return in_order(pieces, me, 1)


def to_channels(values, me, width):
    cols = values.shape[1] // width
    pieces = []
    for k in range(width):
        piece = lax.dynamic_slice_in_dim(values, (me ^ k) * cols, cols, 1)
        pieces.append(swap(piece, "mp", k) if k else piece)
    return in_order(pieces, me, 0)


def gather_columns(block, me, width):
    held = [block]
    bit = width // 2
    offsets = [0]
    while bit:
        other = swap(jnp.stack(held), "mp", bit)
        held = held + [other[i] for i in range(len(held))]
        offsets = offsets + [o ^ bit for o in offsets]
        bit //= 2
    ordered = [None] * width
    for piece, offset in zip(held, offsets):
        ordered[offset] = piece
    return in_order(ordered, me, block.ndim - 1)


def exchange_steps(count):
    steps, stride, rest = [], 1, count
    while rest > 1:
        radix = 2 if (rest.bit_length() - 1) % 2 else 4
        steps.append((stride, radix))
        stride, rest = stride * radix, rest // radix
    return steps


def scatter_sum_dp(total, place):
    for stride, radix in exchange_steps(lax.axis_size("dp")):
        digit = (place // stride) % radix
        rows = total.shape[0] // radix
        summed = lax.dynamic_slice_in_dim(total, digit * rows, rows, 0)
        low = total.astype(BF16)
        for k in range(1, radix):
            piece = lax.dynamic_slice_in_dim(low, (digit ^ k) * rows, rows, 0)
            summed = summed + swap(piece, "dp", k * stride).astype(F32)
        total = summed
    return total


def gather_dp(block, place):
    for stride, radix in reversed(exchange_steps(lax.axis_size("dp"))):
        digit = (place // stride) % radix
        pieces = [block] + [swap(block, "dp", k * stride) for k in range(1, radix)]
        block = in_order(pieces, digit, 0)
    return block


def sum_columns(grads, me, width, place):
    cols = grads.shape[1] // width

    def block(offset):
        return lax.dynamic_slice_in_dim(grads, (me ^ offset) * cols, cols, 1)

    held = {k: block(k) for k in range(width)}
    bit = 1
    while bit < width:
        mine = [k for k in sorted(held) if not k & bit]
        other = swap(jnp.stack([held[k ^ bit] for k in mine]).astype(BF16), "mp", bit)
        held = {k: held[k] + other[i].astype(F32) for i, k in enumerate(mine)}
        bit *= 2
    return gather_dp(scatter_sum_dp(held[0], place).astype(BF16), place).astype(F32)


def sum_everywhere(values, width):
    bit = 1
    while bit < width:
        values = values + swap(values, "mp", bit)
        bit *= 2
    bit = 1
    while bit < lax.axis_size("dp"):
        values = values + swap(values, "dp", bit)
        bit *= 2
    return values


def shift_down(values):
    return jnp.concatenate([jnp.zeros_like(values[:1]), values[:-1]], 0)


def shift_up(values):
    return jnp.concatenate([values[1:], jnp.zeros_like(values[:1])], 0)


def taps(values, prev_ok, next_ok):
    zero = jnp.zeros((), values.dtype)
    return (
        jnp.where(prev_ok > 0, shift_down(values), zero),
        values,
        jnp.where(next_ok > 0, shift_up(values), zero),
    )


def conv_forward(values, weight, bias_row, prev_ok, next_ok):
    before, middle, after = taps(values, prev_ok, next_ok)
    return (
        dot_nn(before, weight[0])
        + dot_nn(middle, weight[1])
        + dot_nn(after, weight[2])
        + bias_row.astype(F32)
    )


def conv_input_grad(grad_out, weight, prev_ok, next_ok):
    return (
        dot_nt(grad_out, weight[1])
        + shift_up(dot_nt(grad_out, weight[0]) * prev_ok)
        + shift_down(dot_nt(grad_out, weight[2]) * next_ok)
    )


def body(
    features,
    lengths,
    enc_conv3,
    enc_bias3,
    enc_conv1,
    enc_bias1,
    codebooks,
    dec_conv3,
    dec_bias3,
    dec_conv1,
    code_buffer,
    buffer_index,
    out_cotangent,
):
    frames = features.shape[0]
    groups, levels, num_codes, group_dim = codebooks.shape
    width = lax.axis_size("mp")
    n_dp = lax.axis_size("dp")
    me = lax.axis_index("mp")
    place = lax.axis_index("dp")
    own = frames // width
    own_rows = slice(HALO, HALO + own)

    clip_ends = jnp.cumsum(lengths[0])
    starts = clip_ends - lengths[0]
    positions = me * own - HALO + jnp.arange(own + 2 * HALO + 1, dtype=jnp.int32)
    is_start = jnp.any(positions[:, None] == starts[None, :], axis=1) | (positions == frames)
    ok = jnp.where(is_start, 0.0, 1.0).astype(F32)[:, None]
    prev_ok, next_ok = ok[:-1], ok[1:]

    feat = to_frames(features, me, width, own)
    w_enc3 = gather_columns(enc_conv3, me, width)
    w_enc1 = gather_columns(enc_conv1, me, width)
    biases = gather_columns(jnp.stack([enc_bias3, enc_bias1, dec_bias3]), me, width)
    w_dec1 = gather_columns(dec_conv1, me, width)
    w_dec3 = gather_columns(dec_conv3, me, width)
    cot = to_frames(out_cotangent, me, width, own)

    feat_f = feat.astype(F32)
    act_in = elu_fn(feat_f).astype(BF16)
    hidden_enc = conv_forward(act_in, w_enc3, biases[0], prev_ok, next_ok)
    act_mid = elu_fn(hidden_enc).astype(BF16)
    latent = (feat_f + dot_nn(act_mid, w_enc1) + biases[1].astype(F32)).astype(BF16)

    saved, usage, quant_parts = [], [], []
    for g in range(groups):
        remain = latent[:, g * group_dim : (g + 1) * group_dim].astype(F32)
        summed = jnp.zeros_like(remain)
        for level in range(levels):
            book = codebooks[g, level]
            book_f = book.astype(F32)
            current = remain.astype(BF16)
            scores = (
                2.0 * dot_nt(current, book) - jnp.sum(book_f * book_f, axis=1)[None, :]
            ) / SOFTMAX_WARMTH
            terms = jnp.exp(scores - jnp.max(scores, axis=1, keepdims=True))
            probab = terms / jnp.sum(terms, axis=1, keepdims=True)
            probab_low = probab.astype(BF16)
            picked = dot_nn(probab_low, book)
            usage.append(jnp.sum(probab[own_rows], axis=0))
            saved.append((current, probab, probab_low))
            remain = remain - picked
            summed = summed + picked
        quant_parts.append(summed)
    quant = jnp.concatenate(quant_parts, axis=1).astype(BF16)
    usage_all = sum_everywhere(jnp.stack(usage), width)

    quant_f = quant.astype(F32)
    act_dec = elu_fn(quant_f).astype(BF16)
    hidden_dec = conv_forward(act_dec, w_dec3, biases[2], prev_ok, next_ok)
    act_dec_mid = elu_fn(hidden_dec).astype(BF16)
    cot_own = cot[own_rows]
    grad_dec_conv1 = sum_columns(dot_tn(act_dec_mid[own_rows], cot_own), me, width, place)
    grad_hidden_dec = (dot_nt(cot, w_dec1) * elu_slope(hidden_dec)).astype(BF16)
    grad_dec_conv3 = jnp.concatenate(
        [
            dot_tn(tap[own_rows], grad_hidden_dec[own_rows])
            for tap in taps(act_dec, prev_ok, next_ok)
        ],
        0,
    )
    grad_dec_conv3 = sum_columns(grad_dec_conv3, me, width, place)
    grad_quant = cot.astype(F32) + elu_slope(quant_f) * conv_input_grad(
        grad_hidden_dec, w_dec3, prev_ok, next_ok
    )

    grad_parts, book_grads = [], []
    for g in range(groups):
        grad_group = grad_quant[:, g * group_dim : (g + 1) * group_dim]
        grad_remain = jnp.zeros_like(grad_group)
        level_grads = []
        for level in reversed(range(levels)):
            current, probab, probab_low = saved[g * levels + level]
            book = codebooks[g, level]
            grad_picked = (grad_group - grad_remain).astype(BF16)
            grad_probab = dot_nt(grad_picked, book)
            grad_scores = (
                probab * (grad_probab - jnp.sum(probab * grad_probab, axis=1, keepdims=True))
            ).astype(BF16)
            grad_remain = grad_remain + dot_nn(grad_scores, book) * (2.0 / SOFTMAX_WARMTH)
            own_scores = grad_scores[own_rows]
            table = dot_tn(probab_low[own_rows], grad_picked[own_rows])
            table = table + (2.0 / SOFTMAX_WARMTH) * (
                dot_tn(own_scores, current[own_rows])
                - jnp.sum(own_scores.astype(F32), axis=0)[:, None] * book.astype(F32)
            )
            level_grads.append(table)
        grad_parts.append(grad_remain)
        book_grads.extend(level_grads[::-1])
    grad_latent = jnp.concatenate(grad_parts, axis=1).astype(BF16)

    total_rows = groups * levels * num_codes
    held = jnp.concatenate(book_grads, 0)
    first = jnp.int32(0)
    bit = 1
    while bit < width:
        rows = held.shape[0] // 2
        side = (me // bit) % 2
        sent = lax.dynamic_slice_in_dim(held, (1 - side) * rows, rows, 0).astype(BF16)
        held = lax.dynamic_slice_in_dim(held, side * rows, rows, 0) + swap(
            sent, "mp", bit
        ).astype(F32)
        first = first + side * rows
        bit *= 2
    rows = held.shape[0]
    held = scatter_sum_dp(held, place)
    for stride, radix in exchange_steps(n_dp):
        rows = rows // radix
        first = first + ((place // stride) % radix) * rows
    ratio = lax.dynamic_slice_in_dim(usage_all.reshape(total_rows), first, rows, 0) * (
        num_codes / (frames * n_dp)
    )
    refresh = jax.nn.sigmoid(SHARPNESS * (THRESHOLD - ratio))[:, None]
    own_books = lax.dynamic_slice_in_dim(
        codebooks.reshape(total_rows, group_dim), first, rows, 0
    ).astype(F32)
    stepped = own_books - STEP_SCALE * (num_codes / (frames * n_dp)) * held
    index = lax.dynamic_slice_in_dim(buffer_index.reshape(total_rows), first, rows, 0)
    row_group = (first + jnp.arange(rows, dtype=jnp.int32)) // (levels * num_codes)
    one_hot = (index[:, None] == jnp.arange(code_buffer.shape[0], dtype=jnp.int32)[None, :]).astype(
        BF16
    )
    both = dot_nn(one_hot, code_buffer)
    chosen = jnp.zeros((rows, group_dim), F32)
    for g in range(groups):
        chosen = jnp.where(
            (row_group == g)[:, None], both[:, g * group_dim : (g + 1) * group_dim], chosen
        )
    fresh = ((1.0 - refresh) * stepped + refresh * chosen).astype(BF16)
    fresh = gather_dp(fresh, place)
    bit = width // 2
    while bit:
        side = (me // bit) % 2
        fresh = in_order([fresh, swap(fresh, "mp", bit)], side, 0)
        bit //= 2
    new_codebooks = fresh.astype(F32).reshape(groups, levels, num_codes, group_dim)

    grad_enc_conv1 = sum_columns(
        dot_tn(act_mid[own_rows], grad_latent[own_rows]), me, width, place
    )
    grad_hidden_enc = (dot_nt(grad_latent, w_enc1) * elu_slope(hidden_enc)).astype(BF16)
    grad_enc_conv3 = jnp.concatenate(
        [
            dot_tn(tap[own_rows], grad_hidden_enc[own_rows])
            for tap in taps(act_in, prev_ok, next_ok)
        ],
        0,
    )
    grad_enc_conv3 = sum_columns(grad_enc_conv3, me, width, place)
    grad_features = (
        grad_latent.astype(F32)
        + elu_slope(feat_f) * conv_input_grad(grad_hidden_enc, w_enc3, prev_ok, next_ok)
    )[own_rows].astype(BF16)
    grad_features = to_channels(grad_features, me, width).astype(F32)

    bias_grads = jnp.stack(
        [
            jnp.sum(v[own_rows].astype(F32), axis=0)
            for v in (grad_hidden_enc, grad_latent, grad_hidden_dec, cot)
        ]
    )
    bias_grads = sum_everywhere(bias_grads, width)
    cols = features.shape[1]
    bias_grads = lax.dynamic_slice_in_dim(bias_grads, me * cols, cols, 1)

    return (
        grad_features,
        grad_enc_conv3.reshape(enc_conv3.shape),
        bias_grads[0],
        grad_enc_conv1,
        bias_grads[1],
        grad_dec_conv3.reshape(dec_conv3.shape),
        bias_grads[2],
        grad_dec_conv1,
        bias_grads[3],
        new_codebooks,
    )


def solution(mesh):
    return jax.shard_map(
        body,
        mesh=mesh,
        in_specs=(
            P("dp", "mp"),
            P("dp", None),
            P(None, None, "mp"),
            P("mp"),
            P(None, "mp"),
            P("mp"),
            P(),
            P(None, None, "mp"),
            P("mp"),
            P(None, "mp"),
            P(),
            P(),
            P("dp", "mp"),
        ),
        out_specs=(
            P("dp", "mp"),
            P(None, None, "mp"),
            P("mp"),
            P(None, "mp"),
            P("mp"),
            P(None, None, "mp"),
            P("mp"),
            P(None, "mp"),
            P("mp"),
            P(),
        ),
        check_vma=False,
    )
```

time: 840 us -> 334 us (0.40)
  waiting for transfers between devices: 452 us -> 94.7 us
  starting transfers between devices: 4.83 us -> 89.5 us
  blocking collectives: 76.6 us -> 0 us
  local copies, waits for them, and re-layouts: 96 us -> 25.7 us
  matrix products: 102 us -> 55.1 us
  other arithmetic: 82.8 us -> 60.8 us
  between operations: 15.8 us -> 3.01 us
    reduce_scatter x3 -> x0, waiting for transfers between devices: 171 us -> none  [the longest x1 71.8 us: body(): lax.psum_scatter(partial_quant + own_cot, 'mp', scatter_dimension=0, tile...]
    psum x2 -> x0, waiting for transfers between devices: 149 us -> none  [the longest x1 103 us: body(): lax.psum((grad_enc_conv3, grad_enc_bias3, grad_enc_conv1, grad_enc_bias1,...]
    all_gather x4 -> x0, waiting for transfers between devices: 95.7 us -> none  [the longest x1 34.5 us: body(): act_mid_all = lax.all_gather(act_mid, 'mp', axis=1, tiled=True)]
    ppermute x0 -> x81, waiting for transfers between devices: none -> 94.7 us  [swap(): return lax.ppermute(values, axis, [(i, i ^ bits) for i in range(size)])]
    ppermute x0 -> x81, starting transfers between devices: none -> 89.5 us  [swap(): return lax.ppermute(values, axis, [(i, i ^ bits) for i in range(size)])]
    psum x2 -> x0, blocking collectives: 59.7 us -> none  [the longest x1 39.7 us: body(): code_grads, usage_all = lax.psum((grad_books, usage_stack), ('dp', 'mp'))]
    dot_general x47 -> x48, matrix products: 102 us -> 55.1 us  [the longest x16 22.9 us: dot_tn(): lax.dot_general(left, right, (((0,), (0,)), ((), ())), preferred_element_...]
    reduce_sum x13 -> x17, other arithmetic: 45.3 us -> 10.6 us  [the longest x4 4.32 us: body(): probab = terms / jnp.sum(terms, axis=1, keepdims=True)]
  transfers between devices with their start and end apart: 11 -> 81, of which waited for: 10 -> 32; matrix products, arithmetic and copies ran while one was open for 19% -> 15% of each run, Pallas kernels for 0% -> 0%
where the time goes in v1:
time: 334 us; the launch traced here: 329 us
  waiting for transfers between devices  94.7 us (28%)
  starting transfers between devices  89.5 us (27%)
  other arithmetic  60.8 us (18%)
  matrix products  55.1 us (16%)
  local copies, waits for them, and re-layouts  25.7 us (8%)
    ppermute x81, waiting for transfers between devices, swap(): return lax.ppermute(values, axis, [(i, i ^ bits) for i in range(size)])  94.7 us
    ppermute x81, starting transfers between devices, swap(): return lax.ppermute(values, axis, [(i, i ^ bits) for i in range(size)])  89.5 us
    dot_general x16, matrix products, dot_tn(): lax.dot_general(left, right, (((0,), (0,)), ((), ())), preferred_element_...  22.9 us
    unnamed x165, local copies, waits for them, and re-layouts  17.7 us
    dot_general x16, matrix products, dot_nn(): return jnp.dot(left, right, preferred_element_type=F32)  16.6 us
    dot_general x16, matrix products, dot_nt(): lax.dot_general(left, right, (((1,), (1,)), ((), ())), preferred_element_...  15.7 us
  transfers between devices with their start and end apart: 81, of which 32 were waited for; matrix products, arithmetic and copies ran while one was open for 15% of the time, Pallas kernels for 0%

profile of v1, /device:TPU:0, one launch (start us, length us, event | category | flops | bytes accessed | tf_op | source)
XLA Modules:
  0.0 328.9 jit_solution(16639431737860678638)
XLA Ops:
  2.1 2.9 collective-permute-start.5
  7.1 2.2 fusion.184
  28.9 2.3 convert_minimum_fusion
  32.4 16.6 %collective-permute-done.10 = bf16[1056,128]{1,0:T(8,128)(2,1)S(1)} collective-permute-done((bf16[1056,128]{1,0:T(8,128)(2,1)}, bf16[1056,128]{1,0:T(8,128)(2,1)S(1)}, u32[]{:S(2)}, u32[]{:S(2)}) %collective-permute-start.10) | collective-permute-done | bytes 270368 | tf_op jit(solution)/shard_map/ppermute | solution.py:37
  49.0 5.1 %collective-permute-done.11 = bf16[1056,128]{1,0:T(8,128)(2,1)S(1)} collective-permute-done((bf16[1056,128]{1,0:T(8,128)(2,1)}, bf16[1056,128]{1,0:T(8,128)(2,1)S(1)}, u32[]{:S(2)}, u32[]{:S(2)}) %collective-permute-start.11) | collective-permute-done | bytes 270368 | tf_op jit(solution)/shard_map/ppermute | solution.py:37
  63.5 2.8 fusion.34
  116.8 2.3 convolution_multiply_fusion.7
  139.9 2.1 fusion.173
  175.9 2.9 collective-permute-start.33
  182.3 2.0 collective-permute-done.67
  184.4 2.7 collective-permute-start.68
  194.1 3.4 %collective-permute-done.18 = bf16[1024,128]{1,0:T(8,128)(2,1)S(1)} collective-permute-done((bf16[1024,128]{1,0:T(8,128)(2,1)S(1)}, bf16[1024,128]{1,0:T(8,128)(2,1)S(1)}, u32[]{:S(2)}, u32[]{:S(2)}) %collective-permute-start.18) | collective-permute-done | bytes 262176 | tf_op jit(solution)/shard_map/ppermute | solution.py:37
  207.8 2.5 collective-permute-start.59
  213.3 2.7 collective-permute-start.39
  216.1 2.0 collective-permute-start.62
  224.4 2.4 collective-permute-start.40
  230.8 2.5 collective-permute-done.63
  240.7 8.0 %collective-permute-done.45 = bf16[1,1536,128]{2,1,0:T(8,128)(2,1)S(1)} collective-permute-done((bf16[1,1536,128]{2,1,0:T(8,128)(2,1)S(1)}, bf16[1,1536,128]{2,1,0:T(8,128)(2,1)S(1)}, u32[]{:S(2)}, u32[]{:S(2)}) %collective-permute-start.45) | collective-permute-done | bytes 393248 | tf_op jit(solution)/shard_map/ppermute | solution.py:37
  251.0 6.1 %collective-permute-done.20 = bf16[1,1536,128]{2,1,0:T(8,128)(2,1)S(1)} collective-permute-done((bf16[1,1536,128]{2,1,0:T(8,128)(2,1)S(1)}, bf16[1,1536,128]{2,1,0:T(8,128)(2,1)S(1)}, u32[]{:S(2)}, u32[]{:S(2)}) %collective-permute-start.20) | collective-permute-done | bytes 393248 | tf_op jit(solution)/shard_map/ppermute | solution.py:37
  257.3 9.1 %collective-permute-done.70 = bf16[1024,256]{1,0:T(8,128)(2,1)S(1)} collective-permute-done((bf16[1024,256]{1,0:T(8,128)(2,1)S(1)}, bf16[1024,256]{1,0:T(8,128)(2,1)S(1)}, u32[]{:S(2)}, u32[]{:S(2)}) %collective-permute-start.70) | collective-permute-done | bytes 524320 | tf_op jit(solution)/shard_map/ppermute | solution.py:37
  268.9 6.3 %collective-permute-done.71 = bf16[512,256]{1,0:T(8,128)(2,1)S(1)} collective-permute-done((bf16[512,256]{1,0:T(8,128)(2,1)S(1)}, bf16[512,256]{1,0:T(8,128)(2,1)S(1)}, u32[]{:S(2)}, u32[]{:S(2)}) %collective-permute-start.71) | collective-permute-done | bytes 262176 | tf_op jit(solution)/shard_map/ppermute | solution.py:37
  275.4 3.4 %collective-permute-start.73 = (bf16[128,256]{1,0:T(8,128)(2,1)S(1)}, bf16[128,256]{1,0:T(8,128)(2,1)S(1)}, u32[]{:S(2)}, u32[]{:S(2)}) collective-permute-start(bf16[128,256]{1,0:T(8,128)(2,1)S(1)} %get-tuple-element.122), channel_id=1, source_target_pairs={{0,16},{4,20},{8,24},{12,28},{16,0},{20,4},{24,8},{28,12},{1,17},{... | collective-permute-start | bytes 196616 | tf_op jit(solution)/shard_map/ppermute | solution.py:37
  281.9 4.5 %collective-permute-done.73 = bf16[128,256]{1,0:T(8,128)(2,1)S(1)} collective-permute-done((bf16[128,256]{1,0:T(8,128)(2,1)S(1)}, bf16[128,256]{1,0:T(8,128)(2,1)S(1)}, u32[]{:S(2)}, u32[]{:S(2)}) %collective-permute-start.73) | collective-permute-done | bytes 65568 | tf_op jit(solution)/shard_map/ppermute | solution.py:37
  288.1 3.0 collective-permute-start.75
  291.1 2.3 collective-permute-done.77
  293.4 3.6 %collective-permute-done.76 = bf16[128,256]{1,0:T(8,128)(2,1)S(1)} collective-permute-done((bf16[128,256]{1,0:T(8,128)(2,1)S(1)}, bf16[128,256]{1,0:T(8,128)(2,1)S(1)}, u32[]{:S(2)}, u32[]{:S(2)}) %collective-permute-start.76) | collective-permute-done | bytes 65568 | tf_op jit(solution)/shard_map/ppermute | solution.py:37
  299.5 2.4 collective-permute-start.23
  308.2 2.1 collective-permute-start.27
  310.3 2.3 collective-permute-start.25
  313.7 2.2 collective-permute-done.79
  319.6 4.4 %collective-permute-done.28 = bf16[768,128]{1,0:T(8,128)(2,1)S(1)} collective-permute-done((bf16[768,128]{1,0:T(8,128)(2,1)S(1)}, bf16[768,128]{1,0:T(8,128)(2,1)S(1)}, u32[]{:S(2)}, u32[]{:S(2)}) %collective-permute-start.28) | collective-permute-done | bytes 196640 | tf_op jit(solution)/shard_map/ppermute | solution.py:37
  326.0 2.4 convert.92
  (513 shorter events, 204.4 us)
Async XLA Ops:
  2.1 13.1 %collective-permute-start.5 = (bf16[1,3,128]{2,1,0:T(4,128)(2,1)}, bf16[1,3,128]{2,1,0:T(4,128)(2,1)}, u32[]{:S(2)}, u32[]{:S(2)}) collective-permute-start(bf16[1,3,128]{2,1,0:T(4,128)(2,1)} %maximum_bitcast_fusion), channel_id=1, source_target_pairs={{0,2},{1,3},{2,0},{3,1},{4,6},{5,7},{6,4},{7,5},{8,10},{9,11},{10,... | collective-permute-start | bytes 2312 | tf_op jit(solution)/shard_map/ppermute | solution.py:37
  5.0 15.7 %collective-permute-start.7 = (bf16[1,512,128]{2,1,0:T(8,128)(2,1)}, bf16[1,512,128]{2,1,0:T(8,128)(2,1)}, u32[]{:S(2)}, u32[]{:S(2)}) collective-permute-start(bf16[1,512,128]{2,1,0:T(8,128)(2,1)} %bitcast.439), channel_id=1, source_target_pairs={{0,2},{1,3},{2,0},{3,1},{4,6},{5,7},{6,4},{7,5},{8,10},{9,11},{10,... | collective-permute-start | bytes 393224 | tf_op jit(solution)/shard_map/ppermute | solution.py:37
  5.1 14.3 %collective-permute-start.12 = (bf16[1,512,128]{2,1,0:T(8,128)(2,1)}, bf16[1,512,128]{2,1,0:T(8,128)(2,1)}, u32[]{:S(2)}, u32[]{:S(2)}) collective-permute-start(bf16[1,512,128]{2,1,0:T(8,128)(2,1)} %bitcast.442), channel_id=1, source_target_pairs={{0,2},{1,3},{2,0},{3,1},{4,6},{5,7},{6,4},{7,5},{8,10},{9,11},{10,... | collective-permute-start | bytes 393224 | tf_op jit(solution)/shard_map/ppermute | solution.py:37
  9.3 14.3 %collective-permute-start = (bf16[1056,128]{1,0:T(8,128)(2,1)}, bf16[1056,128]{1,0:T(8,128)(2,1)}, u32[]{:S(2)}, u32[]{:S(2)}) collective-permute-start(bf16[1056,128]{1,0:T(8,128)(2,1)} %get-tuple-element.91), channel_id=1, source_target_pairs={{0,1},{1,0},{2,3},{3,2},{4,5},{5,4},{6,7},{7,6},{8,9},{9,8},{10,11... | collective-permute-start | bytes 811016 | tf_op jit(solution)/shard_map/ppermute | solution.py:37
  9.3 14.4 %collective-permute-start.1 = (bf16[1056,128]{1,0:T(8,128)(2,1)}, bf16[1056,128]{1,0:T(8,128)(2,1)}, u32[]{:S(2)}, u32[]{:S(2)}) collective-permute-start(bf16[1056,128]{1,0:T(8,128)(2,1)} %get-tuple-element.92), channel_id=1, source_target_pairs={{0,2},{1,3},{2,0},{3,1},{4,6},{5,7},{6,4},{7,5},{8,10},{9,11},{10,... | collective-permute-start | bytes 811016 | tf_op jit(solution)/shard_map/ppermute | solution.py:37
  19.4 37.1 %collective-permute-start.3 = (bf16[1,3,512,128]{3,2,1,0:T(8,128)(2,1)S(1)}, bf16[1,3,512,128]{3,2,1,0:T(8,128)(2,1)S(1)}, u32[]{:S(2)}, u32[]{:S(2)}) collective-permute-start(bf16[1,3,512,128]{3,2,1,0:T(8,128)(2,1)S(1)} %bitcast.429), channel_id=1, source_target_pairs={{0,2},{1,3},{2,0},{3,1},{4,6},{5,7},{6,4},{7,5},{8,10},{9,11},{10,... | collective-permute-start | bytes 1179656 | tf_op jit(solution)/shard_map/ppermute | solution.py:37
  20.8 36.1 %collective-permute-start.14 = (bf16[1,3,512,128]{3,2,1,0:T(8,128)(2,1)}, bf16[1,3,512,128]{3,2,1,0:T(8,128)(2,1)S(1)}, u32[]{:S(2)}, u32[]{:S(2)}) collective-permute-start(bf16[1,3,512,128]{3,2,1,0:T(8,128)(2,1)} %bitcast.432), channel_id=1, source_target_pairs={{0,2},{1,3},{2,0},{3,1},{4,6},{5,7},{6,4},{7,5},{8,10},{9,11},{10,... | collective-permute-start | bytes 1179656 | tf_op jit(solution)/shard_map/ppermute | solution.py:37
  23.7 25.4 %collective-permute-start.10 = (bf16[1056,128]{1,0:T(8,128)(2,1)}, bf16[1056,128]{1,0:T(8,128)(2,1)S(1)}, u32[]{:S(2)}, u32[]{:S(2)}) collective-permute-start(bf16[1056,128]{1,0:T(8,128)(2,1)} %get-tuple-element.88), channel_id=1, source_target_pairs={{0,2},{1,3},{2,0},{3,1},{4,6},{5,7},{6,4},{7,5},{8,10},{9,11},{10,... | collective-permute-start | bytes 811016 | tf_op jit(solution)/shard_map/ppermute | solution.py:37
  25.8 28.4 %collective-permute-start.11 = (bf16[1056,128]{1,0:T(8,128)(2,1)}, bf16[1056,128]{1,0:T(8,128)(2,1)S(1)}, u32[]{:S(2)}, u32[]{:S(2)}) collective-permute-start(bf16[1056,128]{1,0:T(8,128)(2,1)} %get-tuple-element.89), channel_id=1, source_target_pairs={{0,3},{1,2},{2,1},{3,0},{4,7},{5,6},{6,5},{7,4},{8,11},{9,10},{10,... | collective-permute-start | bytes 811016 | tf_op jit(solution)/shard_map/ppermute | solution.py:37
  32.4 24.5 %collective-permute-start.8 = (bf16[2,512,128]{2,1,0:T(8,128)(2,1)S(1)}, bf16[2,512,128]{2,1,0:T(8,128)(2,1)S(1)}, u32[]{:S(2)}, u32[]{:S(2)}) collective-permute-start(bf16[2,512,128]{2,1,0:T(8,128)(2,1)S(1)} %pad_maximum_fusion.27), channel_id=1, source_target_pairs={{0,1},{1,0},{2,3},{3,2},{4,5},{5,4},{6,7},{7,6},{8,9},{9,8},{10,11... | collective-permute-start | bytes 786440 | tf_op jit(solution)/shard_map/ppermute | solution.py:37
  49.0 9.7 %collective-permute-start.13 = (bf16[2,512,128]{2,1,0:T(8,128)(2,1)S(1)}, bf16[2,512,128]{2,1,0:T(8,128)(2,1)S(1)}, u32[]{:S(2)}, u32[]{:S(2)}) collective-permute-start(bf16[2,512,128]{2,1,0:T(8,128)(2,1)S(1)} %pad_maximum_fusion.28), channel_id=1, source_target_pairs={{0,1},{1,0},{2,3},{3,2},{4,5},{5,4},{6,7},{7,6},{8,9},{9,8},{10,11... | collective-permute-start | bytes 786440 | tf_op jit(solution)/shard_map/ppermute | solution.py:37
  142.0 24.6 %collective-permute-start.64 = (f32[4,1024]{1,0:T(4,128)S(1)}, f32[4,1024]{1,0:T(4,128)S(1)}, u32[]{:S(2)}, u32[]{:S(2)}) collective-permute-start(f32[4,1024]{1,0:T(4,128)S(1)} %pad_maximum_fusion.43), channel_id=1, source_target_pairs={{0,1},{1,0},{2,3},{3,2},{4,5},{5,4},{6,7},{7,6},{8,9},{9,8},{10,11... | collective-permute-start | bytes 49160 | tf_op jit(solution)/shard_map/ppermute | solution.py:37
  144.0 91.5 %collective-permute-start.44 = (bf16[2,1536,128]{2,1,0:T(8,128)(2,1)}, bf16[2,1536,128]{2,1,0:T(8,128)(2,1)}, u32[]{:S(2)}, u32[]{:S(2)}) collective-permute-start(bf16[2,1536,128]{2,1,0:T(8,128)(2,1)} %pad_maximum_fusion.20), channel_id=1, source_target_pairs={{0,1},{1,0},{2,3},{3,2},{4,5},{5,4},{6,7},{7,6},{8,9},{9,8},{10,11... | collective-permute-start | bytes 2359304 | tf_op jit(solution)/shard_map/ppermute | solution.py:37
  147.7 41.4 %collective-permute-start.54 = (bf16[2,512,128]{2,1,0:T(8,128)(2,1)}, bf16[2,512,128]{2,1,0:T(8,128)(2,1)S(1)}, u32[]{:S(2)}, u32[]{:S(2)}) collective-permute-start(bf16[2,512,128]{2,1,0:T(8,128)(2,1)} %pad_maximum_fusion.30), channel_id=1, source_target_pairs={{0,1},{1,0},{2,3},{3,2},{4,5},{5,4},{6,7},{7,6},{8,9},{9,8},{10,11... | collective-permute-start | bytes 786440 | tf_op jit(solution)/shard_map/ppermute | solution.py:37
  148.7 16.0 %collective-permute-start.29 = (f32[4,512]{1,0:T(4,128)S(1)}, f32[4,512]{1,0:T(4,128)S(1)}, u32[]{:S(2)}, u32[]{:S(2)}) collective-permute-start(f32[4,512]{1,0:T(4,128)S(1)} %pad_maximum_fusion.44), channel_id=1, source_target_pairs={{0,1},{1,0},{2,3},{3,2},{4,5},{5,4},{6,7},{7,6},{8,9},{9,8},{10,11... | collective-permute-start | bytes 24584 | tf_op jit(solution)/shard_map/ppermute | solution.py:37
  149.9 41.1 %collective-permute-start.34 = (bf16[2,512,128]{2,1,0:T(8,128)(2,1)}, bf16[2,512,128]{2,1,0:T(8,128)(2,1)}, u32[]{:S(2)}, u32[]{:S(2)}) collective-permute-start(bf16[2,512,128]{2,1,0:T(8,128)(2,1)} %pad_maximum_fusion.29), channel_id=1, source_target_pairs={{0,1},{1,0},{2,3},{3,2},{4,5},{5,4},{6,7},{7,6},{8,9},{9,8},{10,11... | collective-permute-start | bytes 786440 | tf_op jit(solution)/shard_map/ppermute | solution.py:37
  179.0 13.0 %collective-permute-start.17 = (bf16[1024,128]{1,0:T(8,128)(2,1)S(1)}, bf16[1024,128]{1,0:T(8,128)(2,1)S(1)}, u32[]{:S(2)}, u32[]{:S(2)}) collective-permute-start(bf16[1024,128]{1,0:T(8,128)(2,1)S(1)} %get-tuple-element.83), channel_id=1, source_target_pairs={{0,2},{1,3},{2,0},{3,1},{4,6},{5,7},{6,4},{7,5},{8,10},{9,11},{10,... | collective-permute-start | bytes 786440 | tf_op jit(solution)/shard_map/ppermute | solution.py:37
  191.0 47.2 %collective-permute-start.19 = (bf16[2,1536,128]{2,1,0:T(8,128)(2,1)S(1)}, bf16[2,1536,128]{2,1,0:T(8,128)(2,1)S(1)}, u32[]{:S(2)}, u32[]{:S(2)}) collective-permute-start(bf16[2,1536,128]{2,1,0:T(8,128)(2,1)S(1)} %pad_maximum_fusion.19), channel_id=1, source_target_pairs={{0,1},{1,0},{2,3},{3,2},{4,5},{5,4},{6,7},{7,6},{8,9},{9,8},{10,11... | collective-permute-start | bytes 2359304 | tf_op jit(solution)/shard_map/ppermute | solution.py:37
  192.0 9.2 %collective-permute-start.55 = (bf16[1,512,128]{2,1,0:T(8,128)(2,1)S(1)}, bf16[1,512,128]{2,1,0:T(8,128)(2,1)S(1)}, u32[]{:S(2)}, u32[]{:S(2)}) collective-permute-start(bf16[1,512,128]{2,1,0:T(8,128)(2,1)S(1)} %fusion.222), channel_id=1, source_target_pairs={{0,2},{1,3},{2,0},{3,1},{4,6},{5,7},{6,4},{7,5},{8,10},{9,11},{10,... | collective-permute-start | bytes 393224 | tf_op jit(solution)/shard_map/ppermute | solution.py:37
  192.5 10.9 %collective-permute-start.35 = (bf16[1,512,128]{2,1,0:T(8,128)(2,1)S(1)}, bf16[1,512,128]{2,1,0:T(8,128)(2,1)S(1)}, u32[]{:S(2)}, u32[]{:S(2)}) collective-permute-start(bf16[1,512,128]{2,1,0:T(8,128)(2,1)S(1)} %fusion.221), channel_id=1, source_target_pairs={{0,2},{1,3},{2,0},{3,1},{4,6},{5,7},{6,4},{7,5},{8,10},{9,11},{10,... | collective-permute-start | bytes 393224 | tf_op jit(solution)/shard_map/ppermute | solution.py:37
  227.7 11.2 %collective-permute-start.69 = (bf16[2048,256]{1,0:T(8,128)(2,1)S(1)}, bf16[2048,256]{1,0:T(8,128)(2,1)S(1)}, u32[]{:S(2)}, u32[]{:S(2)}) collective-permute-start(bf16[2048,256]{1,0:T(8,128)(2,1)S(1)} %dynamic-slice_convert_fusion), channel_id=1, source_target_pairs={{0,1},{1,0},{2,3},{3,2},{4,5},{5,4},{6,7},{7,6},{8,9},{9,8},{10,11... | collective-permute-start | bytes 3145736 | tf_op jit(solution)/shard_map/ppermute | solution.py:37
  236.6 12.1 %collective-permute-start.45 = (bf16[1,1536,128]{2,1,0:T(8,128)(2,1)S(1)}, bf16[1,1536,128]{2,1,0:T(8,128)(2,1)S(1)}, u32[]{:S(2)}, u32[]{:S(2)}) collective-permute-start(bf16[1,1536,128]{2,1,0:T(8,128)(2,1)S(1)} %fusion.183), channel_id=1, source_target_pairs={{0,2},{1,3},{2,0},{3,1},{4,6},{5,7},{6,4},{7,5},{8,10},{9,11},{10,... | collective-permute-start | bytes 1179656 | tf_op jit(solution)/shard_map/ppermute | solution.py:37
  238.3 18.9 %collective-permute-start.20 = (bf16[1,1536,128]{2,1,0:T(8,128)(2,1)S(1)}, bf16[1,1536,128]{2,1,0:T(8,128)(2,1)S(1)}, u32[]{:S(2)}, u32[]{:S(2)}) collective-permute-start(bf16[1,1536,128]{2,1,0:T(8,128)(2,1)S(1)} %fusion.182), channel_id=1, source_target_pairs={{0,2},{1,3},{2,0},{3,1},{4,6},{5,7},{6,4},{7,5},{8,10},{9,11},{10,... | collective-permute-start | bytes 1179656 | tf_op jit(solution)/shard_map/ppermute | solution.py:37
  239.2 27.2 %collective-permute-start.70 = (bf16[1024,256]{1,0:T(8,128)(2,1)S(1)}, bf16[1024,256]{1,0:T(8,128)(2,1)S(1)}, u32[]{:S(2)}, u32[]{:S(2)}) collective-permute-start(bf16[1024,256]{1,0:T(8,128)(2,1)S(1)} %dynamic-slice_convert_fusion.1), channel_id=1, source_target_pairs={{0,2},{1,3},{2,0},{3,1},{4,6},{5,7},{6,4},{7,5},{8,10},{9,11},{10,... | collective-permute-start | bytes 1572872 | tf_op jit(solution)/shard_map/ppermute | solution.py:37
  249.9 18.9 %collective-permute-start.46 = (bf16[768,128]{1,0:T(8,128)(2,1)S(1)}, bf16[768,128]{1,0:T(8,128)(2,1)S(1)}, u32[]{:S(2)}, u32[]{:S(2)}) collective-permute-start(bf16[768,128]{1,0:T(8,128)(2,1)S(1)} %dynamic-slice_convert_fusion.7), channel_id=1, source_target_pairs={{0,4},{4,0},{8,12},{12,8},{16,20},{20,16},{24,28},{28,24},{1,5},{5... | collective-permute-start | bytes 589832 | tf_op jit(solution)/shard_map/ppermute | solution.py:37
  267.6 20.5 %collective-permute-start.21 = (bf16[768,128]{1,0:T(8,128)(2,1)S(1)}, bf16[768,128]{1,0:T(8,128)(2,1)S(1)}, u32[]{:S(2)}, u32[]{:S(2)}) collective-permute-start(bf16[768,128]{1,0:T(8,128)(2,1)S(1)} %dynamic-slice_convert_fusion.8), channel_id=1, source_target_pairs={{0,4},{4,0},{8,12},{12,8},{16,20},{20,16},{24,28},{28,24},{1,5},{5... | collective-permute-start | bytes 589832 | tf_op jit(solution)/shard_map/ppermute | solution.py:37
  275.4 11.0 %collective-permute-start.73 = (bf16[128,256]{1,0:T(8,128)(2,1)S(1)}, bf16[128,256]{1,0:T(8,128)(2,1)S(1)}, u32[]{:S(2)}, u32[]{:S(2)}) collective-permute-start(bf16[128,256]{1,0:T(8,128)(2,1)S(1)} %get-tuple-element.122), channel_id=1, source_target_pairs={{0,16},{4,20},{8,24},{12,28},{16,0},{20,4},{24,8},{28,12},{1,17},{... | collective-permute-start | bytes 196616 | tf_op jit(solution)/shard_map/ppermute | solution.py:37
  278.8 19.6 %collective-permute-start.47 = (bf16[192,128]{1,0:T(8,128)(2,1)S(1)}, bf16[192,128]{1,0:T(8,128)(2,1)S(1)}, u32[]{:S(2)}, u32[]{:S(2)}) collective-permute-start(bf16[192,128]{1,0:T(8,128)(2,1)S(1)} %get-tuple-element.133), channel_id=1, source_target_pairs={{0,8},{4,12},{8,0},{12,4},{16,24},{20,28},{24,16},{28,20},{1,9},{5... | collective-permute-start | bytes 147464 | tf_op jit(solution)/shard_map/ppermute | solution.py:37
  279.9 19.6 %collective-permute-start.49 = (bf16[192,128]{1,0:T(8,128)(2,1)S(1)}, bf16[192,128]{1,0:T(8,128)(2,1)S(1)}, u32[]{:S(2)}, u32[]{:S(2)}) collective-permute-start(bf16[192,128]{1,0:T(8,128)(2,1)S(1)} %get-tuple-element.134), channel_id=1, source_target_pairs={{0,24},{4,28},{8,16},{12,20},{16,8},{20,12},{24,0},{28,4},{1,25},{... | collective-permute-start | bytes 147464 | tf_op jit(solution)/shard_map/ppermute | solution.py:37
  288.1 8.9 %collective-permute-start.76 = (bf16[128,256]{1,0:T(8,128)(2,1)S(1)}, bf16[128,256]{1,0:T(8,128)(2,1)S(1)}, u32[]{:S(2)}, u32[]{:S(2)}) collective-permute-start(bf16[128,256]{1,0:T(8,128)(2,1)S(1)} %fusion.226), channel_id=1, source_target_pairs={{0,16},{4,20},{8,24},{12,28},{16,0},{20,4},{24,8},{28,12},{1,17},{... | collective-permute-start | bytes 196616 | tf_op jit(solution)/shard_map/ppermute | solution.py:37
  288.1 8.9 %collective-permute-start.75 = (bf16[128,256]{1,0:T(8,128)(2,1)S(1)}, bf16[128,256]{1,0:T(8,128)(2,1)S(1)}, u32[]{:S(2)}, u32[]{:S(2)}) collective-permute-start(bf16[128,256]{1,0:T(8,128)(2,1)S(1)} %fusion.226), channel_id=1, source_target_pairs={{0,8},{4,12},{8,0},{12,4},{16,24},{20,28},{24,16},{28,20},{1,9},{5... | collective-permute-start | bytes 196616 | tf_op jit(solution)/shard_map/ppermute | solution.py:37
  306.7 9.2 %collective-permute-start.79 = (bf16[1024,256]{1,0:T(8,128)(2,1)S(1)}, bf16[1024,256]{1,0:T(8,128)(2,1)S(1)}, u32[]{:S(2)}, u32[]{:S(2)}) collective-permute-start(bf16[1024,256]{1,0:T(8,128)(2,1)S(1)} %get-tuple-element.98), channel_id=1, source_target_pairs={{0,2},{1,3},{2,0},{3,1},{4,6},{5,7},{6,4},{7,5},{8,10},{9,11},{10,... | collective-permute-start | bytes 1572872 | tf_op jit(solution)/shard_map/ppermute | solution.py:37
  (130 other events, 726.1 us)

commit v2 on v1

v2 whole, which is shorter than its diff:
```python
import functools
import math

import jax
import jax.numpy as jnp
from jax import lax
from jax.experimental import pallas as pl
from jax.experimental.pallas import tpu as pltpu
from jax.sharding import PartitionSpec as P

SOFTMAX_WARMTH = 8.0
THRESHOLD = 0.7
SHARPNESS = 4.0
STEP_SCALE = 0.5
HALO = 16
LANES = 128
LOG2E = math.log2(math.e)
BF16 = jnp.bfloat16
F32 = jnp.float32
VMEM_LIMIT = 56 * 1024 * 1024


def dot_nn(left, right):
    return jnp.dot(left, right, preferred_element_type=F32)


def dot_nt(left, right):
    return lax.dot_general(left, right, (((1,), (1,)), ((), ())), preferred_element_type=F32)


def dot_tn(left, right):
    return lax.dot_general(left, right, (((0,), (0,)), ((), ())), preferred_element_type=F32)


def elu(values):
    return jnp.where(values > 0, values, jnp.exp(jnp.minimum(values, 0.0)) - 1.0)


def elu_slope(values):
    return jnp.exp(jnp.minimum(values, 0.0))


def swap(values, axis, bits):
    size = lax.axis_size(axis)
    return lax.ppermute(values, axis, [(i, i ^ bits) for i in range(size)])


def after(values, *others):
    return lax.optimization_barrier((values,) + others)[0]


def in_order(pieces, place, dim):
    stacked = jnp.stack(pieces)
    return jnp.concatenate(
        [
            lax.dynamic_index_in_dim(stacked, place ^ j, 0, keepdims=False)
            for j in range(len(pieces))
        ],
        dim,
    )


def frames_out(values, me, own):
    padded = jnp.pad(values, ((HALO, HALO), (0, 0)))

    def rows(k):
        return lax.dynamic_slice_in_dim(padded, (me ^ k) * own, own + 2 * HALO, 0)

    return rows(0), rows(1), jnp.stack([rows(2), rows(3)])


def exchange_steps(count):
    steps, stride, rest = [], 1, count
    while rest > 1:
        radix = 2 if (rest.bit_length() - 1) % 2 else 4
        steps.append((stride, radix))
        stride, rest = stride * radix, rest // radix
    return steps


def scatter_sum_dp(total, place, dim):
    for stride, radix in exchange_steps(lax.axis_size("dp")):
        digit = (place // stride) % radix
        size = total.shape[dim] // radix
        summed = lax.dynamic_slice_in_dim(total, digit * size, size, dim)
        for k in range(1, radix):
            piece = lax.dynamic_slice_in_dim(total, (digit ^ k) * size, size, dim).astype(BF16)
            summed = summed + swap(piece, "dp", k * stride).astype(F32)
        total = summed
    return total


def gather_dp(block, place):
    for stride, radix in reversed(exchange_steps(lax.axis_size("dp"))):
        digit = (place // stride) % radix
        pieces = [block] + [swap(block, "dp", k * stride) for k in range(1, radix)]
        block = in_order(pieces, digit, 0)
    return block


def sum_blocks(sent, kept, place):
    held = kept.astype(F32) + swap(sent, "mp", 1).astype(F32)
    held = held[0] + swap(held[1].astype(BF16), "mp", 2).astype(F32)
    return gather_dp(scatter_sum_dp(held, place, 0).astype(BF16), place)


def sum_everywhere(values, width):
    bit = 1
    while bit < width:
        values = values + swap(values, "mp", bit)
        bit *= 2
    bit = 1
    while bit < lax.axis_size("dp"):
        values = values + swap(values, "dp", bit)
        bit *= 2
    return values


def assemble(me, target, pieces):
    for k, piece in enumerate(pieces):
        columns = pl.ds(pl.multiple_of((me ^ k) * LANES, LANES), LANES)
        target[:, columns] = piece[...]


def taps_into(source, target, first_ok, last_ok, rows, depth):
    step = rows // 3
    for r in range(0, rows, step):
        here = slice(r, r + step)
        before = source[7 + r : 7 + r + step, :] * first_ok[here, :]
        later = source[9 + r : 9 + r + step, :] * last_ok[here, :]
        target[here, 0:depth] = before.astype(BF16)
        target[here, depth : 2 * depth] = source[8 + r : 8 + r + step, :].astype(BF16)
        target[here, 2 * depth : 3 * depth] = later.astype(BF16)


def encoder_kernel(
    me_ref, f0, f1, f2, f3, w0, w1, w2, w3, prev_ok, next_ok,
    hidden_ref, mid_ref, latent_ref, feat, weight, act, act3,
):
    me = me_ref[0]
    rows, depth = hidden_ref.shape
    assemble(me, feat, (f0, f1, f2, f3))
    assemble(me, weight, (w0, w1, w2, w3))
    step = rows // 3
    for r in range(0, rows, step):
        act[8 + r : 8 + r + step, :] = (
            elu(feat[r : r + step, :].astype(F32)).astype(BF16).astype(F32)
        )
    act[0:8, :] = jnp.zeros((8, depth), F32)
    act[8 + rows : 16 + rows, :] = jnp.zeros((8, depth), F32)
    taps_into(act, act3, prev_ok, next_ok, rows, depth)
    biases = weight[4 * depth : 4 * depth + 16, :].astype(F32)
    for r in range(0, rows, step):
        here = slice(r, r + step)
        hidden = dot_nn(act3[here, :], weight[0 : 3 * depth, :]) + biases[0:1, :]
        hidden_ref[here, :] = hidden
        mid = elu(hidden).astype(BF16)
        mid_ref[here, :] = mid
        latent = (
            feat[here, :].astype(F32)
            + dot_nn(mid, weight[3 * depth : 4 * depth, :])
            + biases[1:2, :]
        )
        latent_ref[here, :] = latent.astype(BF16)


def quantize_kernel(latent_ref, books, norms, quant_ref, usage_ref, prob_ref, second_ref, *, own):
    groups, levels, _, depth = books.shape
    rows = latent_ref.shape[0]
    place = pl.program_id(0) * rows + lax.broadcasted_iota(jnp.int32, (rows, 1), 0)
    mine = jnp.where((place >= HALO) & (place < HALO + own), 1.0, 0.0).astype(F32)

    @pl.when(pl.program_id(0) == 0)
    def _():
        usage_ref[...] = jnp.zeros_like(usage_ref)

    current = [latent_ref[:, g * depth : (g + 1) * depth] for g in range(groups)]
    remain = [c.astype(F32) for c in current]
    summed = [None] * groups
    for level in range(levels):
        for g in range(groups):
            book = books[g, level]
            scores = dot_nt(current[g], book) * (2.0 * LOG2E / SOFTMAX_WARMTH) - norms[g, level]
            terms = jnp.exp2(scores - jnp.max(scores, axis=1, keepdims=True))
            prob = terms * (1.0 / jnp.sum(terms, axis=1, keepdims=True))
            low = prob.astype(BF16)
            prob_ref[g, level] = low
            usage_ref[g, level] += jnp.sum(prob * mine, axis=0, keepdims=True)
            picked = dot_nn(low, book)
            summed[g] = picked if summed[g] is None else summed[g] + picked
            if level + 1 < levels:
                remain[g] = remain[g] - picked
                current[g] = remain[g].astype(BF16)
                second_ref[level, :, g * depth : (g + 1) * depth] = current[g]
    for g in range(groups):
        quant_ref[:, g * depth : (g + 1) * depth] = summed[g].astype(BF16)


def weight_grads(me, sent, kept, grad, deep, grad1, deep1, own, depth):
    here = slice(HALO, HALO + own)
    lane = lax.broadcasted_iota(jnp.int32, (own, LANES), 1)
    ones3 = jnp.where(lane == 0, 1.0, 0.0).astype(BF16)
    ones1 = jnp.where(lane == 1, 1.0, 0.0).astype(BF16)
    for k in range(4):
        columns = pl.ds(pl.multiple_of((me ^ k) * LANES, LANES), LANES)
        left = grad[here, columns]
        left1 = grad1[here, columns]
        target = (kept, sent)[k % 2].at[k // 2]
        target[:, 0 : 3 * depth] = dot_tn(left, deep[here, :]).astype(target.dtype)
        target[:, 3 * depth : 4 * depth] = dot_tn(left1, deep1[here, :]).astype(target.dtype)
        target[:, 4 * depth : 4 * depth + LANES] = (
            dot_tn(left, ones3) + dot_tn(left1, ones1)
        ).astype(target.dtype)


def input_grad(taps, weight, here, depth):
    return (
        dot_nt(taps[here, 2 * depth : 3 * depth], weight[0:depth, :])
        + dot_nt(taps[here, depth : 2 * depth], weight[depth : 2 * depth, :])
        + dot_nt(taps[here, 0:depth], weight[2 * depth : 3 * depth, :])
    )


def decoder_kernel(
    me_ref, quant, c0, c1, c2, c3, w0, w1, w2, w3, prev_ok, next_ok,
    grad_ref, sent, kept, cot, weight, act, act3, low, mid,
):
    me = me_ref[0]
    rows, depth = quant.shape
    own = rows - 2 * HALO
    assemble(me, cot, (c0, c1, c2, c3))
    assemble(me, weight, (w0, w1, w2, w3))
    step = rows // 3
    for r in range(0, rows, step):
        act[8 + r : 8 + r + step, :] = (
            elu(quant[r : r + step, :].astype(F32)).astype(BF16).astype(F32)
        )
    act[0:8, :] = jnp.zeros((8, depth), F32)
    act[8 + rows : 16 + rows, :] = jnp.zeros((8, depth), F32)
    taps_into(act, act3, prev_ok, next_ok, rows, depth)
    bias = weight[4 * depth : 4 * depth + 16, :].astype(F32)[0:1, :]
    for r in range(0, rows, step):
        here = slice(r, r + step)
        hidden = dot_nn(act3[here, :], weight[0 : 3 * depth, :]) + bias
        mid[here, :] = elu(hidden).astype(BF16)
        grad = dot_nt(cot[here, :], weight[3 * depth : 4 * depth, :]) * elu_slope(hidden)
        grad = grad.astype(BF16)
        low[here, :] = grad
        act[8 + r : 8 + r + step, :] = grad.astype(F32)
    weight_grads(me, sent, kept, low, act3, cot, mid, own, depth)
    taps_into(act, act3, prev_ok, next_ok, rows, depth)
    for r in range(0, rows, step):
        here = slice(r, r + step)
        grad_ref[here, :] = cot[here, :].astype(F32) + elu_slope(
            quant[here, :].astype(F32)
        ) * input_grad(act3, weight, here, depth)


def quantize_back_kernel(
    group_ref, grad_ref, prob_ref, first_ref, second_ref, books, turned,
    out_ref, table_ref, total, columns, *, own, levels,
):
    step = pl.program_id(0)
    rows = grad_ref.shape[0]
    place = step * rows + lax.broadcasted_iota(jnp.int32, (rows, 1), 0)
    mine = jnp.where((place >= HALO) & (place < HALO + own), 1.0, 0.0).astype(F32)
    mine_low = mine.astype(BF16)
    scale = 2.0 / SOFTMAX_WARMTH

    @pl.when(step == 0)
    def _():
        total[...] = jnp.zeros_like(total)
        columns[...] = jnp.zeros_like(columns)

    grad_remain = None
    for level in reversed(range(levels)):
        book = books[0, level]
        low = prob_ref[0, level]
        current = first_ref[...] if level == 0 else second_ref[level - 1]
        picked = grad_ref[...] if grad_remain is None else grad_ref[...] - grad_remain
        picked = picked.astype(BF16)
        grad_prob = dot_nt(picked, book)
        prob = low.astype(F32)
        inner = jnp.sum(prob * grad_prob, axis=1, keepdims=True)
        grad_scores = (prob * (grad_prob - inner)).astype(BF16)
        through = dot_nn(grad_scores, book) * scale
        grad_remain = through if grad_remain is None else grad_remain + through
        total[level] += dot_tn(picked * mine_low, low) + dot_tn(
            current * (mine_low * scale), grad_scores
        )
        columns[level] += jnp.sum(grad_scores.astype(F32) * mine, axis=0, keepdims=True)
    out_ref[...] = grad_remain.astype(BF16)

    @pl.when(step == pl.num_programs(0) - 1)
    def _():
        for level in range(levels):
            table_ref[level] = (
                total[level] - scale * columns[level] * turned[0, level].astype(F32)
            ).astype(BF16)


def encoder_grad_kernel(
    me_ref, grad_latent, hidden, mid, f0, f1, f2, f3, w0, w1, w2, w3, prev_ok, next_ok,
    sent, kept, out_sent, out_kept, feat, weight, act, act3, low,
):
    me = me_ref[0]
    rows, depth = grad_latent.shape
    own = rows - 2 * HALO
    assemble(me, feat, (f0, f1, f2, f3))
    assemble(me, weight, (w0, w1, w2, w3))
    step = rows // 3
    for r in range(0, rows, step):
        act[8 + r : 8 + r + step, :] = (
            elu(feat[r : r + step, :].astype(F32)).astype(BF16).astype(F32)
        )
    act[0:8, :] = jnp.zeros((8, depth), F32)
    act[8 + rows : 16 + rows, :] = jnp.zeros((8, depth), F32)
    taps_into(act, act3, prev_ok, next_ok, rows, depth)
    for r in range(0, rows, step):
        here = slice(r, r + step)
        grad = dot_nt(grad_latent[here, :], weight[3 * depth : 4 * depth, :])
        grad = (grad * elu_slope(hidden[here, :])).astype(BF16)
        low[here, :] = grad
        act[8 + r : 8 + r + step, :] = grad.astype(F32)
    weight_grads(me, sent, kept, low, act3, grad_latent, mid, own, depth)
    taps_into(act, act3, prev_ok, next_ok, rows, depth)
    for r in range(HALO, HALO + own, own // 4):
        here = slice(r, r + own // 4)
        feat[here, :] = (
            grad_latent[here, :].astype(F32)
            + elu_slope(feat[here, :].astype(F32)) * input_grad(act3, weight, here, depth)
        ).astype(BF16)
    for k in range(4):
        columns = pl.ds(pl.multiple_of((me ^ k) * LANES, LANES), LANES)
        (out_kept, out_sent)[k // 2][k % 2] = feat[HALO : HALO + own, columns]


def whole(count, smem_first=False):
    specs = [pl.BlockSpec(memory_space=pltpu.VMEM)] * count
    if smem_first:
        specs[0] = pl.BlockSpec(memory_space=pltpu.SMEM)
    return specs


def cost(flops, moved):
    return pl.CostEstimate(flops=int(flops), bytes_accessed=int(moved), transcendentals=0)


def shaped(shape, dtype):
    return jax.ShapeDtypeStruct(shape, dtype)


PARAMS = pltpu.CompilerParams(vmem_limit_bytes=VMEM_LIMIT)


def body(
    features,
    lengths,
    enc_conv3,
    enc_bias3,
    enc_conv1,
    enc_bias1,
    codebooks,
    dec_conv3,
    dec_bias3,
    dec_conv1,
    code_buffer,
    buffer_index,
    out_cotangent,
):
    frames, cols = features.shape
    groups, levels, num_codes, group_dim = codebooks.shape
    width = lax.axis_size("mp")
    n_dp = lax.axis_size("dp")
    me = lax.axis_index("mp")
    place = lax.axis_index("dp")
    own = frames // width
    rows = own + 2 * HALO
    depth = cols * width
    me_row = me.reshape(1)

    clip_ends = jnp.cumsum(lengths[0])
    starts = clip_ends - lengths[0]
    positions = me * own - HALO + jnp.arange(rows + 1, dtype=jnp.int32)
    is_start = jnp.any(positions[:, None] == starts[None, :], axis=1) | (positions == frames)
    ok = jnp.where(is_start, 0.0, 1.0).astype(F32)[:, None]
    prev_ok, next_ok = ok[:-1], ok[1:]

    def pack(conv3, conv1, biases):
        rows16 = jnp.pad(jnp.stack(biases), ((0, 16 - len(biases)), (0, 0)))
        return jnp.concatenate([conv3.reshape(3 * depth, cols), conv1, rows16], 0)

    f0, f1, f23 = frames_out(features, me, own)
    enc_own = pack(enc_conv3, enc_conv1, [enc_bias3, enc_bias1])
    got = swap(f23, "mp", 2)
    enc_other = swap(enc_own, "mp", 2)
    feat = (f0, got[0])
    other = swap(jnp.stack([f1, got[1]]), "mp", 1)
    feat = (f0, other[0], got[0], other[1])
    enc = swap(jnp.stack([enc_own, enc_other]), "mp", 1)
    enc = (enc_own, enc[0], enc_other, enc[1])

    c0, c1, c23 = frames_out(out_cotangent, me, own)
    dec_own = pack(dec_conv3, dec_conv1, [dec_bias3])
    dec_start, cot_start = after((dec_own, c23), enc_other, got)
    dec_other = swap(dec_start, "mp", 2)
    got = swap(cot_start, "mp", 2)
    other = swap(jnp.stack([c1, got[1]]), "mp", 1)
    cot = (c0, other[0], got[0], other[1])
    dec = swap(jnp.stack([dec_own, dec_other]), "mp", 1)
    dec = (dec_own, dec[0], dec_other, dec[1])

    books_f = codebooks.astype(F32)
    norms = jnp.sum(books_f * books_f, axis=3) * (LOG2E / SOFTMAX_WARMTH)
    norms = norms[:, :, None, :]
    turned = codebooks.transpose(0, 1, 3, 2)

    hidden_enc, act_mid, latent = pl.pallas_call(
        encoder_kernel,
        out_shape=(
            shaped((rows, depth), F32),
            shaped((rows, depth), BF16),
            shaped((rows, depth), BF16),
        ),
        in_specs=whole(11, True),
        out_specs=tuple(whole(3)),
        scratch_shapes=[
            pltpu.VMEM((rows, depth), BF16),
            pltpu.VMEM((4 * depth + 16, depth), BF16),
            pltpu.VMEM((rows + 16, depth), F32),
            pltpu.VMEM((rows, 3 * depth), BF16),
        ],
        compiler_params=PARAMS,
        cost_estimate=cost(8 * rows * depth * depth, 12e6),
    )(me_row, *feat, *enc, prev_ok, next_ok)

    step = rows // 3
    quant, usage, prob, second = pl.pallas_call(
        functools.partial(quantize_kernel, own=own),
        grid=(3,),
        out_shape=(
            shaped((rows, depth), BF16),
            shaped((groups, levels, 1, num_codes), F32),
            shaped((groups, levels, rows, num_codes), BF16),
            shaped((levels - 1, rows, depth), BF16),
        ),
        in_specs=[
            pl.BlockSpec((step, depth), lambda i: (i, 0)),
            pl.BlockSpec(codebooks.shape, lambda i: (0, 0, 0, 0)),
            pl.BlockSpec(norms.shape, lambda i: (0, 0, 0, 0)),
        ],
        out_specs=(
            pl.BlockSpec((step, depth), lambda i: (i, 0)),
            pl.BlockSpec((groups, levels, 1, num_codes), lambda i: (0, 0, 0, 0)),
            pl.BlockSpec((groups, levels, step, num_codes), lambda i: (0, 0, i, 0)),
            pl.BlockSpec((levels - 1, step, depth), lambda i: (0, i, 0)),
        ),
        compiler_params=PARAMS,
        cost_estimate=cost(16 * rows * num_codes * group_dim, 30e6),
    )(latent, codebooks, norms)
    usage_all = sum_everywhere(usage.reshape(groups * levels, num_codes), width)

    packed = 4 * depth + LANES
    grad_quant, dec_sent, dec_kept = pl.pallas_call(
        decoder_kernel,
        out_shape=(
            shaped((rows, depth), F32),
            shaped((2, cols, packed), BF16),
            shaped((2, cols, packed), F32),
        ),
        in_specs=whole(12, True),
        out_specs=tuple(whole(3)),
        scratch_shapes=[
            pltpu.VMEM((rows, depth), BF16),
            pltpu.VMEM((4 * depth + 16, depth), BF16),
            pltpu.VMEM((rows + 16, depth), F32),
            pltpu.VMEM((rows, 3 * depth), BF16),
            pltpu.VMEM((rows, depth), BF16),
            pltpu.VMEM((rows, depth), BF16),
        ],
        compiler_params=PARAMS,
        cost_estimate=cost(24 * rows * depth * depth, 20e6),
    )(me_row, quant, *cot, *dec, prev_ok, next_ok)

    def quantize_back(group):
        return pl.pallas_call(
            functools.partial(quantize_back_kernel, own=own, levels=levels),
            grid_spec=pltpu.PrefetchScalarGridSpec(
                num_scalar_prefetch=1,
                grid=(3,),
                in_specs=[
                    pl.BlockSpec((step, group_dim), lambda i, g: (i, g[0])),
                    pl.BlockSpec((1, levels, step, num_codes), lambda i, g: (g[0], 0, i, 0)),
                    pl.BlockSpec((step, group_dim), lambda i, g: (i, g[0])),
                    pl.BlockSpec((levels - 1, step, group_dim), lambda i, g: (0, i, g[0])),
                    pl.BlockSpec((1, levels, num_codes, group_dim), lambda i, g: (g[0], 0, 0, 0)),
                    pl.BlockSpec((1, levels, group_dim, num_codes), lambda i, g: (g[0], 0, 0, 0)),
                ],
                out_specs=(
                    pl.BlockSpec((step, group_dim), lambda i, g: (i, 0)),
                    pl.BlockSpec((levels, group_dim, num_codes), lambda i, g: (0, 0, 0)),
                ),
                scratch_shapes=[
                    pltpu.VMEM((levels, group_dim, num_codes), F32),
                    pltpu.VMEM((levels, 1, num_codes), F32),
                ],
            ),
            out_shape=(
                shaped((rows, group_dim), BF16),
                shaped((levels, group_dim, num_codes), BF16),
            ),
            compiler_params=PARAMS,
            cost_estimate=cost(16 * rows * num_codes * group_dim, 15e6),
        )(group.reshape(1), grad_quant, prob, latent, second, codebooks, turned)

    side, level_side = me % 2, me // 2
    grad_other, table_other = quantize_back(1 - side)
    grad_mine, table_mine = quantize_back(side)
    grad_latent = jnp.where(
        side == 0,
        jnp.concatenate([grad_mine, grad_other], 1),
        jnp.concatenate([grad_other, grad_mine], 1),
    )

    enc_sent, enc_kept, out_sent, out_kept = pl.pallas_call(
        encoder_grad_kernel,
        out_shape=(
            shaped((2, cols, packed), BF16),
            shaped((2, cols, packed), F32),
            shaped((2, own, cols), BF16),
            shaped((2, own, cols), BF16),
        ),
        in_specs=whole(14, True),
        out_specs=tuple(whole(4)),
        scratch_shapes=[
            pltpu.VMEM((rows, depth), BF16),
            pltpu.VMEM((4 * depth + 16, depth), BF16),
            pltpu.VMEM((rows + 16, depth), F32),
            pltpu.VMEM((rows, 3 * depth), BF16),
            pltpu.VMEM((rows, depth), BF16),
        ],
        compiler_params=PARAMS,
        cost_estimate=cost(16 * rows * depth * depth, 20e6),
    )(me_row, grad_latent, hidden_enc, act_mid, *feat, *enc, prev_ok, next_ok)

    tables = table_mine.astype(F32) + swap(table_other, "mp", 1).astype(F32)
    kept = lax.dynamic_index_in_dim(tables, level_side, 0, keepdims=False)
    sent = lax.dynamic_index_in_dim(tables, 1 - level_side, 0, keepdims=False)
    held = kept + swap(sent.astype(BF16), "mp", 2).astype(F32)
    held = scatter_sum_dp(held, place, 1)
    codes = held.shape[1]
    first = jnp.int32(0)
    size = num_codes
    for stride, radix in exchange_steps(n_dp):
        size = size // radix
        first = first + ((place // stride) % radix) * size

    def own_codes(array):
        start = (side, level_side, first) + (jnp.int32(0),) * (array.ndim - 3)
        return lax.dynamic_slice(array, start, (1, 1, codes) + array.shape[3:])[0, 0]

    index = own_codes(buffer_index)
    one_hot = index[:, None] == jnp.arange(code_buffer.shape[0], dtype=jnp.int32)[None, :]
    halves = lax.dynamic_slice_in_dim(code_buffer, side * group_dim, group_dim, 1)
    chosen = dot_nn(one_hot.astype(BF16), halves)
    share = num_codes / (frames * n_dp)
    ratio = own_codes(usage_all.reshape(groups, levels, num_codes)) * share
    refresh = jax.nn.sigmoid(SHARPNESS * (THRESHOLD - ratio))[:, None]
    stepped = own_codes(codebooks).astype(F32) - (STEP_SCALE * share) * held.T
    fresh = ((1.0 - refresh) * stepped + refresh * chosen).astype(BF16)
    fresh = gather_dp(fresh, place)
    fresh = in_order([fresh[None], swap(fresh[None], "mp", 2)], level_side, 0)
    fresh = in_order([fresh[None], swap(fresh[None], "mp", 1)], side, 0)
    new_codebooks = fresh.astype(F32)

    def unpack(total):
        total = total.T.astype(F32)
        return (
            total[: 3 * depth].reshape(3, depth, cols),
            total[4 * depth],
            total[3 * depth : 4 * depth],
            total[4 * depth + 1],
        )

    got = swap(out_sent, "mp", 2)
    kept = jnp.stack([out_kept[0], got[0]])
    other = swap(jnp.stack([out_kept[1], got[1]]), "mp", 1)
    grad_features = in_order([kept[0], other[0], kept[1], other[1]], me, 0).astype(F32)

    return (
        grad_features,
        *unpack(sum_blocks(enc_sent, enc_kept, place)),
        *unpack(sum_blocks(dec_sent, dec_kept, place)),
        new_codebooks,
    )


def solution(mesh):
    return jax.shard_map(
        body,
        mesh=mesh,
        in_specs=(
            P("dp", "mp"),
            P("dp", None),
            P(None, None, "mp"),
            P("mp"),
            P(None, "mp"),
            P("mp"),
            P(),
            P(None, None, "mp"),
            P("mp"),
            P(None, "mp"),
            P(),
            P(),
            P("dp", "mp"),
        ),
        out_specs=(
            P("dp", "mp"),
            P(None, None, "mp"),
            P("mp"),
            P(None, "mp"),
            P("mp"),
            P(None, None, "mp"),
            P("mp"),
            P(None, "mp"),
            P("mp"),
            P(),
        ),
        check_vma=False,
    )
```

time: 334 us -> 293 us (0.88)
  Pallas kernels: 0 us -> 79.1 us
  matrix products: 55.1 us -> 1.24 us
  other arithmetic: 60.8 us -> 27.9 us
  starting transfers between devices: 89.5 us -> 56.7 us
  local copies, waits for them, and re-layouts: 25.7 us -> 30.6 us
    pallas_call x0 -> x6, Pallas kernels: none -> 79.1 us  [the longest x2 32.8 us: quantize_back(): pl.pallas_call(functools.partial(quantize_back_kernel, own=own, levels=le...]
    dot_general x32 -> x0, matrix products: 38.6 us -> none  [the longest x16 22.9 us: dot_tn(): lax.dot_general(left, right, (((0,), (0,)), ((), ())), preferred_element_...]
    ppermute x81 -> x47, starting transfers between devices: 89.5 us -> 56.7 us  [swap(): return lax.ppermute(values, axis, [(i, i ^ bits) for i in range(size)])]
    dot_general x16 -> x1, matrix products: 16.6 us -> 1.24 us  [dot_nn(): return jnp.dot(left, right, preferred_element_type=F32)]
    convert_element_type x29 -> x6, other arithmetic: 20.1 us -> 5.59 us  [the longest x1 2.29 us: body(): new_codebooks = fresh.astype(F32)]
    unnamed x165 -> x47, local copies, waits for them, and re-layouts: 17.7 us -> 5.55 us
    reduce_sum x17 -> x1, other arithmetic: 10.6 us -> 0.63 us  [body(): norms = jnp.sum(books_f * books_f, axis=3) * (LOG2E / SOFTMAX_WARMTH)]
    squeeze x1 -> x8, local copies, waits for them, and re-layouts: 0.53 us -> 7.39 us  [the longest x2 2.61 us: body(): feat = (f0, other[0], got[0], other[1])]
  transfers between devices with their start and end apart: 81 -> 47, of which waited for: 32 -> 19; matrix products, arithmetic and copies ran while one was open for 15% -> 16% of each run, Pallas kernels for 0% -> 12%
where the time goes in v2:
time: 293 us; the launch traced here: 289 us
  waiting for transfers between devices  91.5 us (31%)
  Pallas kernels  79.1 us (27%)
  starting transfers between devices  56.7 us (19%)
  local copies, waits for them, and re-layouts  30.6 us (10%)
  other arithmetic  27.9 us (10%)
    ppermute x47, waiting for transfers between devices, swap(): return lax.ppermute(values, axis, [(i, i ^ bits) for i in range(size)])  91.5 us
    ppermute x47, starting transfers between devices, swap(): return lax.ppermute(values, axis, [(i, i ^ bits) for i in range(size)])  56.7 us
    pallas_call x2, Pallas kernels, quantize_back(): pl.pallas_call(functools.partial(quantize_back_kernel, own=own, levels=le...  32.8 us
    pallas_call x1, Pallas kernels, body(): pl.pallas_call(functools.partial(quantize_kernel, own=own), grid=(3,), ou...  13.2 us
    pallas_call x1, Pallas kernels, body(): pl.pallas_call(decoder_kernel, out_shape=(shaped((rows, depth), F32), sha...  12.9 us
    pallas_call x1, Pallas kernels, body(): pl.pallas_call(encoder_grad_kernel, out_shape=(shaped((2, cols, packed),...  12.2 us
    pallas_call x1, Pallas kernels, body(): pl.pallas_call(encoder_kernel, out_shape=(shaped((rows, depth), F32), sha...  8.09 us
    dynamic_slice x6, local copies, waits for them, and re-layouts, in_order(): lax.dynamic_index_in_dim(stacked, place ^ j, 0, keepdims=False)  6.15 us
  transfers between devices with their start and end apart: 47, of which 19 were waited for; matrix products, arithmetic and copies ran while one was open for 16% of the time, Pallas kernels for 12%

profile of v2, /device:TPU:0, one launch (start us, length us, event | category | flops | bytes accessed | tf_op | source)
XLA Modules:
  0.0 288.6 jit_solution(507658262397118341)
XLA Ops:
  0.7 2.1 fusion.26
  3.7 2.9 %collective-permute-start = (bf16[2,1056,128]{2,1,0:T(8,128)(2,1)}, bf16[2,1056,128]{2,1,0:T(8,128)(2,1)}, u32[]{:S(2)}, u32[]{:S(2)}) collective-permute-start(bf16[2,1056,128]{2,1,0:T(8,128)(2,1)} %pad_maximum_fusion.4), channel_id=1, source_target_pairs={{0,2},{1,3},{2,0},{3,1},{4,6},{5,7},{6,4},{7,5},{8,10},{9,11},{10,... | collective-permute-start | bytes 1622024 | tf_op jit(solution)/shard_map/ppermute | solution.py:45
  12.3 2.4 copy.49
  18.2 12.3 %collective-permute-done.2.w2 = bf16[2064,128]{1,0:T(8,128)(2,1)} collective-permute-done((bf16[2064,128]{1,0:T(8,128)(2,1)}, bf16[2064,128]{1,0:T(8,128)(2,1)}, u32[]{:S(2)}, u32[]{:S(2)}) %collective-permute-start.2) | collective-permute-done | bytes 528416 | tf_op jit(solution)/shard_map/ppermute | solution.py:45
  35.8 10.9 %collective-permute-done.6.w2 = bf16[2064,128]{1,0:T(8,128)(2,1)S(1)} collective-permute-done((bf16[2064,128]{1,0:T(8,128)(2,1)S(1)}, bf16[2064,128]{1,0:T(8,128)(2,1)S(1)}, u32[]{:S(2)}, u32[]{:S(2)}) %collective-permute-start.6) | collective-permute-done | bytes 528416 | tf_op jit(solution)/shard_map/ppermute | solution.py:45
  46.8 10.9 %collective-permute-done.4 = bf16[2,1056,128]{2,1,0:T(8,128)(2,1)S(1)} collective-permute-done((bf16[2,1056,128]{2,1,0:T(8,128)(2,1)S(1)}, bf16[2,1056,128]{2,1,0:T(8,128)(2,1)S(1)}, u32[]{:S(2)}, u32[]{:S(2)}) %collective-permute-start.4) | collective-permute-done | bytes 540704 | tf_op jit(solution)/shard_map/ppermute | solution.py:45
  60.6 8.1 %shard_map.204 = (f32[1056,512]{1,0:T(8,128)}, bf16[1056,512]{1,0:T(8,128)(2,1)}, bf16[1056,512]{1,0:T(8,128)(2,1)}) custom-call(s32[1]{0:T(128)} %bitcast.me_ref, bf16[1056,128]{1,0:T(8,128)(2,1)} %get-tuple-element.77.f0, bf16[1056,128]{1,0:T(8,128)(2,1)} %get-tuple-element.93.f1, bf16[1056,128]{1,0:T(8,128)(2,1)} %get-tuple-element.94.f2, ...), custom_call_target="tpu_custom_call" | custom-call | flops 2214592512 | bytes 12000000 | tf_op jit(solution)/shard_map/pallas_call | solution.py:418
  68.7 13.2 %shard_map.205 = (bf16[1056,512]{1,0:T(8,128)(2,1)}, f32[2,2,1,1024]{3,2,1,0:T(1,128)}, bf16[2,2,1056,1024]{3,2,1,0:T(8,128)(2,1)}, bf16[1,1056,512]{2,1,0:T(8,128)(2,1)}) custom-call(bf16[1056,512]{1,0:T(8,128)(2,1)} %get-tuple-element.30.latent_ref.first_ref, bf16[2,2,1024,256]{3,2,1,0:T(8,128)(2,1)} %books.5, f32[2,2,1,1024]{3,2,1,0:T(1,128)} %mul.143.norms), custom_call_target="tpu_custom_call" | custom-call | flops 4429185024 | bytes 30000000 | tf_op jit(solution)/shard_map/pallas_call | solution.py:438
  83.8 12.9 %shard_map.206 = (f32[1056,512]{1,0:T(8,128)}, bf16[2,128,2176]{2,1,0:T(8,128)(2,1)}, f32[2,128,2176]{2,1,0:T(8,128)}) custom-call(s32[1]{0:T(128)} %bitcast.me_ref, bf16[1056,512]{1,0:T(8,128)(2,1)} %get-tuple-element.31.quant, bf16[1056,128]{1,0:T(8,128)(2,1)} %get-tuple-element.73.c0, bf16[1056,128]{1,0:T(8,128)(2,1)} %get-tuple-element.89.c1, ...), custom_call_target="tpu_custom_call" | custom-call | flops 6643777536 | bytes 20000000 | tf_op jit(solution)/shard_map/pallas_call | solution.py:464
  96.7 12.1 %shard_map.207 = (bf16[1056,256]{1,0:T(8,128)(2,1)}, bf16[2,256,1024]{2,1,0:T(8,128)(2,1)}) custom-call(s32[1]{0:T(128)} %bitcast.1.group_ref, f32[1056,512]{1,0:T(8,128)} %get-tuple-element.34.grad_ref, bf16[2,2,1056,1024]{3,2,1,0:T(8,128)(2,1)} %get-tuple-element.35.prob_ref, bf16[1056,512]{1,0:T(8,128)(2,1)} %get-tuple-element.30.latent_ref.first_ref, ...), custom_call_target="tpu_custom_call" | custom-call | flops 4429185024 | bytes 15000000 | tf_op jit(solution)/shard_map/pallas_call | solution.py:486
  108.8 20.7 %shard_map.208 = (bf16[1056,256]{1,0:T(8,128)(2,1)}, bf16[2,256,1024]{2,1,0:T(8,128)(2,1)}) custom-call(s32[1]{0:T(128)} %bitcast.29.group_ref, f32[1056,512]{1,0:T(8,128)} %get-tuple-element.34.grad_ref, bf16[2,2,1056,1024]{3,2,1,0:T(8,128)(2,1)} %get-tuple-element.35.prob_ref, bf16[1056,512]{1,0:T(8,128)(2,1)} %get-tuple-element.30.latent_ref.first_ref, ...), custom_call_target="tpu_custom_call" | custom-call | flops 4429185024 | bytes 15000000 | tf_op jit(solution)/shard_map/pallas_call | solution.py:486
  130.0 2.5 maximum_select_fusion.grad_latent
  132.5 12.2 %shard_map.209 = (bf16[2,128,2176]{2,1,0:T(8,128)(2,1)}, f32[2,128,2176]{2,1,0:T(8,128)}, bf16[2,1024,128]{2,1,0:T(8,128)(2,1)}, bf16[2,1024,128]{2,1,0:T(8,128)(2,1)}) custom-call(s32[1]{0:T(128)} %bitcast.me_ref, bf16[1056,512]{1,0:T(8,128)(2,1)} %maximum_select_fusion.grad_latent, f32[1056,512]{1,0:T(8,128)} %get-tuple-element.39.hidden, ...), custom_call_target="tpu_custom_call" | custom-call | flops 4429185024 | bytes 20000000 | tf_op jit(solution)/shard_map/pallas_call | solution.py:525
  148.0 11.0 %collective-permute-done.31 = f32[4,1024]{1,0:T(4,128)S(1)} collective-permute-done((f32[4,1024]{1,0:T(4,128)S(1)}, f32[4,1024]{1,0:T(4,128)S(1)}, u32[]{:S(2)}, u32[]{:S(2)}) %collective-permute-start.31) | collective-permute-done | bytes 16416 | tf_op jit(solution)/shard_map/ppermute | solution.py:45
  166.6 2.9 collective-permute-start.34
  180.4 8.6 %collective-permute-done.36 = bf16[256,1024]{1,0:T(8,128)(2,1)S(1)} collective-permute-done((bf16[256,1024]{1,0:T(8,128)(2,1)S(1)}, bf16[256,1024]{1,0:T(8,128)(2,1)S(1)}, u32[]{:S(2)}, u32[]{:S(2)}) %collective-permute-start.36) | collective-permute-done | bytes 524320 | tf_op jit(solution)/shard_map/ppermute | solution.py:45
  191.1 9.9 %collective-permute-done.11 = bf16[128,2176]{1,0:T(8,128)(2,1)S(1)} collective-permute-done((bf16[128,2176]{1,0:T(8,128)(2,1)S(1)}, bf16[128,2176]{1,0:T(8,128)(2,1)S(1)}, u32[]{:S(2)}, u32[]{:S(2)}) %collective-permute-start.11) | collective-permute-done | bytes 557088 | tf_op jit(solution)/shard_map/ppermute | solution.py:45
  202.9 9.6 %collective-permute-done.21 = bf16[128,2176]{1,0:T(8,128)(2,1)S(1)} collective-permute-done((bf16[128,2176]{1,0:T(8,128)(2,1)S(1)}, bf16[128,2176]{1,0:T(8,128)(2,1)S(1)}, u32[]{:S(2)}, u32[]{:S(2)}) %collective-permute-start.21) | collective-permute-done | bytes 557088 | tf_op jit(solution)/shard_map/ppermute | solution.py:45
  214.6 2.7 collective-permute-start.39
  219.1 2.7 collective-permute-done.39
  224.9 2.2 collective-permute-start.42
  227.1 2.2 collective-permute-start.43
  229.5 2.1 collective-permute-start.14
  231.7 2.3 collective-permute-start.15
  234.0 6.1 %collective-permute-start.24 = (bf16[16,2176]{1,0:T(8,128)(2,1)S(1)}, bf16[16,2176]{1,0:T(8,128)(2,1)S(1)}, u32[]{:S(2)}, u32[]{:S(2)}) collective-permute-start(bf16[16,2176]{1,0:T(8,128)(2,1)S(1)} %get-tuple-element.82), channel_id=1, source_target_pairs={{0,16},{4,20},{8,24},{12,28},{16,0},{20,4},{24,8},{28,12},{1,17},{... | collective-permute-start | bytes 208904 | tf_op jit(solution)/shard_map/ppermute | solution.py:45
  242.8 3.5 %collective-permute-start.17 = (bf16[16,2176]{1,0:T(8,128)(2,1)S(1)}, bf16[16,2176]{1,0:T(8,128)(2,1)S(1)}, u32[]{:S(2)}, u32[]{:S(2)}) collective-permute-start(bf16[16,2176]{1,0:T(8,128)(2,1)S(1)} %add_convert_fusion.1), channel_id=1, source_target_pairs={{0,16},{4,20},{8,24},{12,28},{16,0},{20,4},{24,8},{28,12},{1,17},{... | collective-permute-start | bytes 208904 | tf_op jit(solution)/shard_map/ppermute | solution.py:45
  251.7 2.0 collective-permute-start.28
  255.5 2.3 collective-permute-done.28
  265.5 2.2 fusion.23
  269.8 2.1 collective-permute-done.45
  276.8 2.0 copy.52
  286.1 2.3 maximum_convert_fusion
  (212 shorter events, 85.4 us)
Async XLA Ops:
  3.7 28.1 %collective-permute-start = (bf16[2,1056,128]{2,1,0:T(8,128)(2,1)}, bf16[2,1056,128]{2,1,0:T(8,128)(2,1)}, u32[]{:S(2)}, u32[]{:S(2)}) collective-permute-start(bf16[2,1056,128]{2,1,0:T(8,128)(2,1)} %pad_maximum_fusion.4), channel_id=1, source_target_pairs={{0,2},{1,3},{2,0},{3,1},{4,6},{5,7},{6,4},{7,5},{8,10},{9,11},{10,... | collective-permute-start | bytes 1622024 | tf_op jit(solution)/shard_map/ppermute | solution.py:45
  7.7 22.8 %collective-permute-start.2 = (bf16[2064,128]{1,0:T(8,128)(2,1)}, bf16[2064,128]{1,0:T(8,128)(2,1)}, u32[]{:S(2)}, u32[]{:S(2)}) collective-permute-start(bf16[2064,128]{1,0:T(8,128)(2,1)} %get-tuple-element.97.w0), channel_id=1, source_target_pairs={{0,2},{1,3},{2,0},{3,1},{4,6},{5,7},{6,4},{7,5},{8,10},{9,11},{10,... | collective-permute-start | bytes 1585160 | tf_op jit(solution)/shard_map/ppermute | solution.py:45
  31.7 27.8 %collective-permute-start.3 = (bf16[2,2064,128]{2,1,0:T(8,128)(2,1)S(1)}, bf16[2,2064,128]{2,1,0:T(8,128)(2,1)S(1)}, u32[]{:S(2)}, u32[]{:S(2)}) collective-permute-start(bf16[2,2064,128]{2,1,0:T(8,128)(2,1)S(1)} %pad_maximum_fusion), channel_id=1, source_target_pairs={{0,1},{1,0},{2,3},{3,2},{4,5},{5,4},{6,7},{7,6},{8,9},{9,8},{10,11... | collective-permute-start | bytes 3170312 | tf_op jit(solution)/shard_map/ppermute | solution.py:45
  31.8 14.9 %collective-permute-start.6 = (bf16[2064,128]{1,0:T(8,128)(2,1)S(1)}, bf16[2064,128]{1,0:T(8,128)(2,1)S(1)}, u32[]{:S(2)}, u32[]{:S(2)}) collective-permute-start(bf16[2064,128]{1,0:T(8,128)(2,1)S(1)} %copy-done.11), channel_id=1, source_target_pairs={{0,2},{1,3},{2,0},{3,1},{4,6},{5,7},{6,4},{7,5},{8,10},{9,11},{10,... | collective-permute-start | bytes 1585160 | tf_op jit(solution)/shard_map/ppermute | solution.py:45
  33.6 24.2 %collective-permute-start.4 = (bf16[2,1056,128]{2,1,0:T(8,128)(2,1)S(1)}, bf16[2,1056,128]{2,1,0:T(8,128)(2,1)S(1)}, u32[]{:S(2)}, u32[]{:S(2)}) collective-permute-start(bf16[2,1056,128]{2,1,0:T(8,128)(2,1)S(1)} %pad_maximum_fusion.6), channel_id=1, source_target_pairs={{0,2},{1,3},{2,0},{3,1},{4,6},{5,7},{6,4},{7,5},{8,10},{9,11},{10,... | collective-permute-start | bytes 1622024 | tf_op jit(solution)/shard_map/ppermute | solution.py:45
  35.7 23.0 %collective-permute-start.1 = (bf16[2,1056,128]{2,1,0:T(8,128)(2,1)S(1)}, bf16[2,1056,128]{2,1,0:T(8,128)(2,1)S(1)}, u32[]{:S(2)}, u32[]{:S(2)}) collective-permute-start(bf16[2,1056,128]{2,1,0:T(8,128)(2,1)S(1)} %pad_maximum_fusion.5), channel_id=1, source_target_pairs={{0,1},{1,0},{2,3},{3,2},{4,5},{5,4},{6,7},{7,6},{8,9},{9,8},{10,11... | collective-permute-start | bytes 1622024 | tf_op jit(solution)/shard_map/ppermute | solution.py:45
  46.8 36.0 %collective-permute-start.7 = (bf16[2,2064,128]{2,1,0:T(8,128)(2,1)S(1)}, bf16[2,2064,128]{2,1,0:T(8,128)(2,1)S(1)}, u32[]{:S(2)}, u32[]{:S(2)}) collective-permute-start(bf16[2,2064,128]{2,1,0:T(8,128)(2,1)S(1)} %pad_maximum_fusion.1), channel_id=1, source_target_pairs={{0,1},{1,0},{2,3},{3,2},{4,5},{5,4},{6,7},{7,6},{8,9},{9,8},{10,11... | collective-permute-start | bytes 3170312 | tf_op jit(solution)/shard_map/ppermute | solution.py:45
  58.6 23.3 %collective-permute-start.5 = (bf16[2,1056,128]{2,1,0:T(8,128)(2,1)S(1)}, bf16[2,1056,128]{2,1,0:T(8,128)(2,1)S(1)}, u32[]{:S(2)}, u32[]{:S(2)}) collective-permute-start(bf16[2,1056,128]{2,1,0:T(8,128)(2,1)S(1)} %pad_maximum_fusion.7), channel_id=1, source_target_pairs={{0,1},{1,0},{2,3},{3,2},{4,5},{5,4},{6,7},{7,6},{8,9},{9,8},{10,11... | collective-permute-start | bytes 1622024 | tf_op jit(solution)/shard_map/ppermute | solution.py:45
  129.5 43.8 %collective-permute-start.35 = (bf16[2,256,1024]{2,1,0:T(8,128)(2,1)}, bf16[2,256,1024]{2,1,0:T(8,128)(2,1)S(1)}, u32[]{:S(2)}, u32[]{:S(2)}) collective-permute-start(bf16[2,256,1024]{2,1,0:T(8,128)(2,1)} %get-tuple-element.49), channel_id=1, source_target_pairs={{0,1},{1,0},{2,3},{3,2},{4,5},{5,4},{6,7},{7,6},{8,9},{9,8},{10,11... | collective-permute-start | bytes 3145736 | tf_op jit(solution)/shard_map/ppermute | solution.py:45
  144.7 27.8 %collective-permute-start.8 = (bf16[2,1024,128]{2,1,0:T(8,128)(2,1)}, bf16[2,1024,128]{2,1,0:T(8,128)(2,1)S(1)}, u32[]{:S(2)}, u32[]{:S(2)}) collective-permute-start(bf16[2,1024,128]{2,1,0:T(8,128)(2,1)} %get-tuple-element.42), channel_id=1, source_target_pairs={{0,2},{1,3},{2,0},{3,1},{4,6},{5,7},{6,4},{7,5},{8,10},{9,11},{10,... | collective-permute-start | bytes 1572872 | tf_op jit(solution)/shard_map/ppermute | solution.py:45
  147.7 11.4 %collective-permute-start.31 = (f32[4,1024]{1,0:T(4,128)S(1)}, f32[4,1024]{1,0:T(4,128)S(1)}, u32[]{:S(2)}, u32[]{:S(2)}) collective-permute-start(f32[4,1024]{1,0:T(4,128)S(1)} %add.305), channel_id=1, source_target_pairs={{0,2},{1,3},{2,0},{3,1},{4,6},{5,7},{6,4},{7,5},{8,10},{9,11},{10,... | collective-permute-start | bytes 49160 | tf_op jit(solution)/shard_map/ppermute | solution.py:45
  174.2 14.8 %collective-permute-start.36 = (bf16[256,1024]{1,0:T(8,128)(2,1)S(1)}, bf16[256,1024]{1,0:T(8,128)(2,1)S(1)}, u32[]{:S(2)}, u32[]{:S(2)}) collective-permute-start(bf16[256,1024]{1,0:T(8,128)(2,1)S(1)} %fusion.14), channel_id=1, source_target_pairs={{0,2},{1,3},{2,0},{3,1},{4,6},{5,7},{6,4},{7,5},{8,10},{9,11},{10,... | collective-permute-start | bytes 1572872 | tf_op jit(solution)/shard_map/ppermute | solution.py:45
  178.0 23.0 %collective-permute-start.11 = (bf16[128,2176]{1,0:T(8,128)(2,1)S(1)}, bf16[128,2176]{1,0:T(8,128)(2,1)S(1)}, u32[]{:S(2)}, u32[]{:S(2)}) collective-permute-start(bf16[128,2176]{1,0:T(8,128)(2,1)S(1)} %fusion.11), channel_id=1, source_target_pairs={{0,2},{1,3},{2,0},{3,1},{4,6},{5,7},{6,4},{7,5},{8,10},{9,11},{10,... | collective-permute-start | bytes 1671176 | tf_op jit(solution)/shard_map/ppermute | solution.py:45
  179.6 32.9 %collective-permute-start.21 = (bf16[128,2176]{1,0:T(8,128)(2,1)S(1)}, bf16[128,2176]{1,0:T(8,128)(2,1)S(1)}, u32[]{:S(2)}, u32[]{:S(2)}) collective-permute-start(bf16[128,2176]{1,0:T(8,128)(2,1)S(1)} %fusion.12), channel_id=1, source_target_pairs={{0,2},{1,3},{2,0},{3,1},{4,6},{5,7},{6,4},{7,5},{8,10},{9,11},{10,... | collective-permute-start | bytes 1671176 | tf_op jit(solution)/shard_map/ppermute | solution.py:45
  189.3 23.3 %collective-permute-start.37 = (bf16[256,512]{1,0:T(8,128)(2,1)S(1)}, bf16[256,512]{1,0:T(8,128)(2,1)S(1)}, u32[]{:S(2)}, u32[]{:S(2)}) collective-permute-start(bf16[256,512]{1,0:T(8,128)(2,1)S(1)} %dynamic-slice_convert_fusion.3), channel_id=1, source_target_pairs={{0,4},{4,0},{8,12},{12,8},{16,20},{20,16},{24,28},{28,24},{1,5},{5... | collective-permute-start | bytes 786440 | tf_op jit(solution)/shard_map/ppermute | solution.py:45
  201.1 28.2 %collective-permute-start.12 = (bf16[64,2176]{1,0:T(8,128)(2,1)S(1)}, bf16[64,2176]{1,0:T(8,128)(2,1)S(1)}, u32[]{:S(2)}, u32[]{:S(2)}) collective-permute-start(bf16[64,2176]{1,0:T(8,128)(2,1)S(1)} %dynamic-slice_convert_fusion.2), channel_id=1, source_target_pairs={{0,4},{4,0},{8,12},{12,8},{16,20},{20,16},{24,28},{28,24},{1,5},{5... | collective-permute-start | bytes 835592 | tf_op jit(solution)/shard_map/ppermute | solution.py:45
  214.6 7.2 %collective-permute-start.39 = (bf16[256,128]{1,0:T(8,128)(2,1)S(1)}, bf16[256,128]{1,0:T(8,128)(2,1)S(1)}, u32[]{:S(2)}, u32[]{:S(2)}) collective-permute-start(bf16[256,128]{1,0:T(8,128)(2,1)S(1)} %get-tuple-element.106), channel_id=1, source_target_pairs={{0,16},{4,20},{8,24},{12,28},{16,0},{20,4},{24,8},{28,12},{1,17},{... | collective-permute-start | bytes 196616 | tf_op jit(solution)/shard_map/ppermute | solution.py:45
  217.4 12.1 %collective-permute-start.22 = (bf16[64,2176]{1,0:T(8,128)(2,1)S(1)}, bf16[64,2176]{1,0:T(8,128)(2,1)S(1)}, u32[]{:S(2)}, u32[]{:S(2)}) collective-permute-start(bf16[64,2176]{1,0:T(8,128)(2,1)S(1)} %dynamic-slice_convert_fusion.1), channel_id=1, source_target_pairs={{0,4},{4,0},{8,12},{12,8},{16,20},{20,16},{24,28},{28,24},{1,5},{5... | collective-permute-start | bytes 835592 | tf_op jit(solution)/shard_map/ppermute | solution.py:45
  224.9 9.1 %collective-permute-start.42 = (bf16[128,256]{0,1:T(8,128)(2,1)S(1)}, bf16[128,256]{0,1:T(8,128)(2,1)S(1)}, u32[]{:S(2)}, u32[]{:S(2)}) collective-permute-start(bf16[128,256]{0,1:T(8,128)(2,1)S(1)} %fusion.1), channel_id=1, source_target_pairs={{0,16},{4,20},{8,24},{12,28},{16,0},{20,4},{24,8},{28,12},{1,17},{... | collective-permute-start | bytes 196616 | tf_op jit(solution)/shard_map/ppermute | solution.py:45
  229.4 10.9 %collective-permute-start.13 = (bf16[16,2176]{1,0:T(8,128)(2,1)S(1)}, bf16[16,2176]{1,0:T(8,128)(2,1)S(1)}, u32[]{:S(2)}, u32[]{:S(2)}) collective-permute-start(bf16[16,2176]{1,0:T(8,128)(2,1)S(1)} %get-tuple-element.85), channel_id=1, source_target_pairs={{0,8},{4,12},{8,0},{12,4},{16,24},{20,28},{24,16},{28,20},{1,9},{5... | collective-permute-start | bytes 208904 | tf_op jit(solution)/shard_map/ppermute | solution.py:45
  229.5 10.9 %collective-permute-start.14 = (bf16[16,2176]{1,0:T(8,128)(2,1)S(1)}, bf16[16,2176]{1,0:T(8,128)(2,1)S(1)}, u32[]{:S(2)}, u32[]{:S(2)}) collective-permute-start(bf16[16,2176]{1,0:T(8,128)(2,1)S(1)} %get-tuple-element.87), channel_id=1, source_target_pairs={{0,16},{4,20},{8,24},{12,28},{16,0},{20,4},{24,8},{28,12},{1,17},{... | collective-permute-start | bytes 208904 | tf_op jit(solution)/shard_map/ppermute | solution.py:45
  231.7 10.2 %collective-permute-start.15 = (bf16[16,2176]{1,0:T(8,128)(2,1)S(1)}, bf16[16,2176]{1,0:T(8,128)(2,1)S(1)}, u32[]{:S(2)}, u32[]{:S(2)}) collective-permute-start(bf16[16,2176]{1,0:T(8,128)(2,1)S(1)} %get-tuple-element.86), channel_id=1, source_target_pairs={{0,24},{4,28},{8,16},{12,20},{16,8},{20,12},{24,0},{28,4},{1,25},{... | collective-permute-start | bytes 208904 | tf_op jit(solution)/shard_map/ppermute | solution.py:45
  234.0 8.8 %collective-permute-start.23 = (bf16[16,2176]{1,0:T(8,128)(2,1)S(1)}, bf16[16,2176]{1,0:T(8,128)(2,1)S(1)}, u32[]{:S(2)}, u32[]{:S(2)}) collective-permute-start(bf16[16,2176]{1,0:T(8,128)(2,1)S(1)} %get-tuple-element.80), channel_id=1, source_target_pairs={{0,8},{4,12},{8,0},{12,4},{16,24},{20,28},{24,16},{28,20},{1,9},{5... | collective-permute-start | bytes 208904 | tf_op jit(solution)/shard_map/ppermute | solution.py:45
  234.0 12.3 %collective-permute-start.24 = (bf16[16,2176]{1,0:T(8,128)(2,1)S(1)}, bf16[16,2176]{1,0:T(8,128)(2,1)S(1)}, u32[]{:S(2)}, u32[]{:S(2)}) collective-permute-start(bf16[16,2176]{1,0:T(8,128)(2,1)S(1)} %get-tuple-element.82), channel_id=1, source_target_pairs={{0,16},{4,20},{8,24},{12,28},{16,0},{20,4},{24,8},{28,12},{1,17},{... | collective-permute-start | bytes 208904 | tf_op jit(solution)/shard_map/ppermute | solution.py:45
  240.4 18.6 %collective-permute-start.44 = (bf16[512,256]{0,1:T(8,128)(2,1)S(1)}, bf16[512,256]{0,1:T(8,128)(2,1)S(1)}, u32[]{:S(2)}, u32[]{:S(2)}) collective-permute-start(bf16[512,256]{0,1:T(8,128)(2,1)S(1)} %get-tuple-element.125), channel_id=1, source_target_pairs={{0,4},{4,0},{8,12},{12,8},{16,20},{20,16},{24,28},{28,24},{1,5},{5... | collective-permute-start | bytes 786440 | tf_op jit(solution)/shard_map/ppermute | solution.py:45
  242.0 7.3 %collective-permute-start.16 = (bf16[16,2176]{1,0:T(8,128)(2,1)S(1)}, bf16[16,2176]{1,0:T(8,128)(2,1)S(1)}, u32[]{:S(2)}, u32[]{:S(2)}) collective-permute-start(bf16[16,2176]{1,0:T(8,128)(2,1)S(1)} %add_convert_fusion.1), channel_id=1, source_target_pairs={{0,8},{4,12},{8,0},{12,4},{16,24},{20,28},{24,16},{28,20},{1,9},{5... | collective-permute-start | bytes 208904 | tf_op jit(solution)/shard_map/ppermute | solution.py:45
  242.8 8.9 %collective-permute-start.17 = (bf16[16,2176]{1,0:T(8,128)(2,1)S(1)}, bf16[16,2176]{1,0:T(8,128)(2,1)S(1)}, u32[]{:S(2)}, u32[]{:S(2)}) collective-permute-start(bf16[16,2176]{1,0:T(8,128)(2,1)S(1)} %add_convert_fusion.1), channel_id=1, source_target_pairs={{0,16},{4,20},{8,24},{12,28},{16,0},{20,4},{24,8},{28,12},{1,17},{... | collective-permute-start | bytes 208904 | tf_op jit(solution)/shard_map/ppermute | solution.py:45
  246.3 7.4 %collective-permute-start.18 = (bf16[16,2176]{1,0:T(8,128)(2,1)S(1)}, bf16[16,2176]{1,0:T(8,128)(2,1)S(1)}, u32[]{:S(2)}, u32[]{:S(2)}) collective-permute-start(bf16[16,2176]{1,0:T(8,128)(2,1)S(1)} %add_convert_fusion.1), channel_id=1, source_target_pairs={{0,24},{4,28},{8,16},{12,20},{16,8},{20,12},{24,0},{28,4},{1,25},{... | collective-permute-start | bytes 208904 | tf_op jit(solution)/shard_map/ppermute | solution.py:45
  247.2 8.3 %collective-permute-start.26 = (bf16[16,2176]{1,0:T(8,128)(2,1)S(1)}, bf16[16,2176]{1,0:T(8,128)(2,1)S(1)}, u32[]{:S(2)}, u32[]{:S(2)}) collective-permute-start(bf16[16,2176]{1,0:T(8,128)(2,1)S(1)} %add_convert_fusion), channel_id=1, source_target_pairs={{0,8},{4,12},{8,0},{12,4},{16,24},{20,28},{24,16},{28,20},{1,9},{5... | collective-permute-start | bytes 208904 | tf_op jit(solution)/shard_map/ppermute | solution.py:45
  254.6 10.3 %collective-permute-start.19 = (bf16[64,2176]{1,0:T(8,128)(2,1)}, bf16[64,2176]{1,0:T(8,128)(2,1)}, u32[]{:S(2)}, u32[]{:S(2)}) collective-permute-start(bf16[64,2176]{1,0:T(8,128)(2,1)} %get-tuple-element.119), channel_id=1, source_target_pairs={{0,4},{4,0},{8,12},{12,8},{16,20},{20,16},{24,28},{28,24},{1,5},{5... | collective-permute-start | bytes 835592 | tf_op jit(solution)/shard_map/ppermute | solution.py:45
  261.9 10.0 %collective-permute-start.45 = (bf16[1,1024,256]{2,1,0:T(8,128)(2,1)}, bf16[1,1024,256]{2,1,0:T(8,128)(2,1)}, u32[]{:S(2)}, u32[]{:S(2)}) collective-permute-start(bf16[1,1024,256]{2,1,0:T(8,128)(2,1)} %get-tuple-element.100), channel_id=1, source_target_pairs={{0,2},{1,3},{2,0},{3,1},{4,6},{5,7},{6,4},{7,5},{8,10},{9,11},{10,... | collective-permute-start | bytes 1572872 | tf_op jit(solution)/shard_map/ppermute | solution.py:45
  274.4 9.7 %collective-permute-start.46 = (bf16[1,2,1024,256]{3,2,1,0:T(8,128)(2,1)}, bf16[1,2,1024,256]{3,2,1,0:T(8,128)(2,1)}, u32[]{:S(2)}, u32[]{:S(2)}) collective-permute-start(bf16[1,2,1024,256]{3,2,1,0:T(8,128)(2,1)} %get-tuple-element.62), channel_id=1, source_target_pairs={{0,1},{1,0},{2,3},{3,2},{4,5},{5,4},{6,7},{7,6},{8,9},{9,8},{10,11... | collective-permute-start | bytes 3145736 | tf_op jit(solution)/shard_map/ppermute | solution.py:45
  (38 other events, 443.5 us)

commit v3 on v2

--- a/solution.py
+++ b/solution.py
@@ -49,77 +49,60 @@
     return lax.optimization_barrier((values,) + others)[0]
 
 
-def in_order(pieces, place, dim):
-    stacked = jnp.stack(pieces)
-    return jnp.concatenate(
-        [
-            lax.dynamic_index_in_dim(stacked, place ^ j, 0, keepdims=False)
-            for j in range(len(pieces))
-        ],
-        dim,
-    )
-
-
 def frames_out(values, me, own):
     padded = jnp.pad(values, ((HALO, HALO), (0, 0)))
-
-    def rows(k):
-        return lax.dynamic_slice_in_dim(padded, (me ^ k) * own, own + 2 * HALO, 0)
-
-    return rows(0), rows(1), jnp.stack([rows(2), rows(3)])
-
-
-def exchange_steps(count):
-    steps, stride, rest = [], 1, count
-    while rest > 1:
-        radix = 2 if (rest.bit_length() - 1) % 2 else 4
-        steps.append((stride, radix))
-        stride, rest = stride * radix, rest // radix
-    return steps
-
-
-def scatter_sum_dp(total, place, dim):
-    for stride, radix in exchange_steps(lax.axis_size("dp")):
-        digit = (place // stride) % radix
-        size = total.shape[dim] // radix
-        summed = lax.dynamic_slice_in_dim(total, digit * size, size, dim)
-        for k in range(1, radix):
-            piece = lax.dynamic_slice_in_dim(total, (digit ^ k) * size, size, dim).astype(BF16)
-            summed = summed + swap(piece, "dp", k * stride).astype(F32)
-        total = summed
-    return total
-
-
-def gather_dp(block, place):
-    for stride, radix in reversed(exchange_steps(lax.axis_size("dp"))):
-        digit = (place // stride) % radix
-        pieces = [block] + [swap(block, "dp", k * stride) for k in range(1, radix)]
-        block = in_order(pieces, digit, 0)
-    return block
-
-
-def sum_blocks(sent, kept, place):
-    held = kept.astype(F32) + swap(sent, "mp", 1).astype(F32)
-    held = held[0] + swap(held[1].astype(BF16), "mp", 2).astype(F32)
-    return gather_dp(scatter_sum_dp(held, place, 0).astype(BF16), place)
-
-
-def sum_everywhere(values, width):
-    bit = 1
-    while bit < width:
-        values = values + swap(values, "mp", bit)
-        bit *= 2
-    bit = 1
-    while bit < lax.axis_size("dp"):
-        values = values + swap(values, "dp", bit)
-        bit *= 2
-    return values
+    return [
+        lax.dynamic_slice_in_dim(padded, (me ^ k) * own, own + 2 * HALO, 0) for k in range(4)
+    ]
+
+
+def bits_of(count):
+    return [1 << i for i in range(count.bit_length() - 1)]
+
+
+def halves(total, place, bit, dim):
+    size = total.shape[dim] // 2
+    side = (place // bit) % 2
+    mine = lax.dynamic_slice_in_dim(total, side * size, size, dim)
+    other = lax.dynamic_slice_in_dim(total, (1 - side) * size, size, dim)
+    return mine, other.astype(BF16)
+
+
+def scatter_step(total, place, bit, dim):
+    mine, other = halves(total, place, bit, dim)
+    return mine + swap(other, "dp", bit).astype(F32)
+
+
+def gather_step(block, axis, bit):
+    return jnp.concatenate([block, swap(block, axis, bit)], 0)
+
+
+def first_of(place, size, bits):
+    first = jnp.int32(0)
+    for bit in bits:
+        size = size // 2
+        first = first + ((place // bit) % 2) * size
+    return first
+
+
+def columns_of(me, k):
+    return pl.ds(pl.multiple_of((me ^ k) * LANES, LANES), LANES)
 
 
 def assemble(me, target, pieces):
     for k, piece in enumerate(pieces):
-        columns = pl.ds(pl.multiple_of((me ^ k) * LANES, LANES), LANES)
-        target[:, columns] = piece[...]
+        target[:, columns_of(me, k)] = piece[...]
+
+
+def assemble_halves(me, side, target, own, across, halves):
+    target[:, columns_of(me, 0)] = own[...]
+    target[:, columns_of(me, 1)] = across[...]
+    for k in (2, 3):
+        for j in range(2):
+            piece = halves[2 * (k - 2) + j]
+            rows = piece.shape[0]
+            start = pl.multiple_of((side ^ j) * rows, 16)
+            target[pl.ds(start, rows), columns_of(me, k)] = piece[...]
 
 
 def taps_into(source, target, first_ok, last_ok, rows, depth):
@@ -134,13 +117,13 @@
 
 
 def encoder_kernel(
-    me_ref, f0, f1, f2, f3, w0, w1, w2, w3, prev_ok, next_ok,
+    me_ref, f0, f1, f2, f3, w0, w1, w2a, w2b, w3a, w3b, prev_ok, next_ok,
     hidden_ref, mid_ref, latent_ref, feat, weight, act, act3,
 ):
     me = me_ref[0]
     rows, depth = hidden_ref.shape
     assemble(me, feat, (f0, f1, f2, f3))
-    assemble(me, weight, (w0, w1, w2, w3))
+    assemble_halves(me, me_ref[1], weight, w0, w1, (w2a, w2b, w3a, w3b))
     step = rows // 3
     for r in range(0, rows, step):
         act[8 + r : 8 + r + step, :] = (
@@ -202,7 +185,7 @@
     ones3 = jnp.where(lane == 0, 1.0, 0.0).astype(BF16)
     ones1 = jnp.where(lane == 1, 1.0, 0.0).astype(BF16)
     for k in range(4):
-        columns = pl.ds(pl.multiple_of((me ^ k) * LANES, LANES), LANES)
+        columns = columns_of(me, k)
         left = grad[here, columns]
         left1 = grad1[here, columns]
         target = (kept, sent)[k % 2].at[k // 2]
@@ -257,7 +240,7 @@
 
 
 def quantize_back_kernel(
-    group_ref, grad_ref, prob_ref, first_ref, second_ref, books, turned,
+    group_ref, grad_ref, prob_ref, first_ref, second_ref, books, turned, usage,
     out_ref, table_ref, total, columns, *, own, levels,
 ):
     step = pl.program_id(0)
@@ -293,21 +276,31 @@
 
     @pl.when(step == pl.num_programs(0) - 1)
     def _():
+        depth = turned.shape[2]
         for level in range(levels):
-            table_ref[level] = (
+            table_ref[level, 0:depth, :] = (
                 total[level] - scale * columns[level] * turned[0, level].astype(F32)
             ).astype(BF16)
+            row = lax.broadcasted_iota(jnp.int32, (16, total.shape[2]), 0)
+            table_ref[level, depth : depth + 16, :] = jnp.where(
+                row == 0, usage[0, level], 0.0
+            ).astype(BF16)
 
 
 def encoder_grad_kernel(
-    me_ref, grad_latent, hidden, mid, f0, f1, f2, f3, w0, w1, w2, w3, prev_ok, next_ok,
-    sent, kept, out_sent, out_kept, feat, weight, act, act3, low,
+    me_ref, grad_mine, grad_other, hidden, mid, f0, f1, f2, f3,
+    w0, w1, w2a, w2b, w3a, w3b, prev_ok, next_ok,
+    sent, kept, o0, o1, o2, o3, feat, weight, act, act3, low, grad_latent,
 ):
     me = me_ref[0]
-    rows, depth = grad_latent.shape
+    rows, depth = hidden.shape
     own = rows - 2 * HALO
+    half = grad_mine.shape[1]
+    side = me_ref[2]
+    grad_latent[:, pl.ds(pl.multiple_of(side * half, half), half)] = grad_mine[...]
+    grad_latent[:, pl.ds(pl.multiple_of((1 - side) * half, half), half)] = grad_other[...]
     assemble(me, feat, (f0, f1, f2, f3))
-    assemble(me, weight, (w0, w1, w2, w3))
+    assemble_halves(me, me_ref[1], weight, w0, w1, (w2a, w2b, w3a, w3b))
     step = rows // 3
     for r in range(0, rows, step):
         act[8 + r : 8 + r + step, :] = (
@@ -330,9 +323,17 @@
             grad_latent[here, :].astype(F32)
             + elu_slope(feat[here, :].astype(F32)) * input_grad(act3, weight, here, depth)
         ).astype(BF16)
-    for k in range(4):
-        columns = pl.ds(pl.multiple_of((me ^ k) * LANES, LANES), LANES)
-        (out_kept, out_sent)[k // 2][k % 2] = feat[HALO : HALO + own, columns]
+    for k, out in enumerate((o0, o1, o2, o3)):
+        out[...] = feat[HALO : HALO + own, columns_of(me, k)]
+
+
+def place_kernel(mask_ref, *refs, block):
+    out, first = refs[-1], 0
+    for ref in refs[:-1]:
+        for r in range(0, ref.shape[0], block):
+            start = pl.multiple_of((first + r) ^ mask_ref[0], block)
+            out[pl.ds(start, block), :] = ref[r : r + block, :].astype(F32)
+        first += ref.shape[0]
 
 
 def whole(count, smem_first=False):
@@ -377,7 +378,29 @@
     own = frames // width
     rows = own + 2 * HALO
     depth = cols * width
-    me_row = me.reshape(1)
+    side, level_side = me % 2, me // 2
+    dp_bits = bits_of(n_dp)
+    where_row = jnp.stack([me, place % 2, side])
+
+    def pack(conv3, conv1, biases):
+        rows32 = jnp.pad(jnp.stack(biases), ((0, 32 - len(biases)), (0, 0)))
+        return jnp.concatenate([conv3.reshape(3 * depth, cols), conv1, rows32], 0)
+
+    enc_own = pack(enc_conv3, enc_conv1, [enc_bias3, enc_bias1])
+    half_rows = enc_own.shape[0] // 2
+    enc_half = lax.dynamic_slice_in_dim(enc_own, (place % 2) * half_rows, half_rows, 0)
+    enc_2a = swap(enc_half, "mp", 2)
+    frames_of = frames_out(after(features, enc_half), me, own)
+    feat = [frames_of[0]] + [swap(frames_of[k], "mp", k) for k in (1, 2, 3)]
+    enc_1 = swap(enc_own, "mp", 1)
+    enc_2b = swap(enc_2a, "dp", 1)
+    enc_3a = swap(enc_2a, "mp", 1)
+    enc_3b = swap(enc_2b, "mp", 1)
+    enc = (enc_own, enc_1, enc_2a, enc_2b, enc_3a, enc_3b)
+
+    dec_own = pack(dec_conv3, dec_conv1, [dec_bias3])
+    dec_1 = swap(after(dec_own, enc_2a), "mp", 1)
+    dec_2 = swap(after(dec_own, feat[2], feat[3]), "mp", 2)
 
     clip_ends = jnp.cumsum(lengths[0])
     starts = clip_ends - lengths[0]
@@ -385,30 +408,6 @@
     is_start = jnp.any(positions[:, None] == starts[None, :], axis=1) | (positions == frames)
     ok = jnp.where(is_start, 0.0, 1.0).astype(F32)[:, None]
     prev_ok, next_ok = ok[:-1], ok[1:]
-
-    def pack(conv3, conv1, biases):
-        rows16 = jnp.pad(jnp.stack(biases), ((0, 16 - len(biases)), (0, 0)))
-        return jnp.concatenate([conv3.reshape(3 * depth, cols), conv1, rows16], 0)
-
-    f0, f1, f23 = frames_out(features, me, own)
-    enc_own = pack(enc_conv3, enc_conv1, [enc_bias3, enc_bias1])
-    got = swap(f23, "mp", 2)
-    enc_other = swap(enc_own, "mp", 2)
-    feat = (f0, got[0])
-    other = swap(jnp.stack([f1, got[1]]), "mp", 1)
-    feat = (f0, other[0], got[0], other[1])
-    enc = swap(jnp.stack([enc_own, enc_other]), "mp", 1)
-    enc = (enc_own, enc[0], enc_other, enc[1])
-
-    c0, c1, c23 = frames_out(out_cotangent, me, own)
-    dec_own = pack(dec_conv3, dec_conv1, [dec_bias3])
-    dec_start, cot_start = after((dec_own, c23), enc_other, got)
-    dec_other = swap(dec_start, "mp", 2)
-    got = swap(cot_start, "mp", 2)
-    other = swap(jnp.stack([c1, got[1]]), "mp", 1)
-    cot = (c0, other[0], got[0], other[1])
-    dec = swap(jnp.stack([dec_own, dec_other]), "mp", 1)
-    dec = (dec_own, dec[0], dec_other, dec[1])
 
     books_f = codebooks.astype(F32)
     norms = jnp.sum(books_f * books_f, axis=3) * (LOG2E / SOFTMAX_WARMTH)
@@ -422,17 +421,22 @@
             shaped((rows, depth), BF16),
             shaped((rows, depth), BF16),
         ),
-        in_specs=whole(11, True),
+        in_specs=whole(13, True),
         out_specs=tuple(whole(3)),
         scratch_shapes=[
             pltpu.VMEM((rows, depth), BF16),
-            pltpu.VMEM((4 * depth + 16, depth), BF16),
+            pltpu.VMEM((4 * depth + 32, depth), BF16),
             pltpu.VMEM((rows + 16, depth), F32),
             pltpu.VMEM((rows, 3 * depth), BF16),
         ],
         compiler_params=PARAMS,
         cost_estimate=cost(8 * rows * depth * depth, 12e6),
-    )(me_row, *feat, *enc, prev_ok, next_ok)
+    )(where_row, *feat, *enc, prev_ok, next_ok)
+
+    dec_3 = swap(after(dec_2, latent), "mp", 1)
+    dec = (dec_own, dec_1, dec_2, dec_3)
+    frames_of = frames_out(after(out_cotangent, dec_2), me, own)
+    cot = [frames_of[0]] + [swap(frames_of[k], "mp", k) for k in (1, 2, 3)]
 
     step = rows // 3
     quant, usage, prob, second = pl.pallas_call(
@@ -458,7 +462,6 @@
         compiler_params=PARAMS,
         cost_estimate=cost(16 * rows * num_codes * group_dim, 30e6),
     )(latent, codebooks, norms)
-    usage_all = sum_everywhere(usage.reshape(groups * levels, num_codes), width)
 
     packed = 4 * depth + LANES
     grad_quant, dec_sent, dec_kept = pl.pallas_call(
@@ -472,7 +475,7 @@
         out_specs=tuple(whole(3)),
         scratch_shapes=[
             pltpu.VMEM((rows, depth), BF16),
-            pltpu.VMEM((4 * depth + 16, depth), BF16),
+            pltpu.VMEM((4 * depth + 32, depth), BF16),
             pltpu.VMEM((rows + 16, depth), F32),
             pltpu.VMEM((rows, 3 * depth), BF16),
             pltpu.VMEM((rows, depth), BF16),
@@ -480,9 +483,9 @@
         ],
         compiler_params=PARAMS,
         cost_estimate=cost(24 * rows * depth * depth, 20e6),
-    )(me_row, quant, *cot, *dec, prev_ok, next_ok)
-
-    def quantize_back(group):
+    )(where_row, quant, *cot, *dec, prev_ok, next_ok)
+
+    def quantize_back(group, grads):
         return pl.pallas_call(
             functools.partial(quantize_back_kernel, own=own, levels=levels),
             grid_spec=pltpu.PrefetchScalarGridSpec(
@@ -495,10 +498,11 @@
                     pl.BlockSpec((levels - 1, step, group_dim), lambda i, g: (0, i, g[0])),
                     pl.BlockSpec((1, levels, num_codes, group_dim), lambda i, g: (g[0], 0, 0, 0)),
                     pl.BlockSpec((1, levels, group_dim, num_codes), lambda i, g: (g[0], 0, 0, 0)),
+                    pl.BlockSpec((1, levels, 1, num_codes), lambda i, g: (g[0], 0, 0, 0)),
                 ],
                 out_specs=(
                     pl.BlockSpec((step, group_dim), lambda i, g: (i, 0)),
-                    pl.BlockSpec((levels, group_dim, num_codes), lambda i, g: (0, 0, 0)),
+                    pl.BlockSpec((levels, group_dim + 16, num_codes), lambda i, g: (0, 0, 0)),
                 ),
                 scratch_shapes=[
                     pltpu.VMEM((levels, group_dim, num_codes), F32),
@@ -507,53 +511,67 @@
             ),
             out_shape=(
                 shaped((rows, group_dim), BF16),
-                shaped((levels, group_dim, num_codes), BF16),
+                shaped((levels, group_dim + 16, num_codes), BF16),
             ),
             compiler_params=PARAMS,
             cost_estimate=cost(16 * rows * num_codes * group_dim, 15e6),
-        )(group.reshape(1), grad_quant, prob, latent, second, codebooks, turned)
-
-    side, level_side = me % 2, me // 2
-    grad_other, table_other = quantize_back(1 - side)
-    grad_mine, table_mine = quantize_back(side)
-    grad_latent = jnp.where(
-        side == 0,
-        jnp.concatenate([grad_mine, grad_other], 1),
-        jnp.concatenate([grad_other, grad_mine], 1),
+        )(group.reshape(1), grads, prob, latent, second, codebooks, turned, usage)
+
+    grad_other, table_other = quantize_back(1 - side, grad_quant)
+    dec_got = swap(dec_sent, "mp", 1)
+    dec_held = dec_kept + after(dec_got, table_other).astype(F32)
+    dec_x = swap(dec_held[1].astype(BF16), "mp", 2)
+    table_got = swap(table_other, "mp", 1)
+    grad_mine, table_mine = quantize_back(side, after(grad_quant, dec_held))
+    dec_x, table_got, grad_mine, table_mine = lax.optimization_barrier(
+        (dec_x, table_got, grad_mine, table_mine)
     )
-
-    enc_sent, enc_kept, out_sent, out_kept = pl.pallas_call(
+    dec_held = dec_held[0] + dec_x.astype(F32)
+    tables = table_mine.astype(F32) + table_got.astype(F32)
+    book_held = lax.dynamic_index_in_dim(tables, level_side, 0, keepdims=False)
+    sent = lax.dynamic_index_in_dim(tables, 1 - level_side, 0, keepdims=False)
+    sent = sent.astype(BF16)
+    dec_mine, dec_y = halves(dec_held, place, dp_bits[0], 0)
+    grad_mine = after(grad_mine, sent, dec_y)
+    book_x = swap(sent, "mp", 2)
+    dec_y = swap(dec_y, "dp", dp_bits[0])
+
+    enc_sent, enc_kept, *outs = pl.pallas_call(
         encoder_grad_kernel,
         out_shape=(
             shaped((2, cols, packed), BF16),
             shaped((2, cols, packed), F32),
-            shaped((2, own, cols), BF16),
-            shaped((2, own, cols), BF16),
-        ),
-        in_specs=whole(14, True),
-        out_specs=tuple(whole(4)),
+        )
+        + (shaped((own, cols), BF16),) * 4,
+        in_specs=whole(17, True),
+        out_specs=tuple(whole(6)),
         scratch_shapes=[
             pltpu.VMEM((rows, depth), BF16),
-            pltpu.VMEM((4 * depth + 16, depth), BF16),
+            pltpu.VMEM((4 * depth + 32, depth), BF16),
             pltpu.VMEM((rows + 16, depth), F32),
             pltpu.VMEM((rows, 3 * depth), BF16),
+            pltpu.VMEM((rows, depth), BF16),
             pltpu.VMEM((rows, depth), BF16),
         ],
         compiler_params=PARAMS,
         cost_estimate=cost(16 * rows * depth * depth, 20e6),
-    )(me_row, grad_latent, hidden_enc, act_mid, *feat, *enc, prev_ok, next_ok)
-
-    tables = table_mine.astype(F32) + swap(table_other, "mp", 1).astype(F32)
-    kept = lax.dynamic_index_in_dim(tables, level_side, 0, keepdims=False)
-    sent = lax.dynamic_index_in_dim(tables, 1 - level_side, 0, keepdims=False)
-    held = kept + swap(sent.astype(BF16), "mp", 2).astype(F32)
-    held = scatter_sum_dp(held, place, 1)
-    codes = held.shape[1]
-    first = jnp.int32(0)
-    size = num_codes
-    for stride, radix in exchange_steps(n_dp):
-        size = size // radix
-        first = first + ((place // stride) % radix) * size
+    )(where_row, grad_mine, grad_other, hidden_enc, act_mid, *feat, *enc, prev_ok, next_ok)
+
+    enc_sent, book_x, dec_y = lax.optimization_barrier((enc_sent, book_x, dec_y))
+    enc_got = swap(enc_sent, "mp", 1)
+    book_held = book_held + book_x.astype(F32)
+    dec_held = dec_mine + dec_y.astype(F32)
+    enc_held = enc_kept + enc_got.astype(F32)
+    enc_held = enc_held[0] + swap(enc_held[1].astype(BF16), "mp", 2).astype(F32)
+    for bit in dp_bits:
+        book_held = scatter_step(book_held, place, bit, 1)
+    for bit in dp_bits[1:]:
+        dec_held = scatter_step(dec_held, place, bit, 0)
+    for bit in dp_bits:
+        enc_held = scatter_step(enc_held, place, bit, 0)
+
+    codes = book_held.shape[1]
+    first = first_of(place, num_codes, dp_bits)
 
     def own_codes(array):
         start = (side, level_side, first) + (jnp.int32(0),) * (array.ndim - 3)
@@ -561,37 +579,56 @@
 
     index = own_codes(buffer_index)
     one_hot = index[:, None] == jnp.arange(code_buffer.shape[0], dtype=jnp.int32)[None, :]
-    halves = lax.dynamic_slice_in_dim(code_buffer, side * group_dim, group_dim, 1)
-    chosen = dot_nn(one_hot.astype(BF16), halves)
+    buffer_half = lax.dynamic_slice_in_dim(code_buffer, side * group_dim, group_dim, 1)
+    chosen = dot_nn(one_hot.astype(BF16), buffer_half)
     share = num_codes / (frames * n_dp)
-    ratio = own_codes(usage_all.reshape(groups, levels, num_codes)) * share
-    refresh = jax.nn.sigmoid(SHARPNESS * (THRESHOLD - ratio))[:, None]
-    stepped = own_codes(codebooks).astype(F32) - (STEP_SCALE * share) * held.T
+    book_held = book_held.T
+    ratio = book_held[:, group_dim : group_dim + 1] * share
+    refresh = jax.nn.sigmoid(SHARPNESS * (THRESHOLD - ratio))
+    stepped = own_codes(codebooks).astype(F32) - (STEP_SCALE * share) * book_held[:, :group_dim]
     fresh = ((1.0 - refresh) * stepped + refresh * chosen).astype(BF16)
-    fresh = gather_dp(fresh, place)
-    fresh = in_order([fresh[None], swap(fresh[None], "mp", 2)], level_side, 0)
-    fresh = in_order([fresh[None], swap(fresh[None], "mp", 1)], side, 0)
-    new_codebooks = fresh.astype(F32)
-
-    def unpack(total):
-        total = total.T.astype(F32)
+    for bit in reversed(dp_bits):
+        fresh = gather_step(fresh, "dp", bit)
+    fresh = gather_step(fresh, "mp", 2)
+    fresh_other = swap(fresh, "mp", 1)
+
+    def put(mask, block, total, *pieces):
+        return pl.pallas_call(
+            functools.partial(place_kernel, block=block),
+            out_shape=shaped((total, pieces[0].shape[1]), F32),
+            in_specs=whole(1 + len(pieces), True),
+            out_specs=whole(1)[0],
+            compiler_params=PARAMS,
+            cost_estimate=cost(0, 8 * total * pieces[0].shape[1]),
+        )(mask.reshape(1), *pieces)
+
+    mask = (side * levels + level_side) * num_codes + first
+    new_codebooks = put(mask, codes, groups * levels * num_codes, fresh, fresh_other)
+
+    turn = jnp.arange(cols, dtype=jnp.int32)
+    turn = (turn[:, None] ^ first_of(place, cols, dp_bits)) == turn[None, :]
+    turn = turn.astype(BF16)
+
+    def unpack(held):
+        held = held.astype(BF16)
+        for bit in reversed(dp_bits):
+            held = gather_step(held, "dp", bit)
+        biases = dot_tn(held[:, 4 * depth :], turn)
         return (
-            total[: 3 * depth].reshape(3, depth, cols),
-            total[4 * depth],
-            total[3 * depth : 4 * depth],
-            total[4 * depth + 1],
+            dot_tn(held[:, : 3 * depth], turn).reshape(3, depth, cols),
+            biases[0],
+            dot_tn(held[:, 3 * depth : 4 * depth], turn),
+            biases[1],
         )
 
-    got = swap(out_sent, "mp", 2)
-    kept = jnp.stack([out_kept[0], got[0]])
-    other = swap(jnp.stack([out_kept[1], got[1]]), "mp", 1)
-    grad_features = in_order([kept[0], other[0], kept[1], other[1]], me, 0).astype(F32)
+    outs = [outs[0]] + [swap(outs[k], "mp", k) for k in (1, 2, 3)]
+    grad_features = put(me * own, own, frames, *outs)
 
     return (
         grad_features,
-        *unpack(sum_blocks(enc_sent, enc_kept, place)),
-        *unpack(sum_blocks(dec_sent, dec_kept, place)),
-        new_codebooks,
+        *unpack(enc_held),
+        *unpack(dec_held),
+        new_codebooks.reshape(codebooks.shape),
     )
 
 

time: 293 us -> 246 us (0.84); the launches traced: 289 us -> 247 us
  starting transfers between devices: 56.7 us -> 32 us
  other arithmetic: 27.9 us -> 13.3 us
  waiting for transfers between devices: 91.5 us -> 82.2 us
  local copies, waits for them, and re-layouts: 30.6 us -> 35.3 us
  matrix products: 1.24 us -> 5.88 us
    ppermute x47 -> x43, starting transfers between devices: 56.7 us -> 32 us  [swap(): return lax.ppermute(values, axis, [(i, i ^ bits) for i in range(size)])]
    unnamed x47 -> x56, local copies, waits for them, and re-layouts: 5.55 us -> 20.4 us
    ppermute x47 -> x43, waiting for transfers between devices: 91.5 us -> 82.2 us  [swap(): return lax.ppermute(values, axis, [(i, i ^ bits) for i in range(size)])]
    pallas_call x2, Pallas kernels: 32.8 us -> 24.4 us  [quantize_back(): pl.pallas_call(functools.partial(quantize_back_kernel, own=own, levels=le...]
    another operation x17 -> x3, other arithmetic: 8.43 us -> 1.66 us  [the longest x1 0.83 us: pack(): rows32 = jnp.pad(jnp.stack(biases), ((0, 32 - len(biases)), (0, 0)))]
    squeeze x12 -> x2, local copies, waits for them, and re-layouts: 7.57 us -> 1.04 us  [unpack(): biases[1]]
    pallas_call x0 -> x2, Pallas kernels: none -> 6.47 us  [put(): pl.pallas_call(functools.partial(place_kernel, block=block), out_shape=sh...]
    convert_element_type x6 -> x2, other arithmetic: 5.59 us -> 0.03 us  [unpack(): held = held.astype(BF16)]
  transfers between devices with their start and end apart: 47 -> 43, of which waited for: 19 -> 22; matrix products, arithmetic and copies ran while one was open for 16% -> 17% of each run, Pallas kernels for 12% -> 26%
where the time goes in v3:
time: 246 us; the launch traced here: 247 us
  waiting for transfers between devices  82.2 us (33%)
  Pallas kernels  77.3 us (31%)
  local copies, waits for them, and re-layouts  35.3 us (14%)
  starting transfers between devices  32 us (13%)
  other arithmetic  13.3 us (5%)
  matrix products  5.88 us (2%)
    ppermute x43, waiting for transfers between devices, swap(): return lax.ppermute(values, axis, [(i, i ^ bits) for i in range(size)])  82.2 us
    ppermute x43, starting transfers between devices, swap(): return lax.ppermute(values, axis, [(i, i ^ bits) for i in range(size)])  32 us
    pallas_call x2, Pallas kernels, quantize_back(): pl.pallas_call(functools.partial(quantize_back_kernel, own=own, levels=le...  24.4 us
    unnamed x56, local copies, waits for them, and re-layouts  20.4 us
    pallas_call x1, Pallas kernels, body(): pl.pallas_call(decoder_kernel, out_shape=(shaped((rows, depth), F32), sha...  13.1 us
    pallas_call x1, Pallas kernels, body(): pl.pallas_call(functools.partial(quantize_kernel, own=own), grid=(3,), ou...  13.1 us
    pallas_call x1, Pallas kernels, body(): pl.pallas_call(encoder_grad_kernel, out_shape=(shaped((2, cols, packed),...  12.1 us
    pallas_call x1, Pallas kernels, body(): pl.pallas_call(encoder_kernel, out_shape=(shaped((rows, depth), F32), sha...  8.15 us
  transfers between devices with their start and end apart: 43, of which 22 were waited for; matrix products, arithmetic and copies ran while one was open for 17% of the time, Pallas kernels for 26%

profile of v3, /device:TPU:0, one launch (start us, length us, event | category | flops | bytes accessed | tf_op | source)
XLA Modules:
  0.0 247.4 jit_solution(11493293980001575607)
XLA Ops:
  1.5 1.9 pad_maximum_fusion.2.w0
  5.5 2.5 %collective-permute-start.4 = (bf16[1040,128]{1,0:T(8,128)(2,1)}, bf16[1040,128]{1,0:T(8,128)(2,1)}, u32[]{:S(2)}, u32[]{:S(2)}) collective-permute-start(bf16[1040,128]{1,0:T(8,128)(2,1)} %constant_dynamic-slice_fusion.1), channel_id=1, source_target_pairs={{0,2},{1,3},{2,0},{3,1},{4,6},{5,7},{6,4},{7,5},{8,10},{9,11},{10,... | collective-permute-start | bytes 798728 | tf_op jit(solution)/shard_map/ppermute | solution.py:45
  11.1 1.9 fusion.8.w0
  13.1 2.5 %collective-permute-done.4.w2a = bf16[1040,128]{1,0:T(8,128)(2,1)} collective-permute-done((bf16[1040,128]{1,0:T(8,128)(2,1)}, bf16[1040,128]{1,0:T(8,128)(2,1)}, u32[]{:S(2)}, u32[]{:S(2)}) %collective-permute-start.4) | collective-permute-done | bytes 266272 | tf_op jit(solution)/shard_map/ppermute | solution.py:45
  15.6 2.0 collective-permute-start.5
  21.4 5.4 %collective-permute-done.2.f3 = bf16[1056,128]{1,0:T(8,128)(2,1)} collective-permute-done((bf16[1056,128]{1,0:T(8,128)(2,1)}, bf16[1056,128]{1,0:T(8,128)(2,1)}, u32[]{:S(2)}, u32[]{:S(2)}) %collective-permute-start.2) | collective-permute-done | bytes 270368 | tf_op jit(solution)/shard_map/ppermute | solution.py:45
  31.0 8.1 %shard_map.204 = (f32[1056,512]{1,0:T(8,128)}, bf16[1056,512]{1,0:T(8,128)(2,1)}, bf16[1056,512]{1,0:T(8,128)(2,1)}) custom-call(s32[3]{0:T(128)} %pad_add_fusion.me_ref, bf16[1056,128]{1,0:T(8,128)(2,1)} %get-tuple-element.89.f0, bf16[1056,128]{1,0:T(8,128)(2,1)} %collective-permute-done.f1, bf16[1056,128]{1,0:T(8,128)(2,1)} %collective-permute-done.1.f2, ...), custom_call_target="tpu_custom_call" | custom-call | flops 2214592512 | bytes 12000000 | tf_op jit(solution)/shard_map/pallas_call | solution.py:417
  39.2 2.0 collective-permute-done.8.w2
  44.2 13.1 %shard_map.205 = (bf16[1056,512]{1,0:T(8,128)(2,1)}, f32[2,2,1,1024]{3,2,1,0:T(1,128)}, bf16[2,2,1056,1024]{3,2,1,0:T(8,128)(2,1)}, bf16[1,1056,512]{2,1,0:T(8,128)(2,1)}) custom-call(bf16[1056,512]{1,0:T(8,128)(2,1)} %get-tuple-element.46.latent_ref.first_ref, bf16[2,2,1024,256]{3,2,1,0:T(8,128)(2,1)} %books.5, f32[2,2,1,1024]{3,2,1,0:T(1,128)} %mul.143.norms), custom_call_target="tpu_custom_call" | custom-call | flops 4429185024 | bytes 30000000 | tf_op jit(solution)/shard_map/pallas_call | solution.py:442
  58.6 13.1 %shard_map.206 = (f32[1056,512]{1,0:T(8,128)}, bf16[2,128,2176]{2,1,0:T(8,128)(2,1)}, f32[2,128,2176]{2,1,0:T(8,128)}) custom-call(s32[3]{0:T(128)} %pad_add_fusion.me_ref, bf16[1056,512]{1,0:T(8,128)(2,1)} %get-tuple-element.47.quant, bf16[1056,128]{1,0:T(8,128)(2,1)} %get-tuple-element.85.c0, bf16[1056,128]{1,0:T(8,128)(2,1)} %copy-done.21, ...), custom_call_target="tpu_custom_call" | custom-call | flops 6643777536 | bytes 20000000 | tf_op jit(solution)/shard_map/pallas_call | solution.py:467
  71.8 16.3 %copy.57 = bf16[2,2,1024,256]{2,3,1,0:T(8,128)(2,1)} copy(bf16[2,2,1024,256]{3,2,1,0:T(8,128)(2,1)S(1)} %copy-done.2) | data formatting | bytes 4194304 | tf_op args[6]
  88.1 12.3 %shard_map.207 = (bf16[1056,256]{1,0:T(8,128)(2,1)}, bf16[2,272,1024]{2,1,0:T(8,128)(2,1)}) custom-call(s32[1]{0:T(128)} %bitcast.10.group_ref, f32[1056,512]{1,0:T(8,128)} %get-tuple-element.60.grad_ref, bf16[2,2,1056,1024]{3,2,1,0:T(8,128)(2,1)} %get-tuple-element.55.prob_ref, bf16[1056,512]{1,0:T(8,128)(2,1)} %get-tuple-element.46.latent_ref.first_ref, ...), custom_call_target="tpu_custom_call" | custom-call | flops 4429185024 | bytes 15000000 | tf_op jit(solution)/shard_map/pallas_call | solution.py:489
  104.8 12.1 %shard_map.208 = (bf16[1056,256]{1,0:T(8,128)(2,1)}, bf16[2,272,1024]{2,1,0:T(8,128)(2,1)}) custom-call(s32[1]{0:T(128)} %bitcast.3.group_ref, f32[1056,512]{1,0:T(8,128)} %get-tuple-element.60.grad_ref, bf16[2,2,1056,1024]{3,2,1,0:T(8,128)(2,1)} %get-tuple-element.55.prob_ref, bf16[1056,512]{1,0:T(8,128)(2,1)} %get-tuple-element.46.latent_ref.first_ref, ...), custom_call_target="tpu_custom_call" | custom-call | flops 4429185024 | bytes 15000000 | tf_op jit(solution)/shard_map/pallas_call | solution.py:489
  126.1 12.1 %shard_map.209 = (bf16[2,128,2176]{2,1,0:T(8,128)(2,1)}, f32[2,128,2176]{2,1,0:T(8,128)}, bf16[1024,128]{1,0:T(8,128)(2,1)}, bf16[1024,128]{1,0:T(8,128)(2,1)}, ...) custom-call(s32[3]{0:T(128)} %pad_add_fusion.me_ref, bf16[1056,256]{1,0:T(8,128)(2,1)} %get-tuple-element.67.grad_mine, ...), custom_call_target="tpu_custom_call" | custom-call | flops 4429185024 | bytes 20000000 | tf_op jit(solution)/shard_map/pallas_call | solution.py:539
  144.6 3.1 %collective-permute-done.18.refs_2_ = bf16[1024,128]{1,0:T(8,128)(2,1)} collective-permute-done((bf16[1024,128]{1,0:T(8,128)(2,1)}, bf16[1024,128]{1,0:T(8,128)(2,1)}, u32[]{:S(2)}, u32[]{:S(2)}) %collective-permute-start.18) | collective-permute-done | bytes 262176 | tf_op jit(solution)/shard_map/ppermute | solution.py:45
  147.7 4.7 %collective-permute-done.19.refs_3_ = bf16[1024,128]{1,0:T(8,128)(2,1)} collective-permute-done((bf16[1024,128]{1,0:T(8,128)(2,1)}, bf16[1024,128]{1,0:T(8,128)(2,1)}, u32[]{:S(2)}, u32[]{:S(2)}) %collective-permute-start.19) | collective-permute-done | bytes 262176 | tf_op jit(solution)/shard_map/ppermute | solution.py:45
  152.4 2.6 %shard_map.210 = f32[4096,128]{1,0:T(8,128)} custom-call(s32[1]{0:T(128)} %bitcast.mask_ref, bf16[1024,128]{1,0:T(8,128)(2,1)} %get-tuple-element.71.refs_0_, bf16[1024,128]{1,0:T(8,128)(2,1)} %collective-permute-done.17.refs_1_, bf16[1024,128]{1,0:T(8,128)(2,1)} %collective-permute-done.18.refs_2_, bf16[1024,128]{1,0:T(8,128)(2,1)} %collective-permute-done.19.refs_3_), custom_call_target="tpu_custom_call" | custom-call | bytes 4194304 | tf_op jit(solution)/shard_map/pallas_call | solution.py:596
  160.2 3.5 %collective-permute-done.30 = bf16[32,2176]{1,0:T(8,128)(2,1)S(1)} collective-permute-done((bf16[32,2176]{1,0:T(8,128)(2,1)S(1)}, bf16[32,2176]{1,0:T(8,128)(2,1)S(1)}, u32[]{:S(2)}, u32[]{:S(2)}) %collective-permute-start.30) | collective-permute-done | bytes 139296 | tf_op jit(solution)/shard_map/ppermute | solution.py:45
  163.7 7.0 %collective-permute-done.35 = bf16[272,512]{0,1:T(8,128)(2,1)S(1)} collective-permute-done((bf16[272,512]{0,1:T(8,128)(2,1)S(1)}, bf16[272,512]{0,1:T(8,128)(2,1)S(1)}, u32[]{:S(2)}, u32[]{:S(2)}) %collective-permute-start.35) | collective-permute-done | bytes 278560 | tf_op jit(solution)/shard_map/ppermute | solution.py:45
  171.3 2.7 %collective-permute-start.31 = (bf16[16,2176]{1,0:T(8,128)(2,1)S(1)}, bf16[16,2176]{1,0:T(8,128)(2,1)S(1)}, u32[]{:S(2)}, u32[]{:S(2)}) collective-permute-start(bf16[16,2176]{1,0:T(8,128)(2,1)S(1)} %dynamic-slice_convert_fusion.8), channel_id=1, source_target_pairs={{0,16},{4,20},{8,24},{12,28},{16,0},{20,4},{24,8},{28,12},{1,17},{... | collective-permute-start | bytes 208904 | tf_op jit(solution)/shard_map/ppermute | solution.py:45
  173.9 4.3 %collective-permute-done.36 = bf16[272,256]{0,1:T(8,128)(2,1)S(1)} collective-permute-done((bf16[272,256]{0,1:T(8,128)(2,1)S(1)}, bf16[272,256]{0,1:T(8,128)(2,1)S(1)}, u32[]{:S(2)}, u32[]{:S(2)}) %collective-permute-start.36) | collective-permute-done | bytes 139296 | tf_op jit(solution)/shard_map/ppermute | solution.py:45
  178.4 2.5 %collective-permute-start.37 = (bf16[272,128]{0,1:T(8,128)(2,1)S(1)}, bf16[272,128]{0,1:T(8,128)(2,1)S(1)}, u32[]{:S(2)}, u32[]{:S(2)}) collective-permute-start(bf16[272,128]{0,1:T(8,128)(2,1)S(1)} %dynamic-slice_convert_fusion.7), channel_id=1, source_target_pairs={{0,16},{4,20},{8,24},{12,28},{16,0},{20,4},{24,8},{28,12},{1,17},{... | collective-permute-start | bytes 208904 | tf_op jit(solution)/shard_map/ppermute | solution.py:45
  181.4 4.3 %collective-permute-done.37 = bf16[272,128]{0,1:T(8,128)(2,1)S(1)} collective-permute-done((bf16[272,128]{0,1:T(8,128)(2,1)S(1)}, bf16[272,128]{0,1:T(8,128)(2,1)S(1)}, u32[]{:S(2)}, u32[]{:S(2)}) %collective-permute-start.37) | collective-permute-done | bytes 69664 | tf_op jit(solution)/shard_map/ppermute | solution.py:45
  188.3 4.1 %collective-permute-done.38 = bf16[128,256]{1,0:T(8,128)(2,1)S(1)} collective-permute-done((bf16[128,256]{1,0:T(8,128)(2,1)S(1)}, bf16[128,256]{1,0:T(8,128)(2,1)S(1)}, u32[]{:S(2)}, u32[]{:S(2)}) %collective-permute-start.38) | collective-permute-done | bytes 65568 | tf_op jit(solution)/shard_map/ppermute | solution.py:45
  193.5 1.9 collective-permute-done.33
  198.1 7.6 %collective-permute-done.23 = bf16[128,2176]{1,0:T(8,128)(2,1)S(1)} collective-permute-done((bf16[128,2176]{1,0:T(8,128)(2,1)S(1)}, bf16[128,2176]{1,0:T(8,128)(2,1)S(1)}, u32[]{:S(2)}, u32[]{:S(2)}) %collective-permute-start.23) | collective-permute-done | bytes 557088 | tf_op jit(solution)/shard_map/ppermute | solution.py:45
  206.5 7.4 %collective-permute-done.24 = bf16[64,2176]{1,0:T(8,128)(2,1)S(1)} collective-permute-done((bf16[64,2176]{1,0:T(8,128)(2,1)S(1)}, bf16[64,2176]{1,0:T(8,128)(2,1)S(1)}, u32[]{:S(2)}, u32[]{:S(2)}) %collective-permute-start.24) | collective-permute-done | bytes 278560 | tf_op jit(solution)/shard_map/ppermute | solution.py:45
  216.1 3.1 %collective-permute-done.25 = bf16[32,2176]{1,0:T(8,128)(2,1)S(1)} collective-permute-done((bf16[32,2176]{1,0:T(8,128)(2,1)S(1)}, bf16[32,2176]{1,0:T(8,128)(2,1)S(1)}, u32[]{:S(2)}, u32[]{:S(2)}) %collective-permute-start.25) | collective-permute-done | bytes 139296 | tf_op jit(solution)/shard_map/ppermute | solution.py:45
  219.3 7.2 %collective-permute-done.26 = bf16[16,2176]{1,0:T(8,128)(2,1)S(1)} collective-permute-done((bf16[16,2176]{1,0:T(8,128)(2,1)S(1)}, bf16[16,2176]{1,0:T(8,128)(2,1)S(1)}, u32[]{:S(2)}, u32[]{:S(2)}) %collective-permute-start.26) | collective-permute-done | bytes 69664 | tf_op jit(solution)/shard_map/ppermute | solution.py:45
  227.2 4.7 %collective-permute-done.27 = bf16[16,2176]{1,0:T(8,128)(2,1)S(1)} collective-permute-done((bf16[16,2176]{1,0:T(8,128)(2,1)S(1)}, bf16[16,2176]{1,0:T(8,128)(2,1)S(1)}, u32[]{:S(2)}, u32[]{:S(2)}) %collective-permute-start.27) | collective-permute-done | bytes 69664 | tf_op jit(solution)/shard_map/ppermute | solution.py:45
  232.3 4.8 %collective-permute-done.28 = bf16[32,2176]{1,0:T(8,128)(2,1)S(1)} collective-permute-done((bf16[32,2176]{1,0:T(8,128)(2,1)S(1)}, bf16[32,2176]{1,0:T(8,128)(2,1)S(1)}, u32[]{:S(2)}, u32[]{:S(2)}) %collective-permute-start.28) | collective-permute-done | bytes 139296 | tf_op jit(solution)/shard_map/ppermute | solution.py:45
  240.5 3.8 %shard_map.211 = f32[4096,256]{1,0:T(8,128)} custom-call(s32[1]{0:T(128)} %bitcast.23.mask_ref, bf16[2048,256]{1,0:T(8,128)(2,1)} %copy-done.7, bf16[2048,256]{1,0:T(8,128)(2,1)} %copy-done.8), custom_call_target="tpu_custom_call" | custom-call | bytes 8388608 | tf_op jit(solution)/shard_map/pallas_call | solution.py:596
  (188 shorter events, 61.3 us)
Async XLA Ops:
  3.4 26.7 %collective-permute-start.3 = (bf16[2080,128]{1,0:T(8,128)(2,1)}, bf16[2080,128]{1,0:T(8,128)(2,1)}, u32[]{:S(2)}, u32[]{:S(2)}) collective-permute-start(bf16[2080,128]{1,0:T(8,128)(2,1)} %pad_maximum_fusion.2.w0), channel_id=1, source_target_pairs={{0,1},{1,0},{2,3},{3,2},{4,5},{5,4},{6,7},{7,6},{8,9},{9,8},{10,11... | collective-permute-start | bytes 1597448 | tf_op jit(solution)/shard_map/ppermute | solution.py:45
  5.5 10.0 %collective-permute-start.4 = (bf16[1040,128]{1,0:T(8,128)(2,1)}, bf16[1040,128]{1,0:T(8,128)(2,1)}, u32[]{:S(2)}, u32[]{:S(2)}) collective-permute-start(bf16[1040,128]{1,0:T(8,128)(2,1)} %constant_dynamic-slice_fusion.1), channel_id=1, source_target_pairs={{0,2},{1,3},{2,0},{3,1},{4,6},{5,7},{6,4},{7,5},{8,10},{9,11},{10,... | collective-permute-start | bytes 798728 | tf_op jit(solution)/shard_map/ppermute | solution.py:45
  9.0 20.7 %collective-permute-start = (bf16[1056,128]{1,0:T(8,128)(2,1)}, bf16[1056,128]{1,0:T(8,128)(2,1)}, u32[]{:S(2)}, u32[]{:S(2)}) collective-permute-start(bf16[1056,128]{1,0:T(8,128)(2,1)} %get-tuple-element.87), channel_id=1, source_target_pairs={{0,1},{1,0},{2,3},{3,2},{4,5},{5,4},{6,7},{7,6},{8,9},{9,8},{10,11... | collective-permute-start | bytes 811016 | tf_op jit(solution)/shard_map/ppermute | solution.py:45
  9.3 12.1 %collective-permute-start.1 = (bf16[1056,128]{1,0:T(8,128)(2,1)}, bf16[1056,128]{1,0:T(8,128)(2,1)}, u32[]{:S(2)}, u32[]{:S(2)}) collective-permute-start(bf16[1056,128]{1,0:T(8,128)(2,1)} %get-tuple-element.88), channel_id=1, source_target_pairs={{0,2},{1,3},{2,0},{3,1},{4,6},{5,7},{6,4},{7,5},{8,10},{9,11},{10,... | collective-permute-start | bytes 811016 | tf_op jit(solution)/shard_map/ppermute | solution.py:45
  9.6 17.2 %collective-permute-start.2 = (bf16[1056,128]{1,0:T(8,128)(2,1)}, bf16[1056,128]{1,0:T(8,128)(2,1)}, u32[]{:S(2)}, u32[]{:S(2)}) collective-permute-start(bf16[1056,128]{1,0:T(8,128)(2,1)} %get-tuple-element.86), channel_id=1, source_target_pairs={{0,3},{1,2},{2,1},{3,0},{4,7},{5,6},{6,5},{7,4},{8,11},{9,10},{10,... | collective-permute-start | bytes 811016 | tf_op jit(solution)/shard_map/ppermute | solution.py:45
  15.6 12.8 %collective-permute-start.5 = (bf16[1040,128]{1,0:T(8,128)(2,1)}, bf16[1040,128]{1,0:T(8,128)(2,1)S(1)}, u32[]{:S(2)}, u32[]{:S(2)}) collective-permute-start(bf16[1040,128]{1,0:T(8,128)(2,1)} %collective-permute-done.4.w2a), channel_id=1, source_target_pairs={{0,4},{4,0},{8,12},{12,8},{16,20},{20,16},{24,28},{28,24},{1,5},{5... | collective-permute-start | bytes 798728 | tf_op jit(solution)/shard_map/ppermute | solution.py:45
  21.4 8.8 %collective-permute-start.6 = (bf16[1040,128]{1,0:T(8,128)(2,1)}, bf16[1040,128]{1,0:T(8,128)(2,1)S(1)}, u32[]{:S(2)}, u32[]{:S(2)}) collective-permute-start(bf16[1040,128]{1,0:T(8,128)(2,1)} %collective-permute-done.4.w2a), channel_id=1, source_target_pairs={{0,1},{1,0},{2,3},{3,2},{4,5},{5,4},{6,7},{7,6},{8,9},{9,8},{10,11... | collective-permute-start | bytes 798728 | tf_op jit(solution)/shard_map/ppermute | solution.py:45
  26.8 14.3 %collective-permute-start.8 = (bf16[2080,128]{1,0:T(8,128)(2,1)}, bf16[2080,128]{1,0:T(8,128)(2,1)S(1)}, u32[]{:S(2)}, u32[]{:S(2)}) collective-permute-start(bf16[2080,128]{1,0:T(8,128)(2,1)} %fusion.8.w0), channel_id=1, source_target_pairs={{0,2},{1,3},{2,0},{3,1},{4,6},{5,7},{6,4},{7,5},{8,10},{9,11},{10,... | collective-permute-start | bytes 1597448 | tf_op jit(solution)/shard_map/ppermute | solution.py:45
  29.7 27.7 %collective-permute-start.12 = (bf16[2080,128]{1,0:T(8,128)(2,1)}, bf16[2080,128]{1,0:T(8,128)(2,1)S(1)}, u32[]{:S(2)}, u32[]{:S(2)}) collective-permute-start(bf16[2080,128]{1,0:T(8,128)(2,1)} %fusion.8.w0), channel_id=1, source_target_pairs={{0,1},{1,0},{2,3},{3,2},{4,5},{5,4},{6,7},{7,6},{8,9},{9,8},{10,11... | collective-permute-start | bytes 1597448 | tf_op jit(solution)/shard_map/ppermute | solution.py:45
  41.1 16.3 %collective-permute-start.13 = (bf16[2080,128]{1,0:T(8,128)(2,1)S(1)}, bf16[2080,128]{1,0:T(8,128)(2,1)S(1)}, u32[]{:S(2)}, u32[]{:S(2)}) collective-permute-start(bf16[2080,128]{1,0:T(8,128)(2,1)S(1)} %collective-permute-done.8.w2), channel_id=1, source_target_pairs={{0,1},{1,0},{2,3},{3,2},{4,5},{5,4},{6,7},{7,6},{8,9},{9,8},{10,11... | collective-permute-start | bytes 1597448 | tf_op jit(solution)/shard_map/ppermute | solution.py:45
  42.1 15.3 %collective-permute-start.10 = (bf16[1056,128]{1,0:T(8,128)(2,1)S(1)}, bf16[1056,128]{1,0:T(8,128)(2,1)S(1)}, u32[]{:S(2)}, u32[]{:S(2)}) collective-permute-start(bf16[1056,128]{1,0:T(8,128)(2,1)S(1)} %get-tuple-element.84), channel_id=1, source_target_pairs={{0,2},{1,3},{2,0},{3,1},{4,6},{5,7},{6,4},{7,5},{8,10},{9,11},{10,... | collective-permute-start | bytes 811016 | tf_op jit(solution)/shard_map/ppermute | solution.py:45
  43.7 13.7 %collective-permute-start.11 = (bf16[1056,128]{1,0:T(8,128)(2,1)S(1)}, bf16[1056,128]{1,0:T(8,128)(2,1)S(1)}, u32[]{:S(2)}, u32[]{:S(2)}) collective-permute-start(bf16[1056,128]{1,0:T(8,128)(2,1)S(1)} %get-tuple-element.82), channel_id=1, source_target_pairs={{0,3},{1,2},{2,1},{3,0},{4,7},{5,6},{6,5},{7,4},{8,11},{9,10},{10,... | collective-permute-start | bytes 811016 | tf_op jit(solution)/shard_map/ppermute | solution.py:45
  43.8 13.6 %collective-permute-start.9 = (bf16[1056,128]{1,0:T(8,128)(2,1)S(1)}, bf16[1056,128]{1,0:T(8,128)(2,1)S(1)}, u32[]{:S(2)}, u32[]{:S(2)}) collective-permute-start(bf16[1056,128]{1,0:T(8,128)(2,1)S(1)} %get-tuple-element.83), channel_id=1, source_target_pairs={{0,1},{1,0},{2,3},{3,2},{4,5},{5,4},{6,7},{7,6},{8,9},{9,8},{10,11... | collective-permute-start | bytes 811016 | tf_op jit(solution)/shard_map/ppermute | solution.py:45
  71.7 29.1 %collective-permute-start.14 = (bf16[2,128,2176]{2,1,0:T(8,128)(2,1)}, bf16[2,128,2176]{2,1,0:T(8,128)(2,1)}, u32[]{:S(2)}, u32[]{:S(2)}) collective-permute-start(bf16[2,128,2176]{2,1,0:T(8,128)(2,1)} %get-tuple-element.53), channel_id=1, source_target_pairs={{0,1},{1,0},{2,3},{3,2},{4,5},{5,4},{6,7},{7,6},{8,9},{9,8},{10,11... | collective-permute-start | bytes 3342344 | tf_op jit(solution)/shard_map/ppermute | solution.py:45
  100.4 16.5 %collective-permute-start.16 = (bf16[2,272,1024]{2,1,0:T(8,128)(2,1)}, bf16[2,272,1024]{2,1,0:T(8,128)(2,1)}, u32[]{:S(2)}, u32[]{:S(2)}) collective-permute-start(bf16[2,272,1024]{2,1,0:T(8,128)(2,1)} %get-tuple-element.58), channel_id=1, source_target_pairs={{0,1},{1,0},{2,3},{3,2},{4,5},{5,4},{6,7},{7,6},{8,9},{9,8},{10,11... | collective-permute-start | bytes 3342344 | tf_op jit(solution)/shard_map/ppermute | solution.py:45
  103.1 14.9 %collective-permute-start.15 = (bf16[128,2176]{1,0:T(8,128)(2,1)}, bf16[128,2176]{1,0:T(8,128)(2,1)}, u32[]{:S(2)}, u32[]{:S(2)}) collective-permute-start(bf16[128,2176]{1,0:T(8,128)(2,1)} %fusion.6), channel_id=1, source_target_pairs={{0,2},{1,3},{2,0},{3,1},{4,6},{5,7},{6,4},{7,5},{8,10},{9,11},{10,... | collective-permute-start | bytes 1671176 | tf_op jit(solution)/shard_map/ppermute | solution.py:45
  120.4 34.7 %collective-permute-start.21 = (bf16[64,2176]{1,0:T(8,128)(2,1)S(1)}, bf16[64,2176]{1,0:T(8,128)(2,1)}, u32[]{:S(2)}, u32[]{:S(2)}) collective-permute-start(bf16[64,2176]{1,0:T(8,128)(2,1)S(1)} %dynamic-slice_convert_fusion.3), channel_id=1, source_target_pairs={{0,4},{4,0},{8,12},{12,8},{16,20},{20,16},{24,28},{28,24},{1,5},{5... | collective-permute-start | bytes 835592 | tf_op jit(solution)/shard_map/ppermute | solution.py:45
  124.6 30.4 %collective-permute-start.20 = (bf16[272,1024]{1,0:T(8,128)(2,1)}, bf16[272,1024]{1,0:T(8,128)(2,1)}, u32[]{:S(2)}, u32[]{:S(2)}) collective-permute-start(bf16[272,1024]{1,0:T(8,128)(2,1)} %fusion.5), channel_id=1, source_target_pairs={{0,2},{1,3},{2,0},{3,1},{4,6},{5,7},{6,4},{7,5},{8,10},{9,11},{10,... | collective-permute-start | bytes 1671176 | tf_op jit(solution)/shard_map/ppermute | solution.py:45
  138.2 9.5 %collective-permute-start.18 = (bf16[1024,128]{1,0:T(8,128)(2,1)}, bf16[1024,128]{1,0:T(8,128)(2,1)}, u32[]{:S(2)}, u32[]{:S(2)}) collective-permute-start(bf16[1024,128]{1,0:T(8,128)(2,1)} %get-tuple-element.73), channel_id=1, source_target_pairs={{0,2},{1,3},{2,0},{3,1},{4,6},{5,7},{6,4},{7,5},{8,10},{9,11},{10,... | collective-permute-start | bytes 786440 | tf_op jit(solution)/shard_map/ppermute | solution.py:45
  138.8 13.6 %collective-permute-start.19 = (bf16[1024,128]{1,0:T(8,128)(2,1)}, bf16[1024,128]{1,0:T(8,128)(2,1)}, u32[]{:S(2)}, u32[]{:S(2)}) collective-permute-start(bf16[1024,128]{1,0:T(8,128)(2,1)} %get-tuple-element.74), channel_id=1, source_target_pairs={{0,3},{1,2},{2,1},{3,0},{4,7},{5,6},{6,5},{7,4},{8,11},{9,10},{10,... | collective-permute-start | bytes 786440 | tf_op jit(solution)/shard_map/ppermute | solution.py:45
  159.5 11.1 %collective-permute-start.35 = (bf16[272,512]{0,1:T(8,128)(2,1)S(1)}, bf16[272,512]{0,1:T(8,128)(2,1)S(1)}, u32[]{:S(2)}, u32[]{:S(2)}) collective-permute-start(bf16[272,512]{0,1:T(8,128)(2,1)S(1)} %dynamic-slice_convert_fusion.1), channel_id=1, source_target_pairs={{0,4},{4,0},{8,12},{12,8},{16,20},{20,16},{24,28},{28,24},{1,5},{5... | collective-permute-start | bytes 835592 | tf_op jit(solution)/shard_map/ppermute | solution.py:45
  160.1 32.4 %collective-permute-start.22 = (bf16[2,128,2176]{2,1,0:T(8,128)(2,1)S(1)}, bf16[2,128,2176]{2,1,0:T(8,128)(2,1)S(1)}, u32[]{:S(2)}, u32[]{:S(2)}) collective-permute-start(bf16[2,128,2176]{2,1,0:T(8,128)(2,1)S(1)} %copy-done.15), channel_id=1, source_target_pairs={{0,1},{1,0},{2,3},{3,2},{4,5},{5,4},{6,7},{7,6},{8,9},{9,8},{10,11... | collective-permute-start | bytes 3342344 | tf_op jit(solution)/shard_map/ppermute | solution.py:45
  170.8 7.5 %collective-permute-start.36 = (bf16[272,256]{0,1:T(8,128)(2,1)S(1)}, bf16[272,256]{0,1:T(8,128)(2,1)S(1)}, u32[]{:S(2)}, u32[]{:S(2)}) collective-permute-start(bf16[272,256]{0,1:T(8,128)(2,1)S(1)} %dynamic-slice_convert_fusion.4), channel_id=1, source_target_pairs={{0,8},{4,12},{8,0},{12,4},{16,24},{20,28},{24,16},{28,20},{1,9},{5... | collective-permute-start | bytes 417800 | tf_op jit(solution)/shard_map/ppermute | solution.py:45
  171.3 9.6 %collective-permute-start.31 = (bf16[16,2176]{1,0:T(8,128)(2,1)S(1)}, bf16[16,2176]{1,0:T(8,128)(2,1)S(1)}, u32[]{:S(2)}, u32[]{:S(2)}) collective-permute-start(bf16[16,2176]{1,0:T(8,128)(2,1)S(1)} %dynamic-slice_convert_fusion.8), channel_id=1, source_target_pairs={{0,16},{4,20},{8,24},{12,28},{16,0},{20,4},{24,8},{28,12},{1,17},{... | collective-permute-start | bytes 208904 | tf_op jit(solution)/shard_map/ppermute | solution.py:45
  178.4 7.4 %collective-permute-start.37 = (bf16[272,128]{0,1:T(8,128)(2,1)S(1)}, bf16[272,128]{0,1:T(8,128)(2,1)S(1)}, u32[]{:S(2)}, u32[]{:S(2)}) collective-permute-start(bf16[272,128]{0,1:T(8,128)(2,1)S(1)} %dynamic-slice_convert_fusion.7), channel_id=1, source_target_pairs={{0,16},{4,20},{8,24},{12,28},{16,0},{20,4},{24,8},{28,12},{1,17},{... | collective-permute-start | bytes 208904 | tf_op jit(solution)/shard_map/ppermute | solution.py:45
  192.8 12.9 %collective-permute-start.23 = (bf16[128,2176]{1,0:T(8,128)(2,1)S(1)}, bf16[128,2176]{1,0:T(8,128)(2,1)S(1)}, u32[]{:S(2)}, u32[]{:S(2)}) collective-permute-start(bf16[128,2176]{1,0:T(8,128)(2,1)S(1)} %fusion.7), channel_id=1, source_target_pairs={{0,2},{1,3},{2,0},{3,1},{4,6},{5,7},{6,4},{7,5},{8,10},{9,11},{10,... | collective-permute-start | bytes 1671176 | tf_op jit(solution)/shard_map/ppermute | solution.py:45
  195.5 11.0 %collective-permute-start.34 = (bf16[64,2176]{1,0:T(8,128)(2,1)S(1)}, bf16[64,2176]{1,0:T(8,128)(2,1)S(1)}, u32[]{:S(2)}, u32[]{:S(2)}) collective-permute-start(bf16[64,2176]{1,0:T(8,128)(2,1)S(1)} %pad_maximum_fusion.5), channel_id=1, source_target_pairs={{0,4},{4,0},{8,12},{12,8},{16,20},{20,16},{24,28},{28,24},{1,5},{5... | collective-permute-start | bytes 835592 | tf_op jit(solution)/shard_map/ppermute | solution.py:45
  197.5 17.8 %collective-permute-start.40 = (bf16[512,256]{1,0:T(8,128)(2,1)S(1)}, bf16[512,256]{1,0:T(8,128)(2,1)S(1)}, u32[]{:S(2)}, u32[]{:S(2)}) collective-permute-start(bf16[512,256]{1,0:T(8,128)(2,1)S(1)} %pad_maximum_fusion.6), channel_id=1, source_target_pairs={{0,4},{4,0},{8,12},{12,8},{16,20},{20,16},{24,28},{28,24},{1,5},{5... | collective-permute-start | bytes 786440 | tf_op jit(solution)/shard_map/ppermute | solution.py:45
  205.9 8.1 %collective-permute-start.24 = (bf16[64,2176]{1,0:T(8,128)(2,1)S(1)}, bf16[64,2176]{1,0:T(8,128)(2,1)S(1)}, u32[]{:S(2)}, u32[]{:S(2)}) collective-permute-start(bf16[64,2176]{1,0:T(8,128)(2,1)S(1)} %dynamic-slice_convert_fusion.2), channel_id=1, source_target_pairs={{0,4},{4,0},{8,12},{12,8},{16,20},{20,16},{24,28},{28,24},{1,5},{5... | collective-permute-start | bytes 835592 | tf_op jit(solution)/shard_map/ppermute | solution.py:45
  215.3 11.8 %collective-permute-start.41 = (bf16[1024,256]{1,0:T(8,128)(2,1)S(1)}, bf16[1024,256]{1,0:T(8,128)(2,1)S(1)}, u32[]{:S(2)}, u32[]{:S(2)}) collective-permute-start(bf16[1024,256]{1,0:T(8,128)(2,1)S(1)} %pad_maximum_fusion.3), channel_id=1, source_target_pairs={{0,2},{1,3},{2,0},{3,1},{4,6},{5,7},{6,4},{7,5},{8,10},{9,11},{10,... | collective-permute-start | bytes 1572872 | tf_op jit(solution)/shard_map/ppermute | solution.py:45
  219.2 7.3 %collective-permute-start.26 = (bf16[16,2176]{1,0:T(8,128)(2,1)S(1)}, bf16[16,2176]{1,0:T(8,128)(2,1)S(1)}, u32[]{:S(2)}, u32[]{:S(2)}) collective-permute-start(bf16[16,2176]{1,0:T(8,128)(2,1)S(1)} %dynamic-slice_convert_fusion.9), channel_id=1, source_target_pairs={{0,16},{4,20},{8,24},{12,28},{16,0},{20,4},{24,8},{28,12},{1,17},{... | collective-permute-start | bytes 208904 | tf_op jit(solution)/shard_map/ppermute | solution.py:45
  227.1 12.3 %collective-permute-start.42 = (bf16[2048,256]{1,0:T(8,128)(2,1)S(1)}, bf16[2048,256]{1,0:T(8,128)(2,1)S(1)}, u32[]{:S(2)}, u32[]{:S(2)}) collective-permute-start(bf16[2048,256]{1,0:T(8,128)(2,1)S(1)} %constant_dynamic-update-slice_fusion.refs_0_), channel_id=1, source_target_pairs={{0,1},{1,0},{2,3},{3,2},{4,5},{5,4},{6,7},{7,6},{8,9},{9,8},{10,11... | collective-permute-start | bytes 3145736 | tf_op jit(solution)/shard_map/ppermute | solution.py:45
  (37 other events, 398.0 us)

commit v4 on v3

--- a/solution.py
+++ b/solution.py
@@ -49,40 +49,20 @@
     return lax.optimization_barrier((values,) + others)[0]
 
 
-def frames_out(values, me, own):
-    padded = jnp.pad(values, ((HALO, HALO), (0, 0)))
-    return [
-        lax.dynamic_slice_in_dim(padded, (me ^ k) * own, own + 2 * HALO, 0) for k in range(4)
-    ]
-
-
-def bits_of(count):
-    return [1 << i for i in range(count.bit_length() - 1)]
-
-
-def halves(total, place, bit, dim):
-    size = total.shape[dim] // 2
-    side = (place // bit) % 2
-    mine = lax.dynamic_slice_in_dim(total, side * size, size, dim)
-    other = lax.dynamic_slice_in_dim(total, (1 - side) * size, size, dim)
-    return mine, other.astype(BF16)
-
-
-def scatter_step(total, place, bit, dim):
-    mine, other = halves(total, place, bit, dim)
-    return mine + swap(other, "dp", bit).astype(F32)
-
-
-def gather_step(block, axis, bit):
-    return jnp.concatenate([block, swap(block, axis, bit)], 0)
-
-
-def first_of(place, size, bits):
-    first = jnp.int32(0)
-    for bit in bits:
-        size = size // 2
-        first = first + ((place // bit) % 2) * size
-    return first
+def parts_of(total, count):
+    size = total.shape[0] // count
+    return [total[k * size : k * size + size] for k in range(count)]
+
+
+def swap_both(values, dp_bits, mp_bits):
+    mp = lax.axis_size("mp")
+    count = lax.axis_size("dp") * mp
+    pairs = [(i, i ^ (dp_bits * mp + mp_bits)) for i in range(count)]
+    return lax.ppermute(values, ("dp", "mp"), pairs)
+
+
+def low_sum(*terms):
+    return functools.reduce(lambda x, y: x + y, [t.astype(F32) for t in terms])
 
 
 def columns_of(me, k):
@@ -103,6 +83,32 @@
             rows = piece.shape[0]
             start = pl.multiple_of((side ^ j) * rows, 16)
             target[pl.ds(start, rows), columns_of(me, k)] = piece[...]
+
+
+def frames_kernel(where_ref, values, *outs):
+    own = outs[0].shape[0] - 2 * HALO
+    for k, out in enumerate(outs):
+        start = pl.multiple_of((where_ref[0] ^ k) * own, own)
+        above = pl.multiple_of(jnp.maximum(start - HALO, 0), HALO)
+        below = pl.multiple_of(jnp.minimum(start + own, values.shape[0] - HALO), HALO)
+        out[0:HALO, :] = values[pl.ds(above, HALO), :]
+        out[HALO : HALO + own, :] = values[pl.ds(start, own), :]
+        out[HALO + own : 2 * HALO + own, :] = values[pl.ds(below, HALO), :]
+
+
+def pack_kernel(where_ref, conv3, conv1, *refs, count):
+    biases, weight = refs[:count], refs[count]
+    first, second = conv3.shape[0], conv3.shape[0] + conv1.shape[0]
+    weight[0:first, :] = conv3[...]
+    weight[first:second, :] = conv1[...]
+    row = lax.broadcasted_iota(jnp.int32, (32, LANES), 0)
+    rows = jnp.zeros((32, LANES), F32)
+    for i, bias in enumerate(biases):
+        rows = jnp.where(row == i, bias[...].astype(F32), rows)
+    weight[second : second + 32, :] = rows.astype(BF16)
+    for half in refs[count + 1 :]:
+        size = half.shape[0]
+        half[...] = weight[pl.ds(pl.multiple_of(where_ref[1] * size, 16), size), :]
 
 
 def taps_into(source, target, first_ok, last_ok, rows, depth):
@@ -179,21 +185,26 @@
         quant_ref[:, g * depth : (g + 1) * depth] = summed[g].astype(BF16)
 
 
-def weight_grads(me, sent, kept, grad, deep, grad1, deep1, own, depth):
+def weight_grads(where_ref, near, targets, grad, deep, grad1, deep1, own, depth):
     here = slice(HALO, HALO + own)
     lane = lax.broadcasted_iota(jnp.int32, (own, LANES), 1)
     ones3 = jnp.where(lane == 0, 1.0, 0.0).astype(BF16)
     ones1 = jnp.where(lane == 1, 1.0, 0.0).astype(BF16)
-    for k in range(4):
-        columns = columns_of(me, k)
-        left = grad[here, columns]
-        left1 = grad1[here, columns]
-        target = (kept, sent)[k % 2].at[k // 2]
-        target[:, 0 : 3 * depth] = dot_tn(left, deep[here, :]).astype(target.dtype)
-        target[:, 3 * depth : 4 * depth] = dot_tn(left1, deep1[here, :]).astype(target.dtype)
-        target[:, 4 * depth : 4 * depth + LANES] = (
-            dot_tn(left, ones3) + dot_tn(left1, ones1)
-        ).astype(target.dtype)
+    size = LANES // near
+    for k, target in enumerate(targets):
+        left = grad[here, columns_of(where_ref[0], k)]
+        left1 = grad1[here, columns_of(where_ref[0], k)]
+
+        def put(first, count, values, target=target):
+            for j in range(near):
+                start = pl.multiple_of((where_ref[1] ^ j) * size, size)
+                target[pl.ds(start, size), first : first + count] = values[
+                    j * size : j * size + size, :
+                ].astype(target.dtype)
+
+        put(0, 3 * depth, dot_tn(left, deep[here, :]))
+        put(3 * depth, depth, dot_tn(left1, deep1[here, :]))
+        put(4 * depth, LANES, dot_tn(left, ones3) + dot_tn(left1, ones1))
 
 
 def input_grad(taps, weight, here, depth):
@@ -206,7 +217,7 @@
 
 def decoder_kernel(
     me_ref, quant, c0, c1, c2, c3, w0, w1, w2, w3, prev_ok, next_ok,
-    grad_ref, sent, kept, cot, weight, act, act3, low, mid,
+    grad_ref, g0, g1, g2, g3, cot, weight, act, act3, low, mid, *, near,
 ):
     me = me_ref[0]
     rows, depth = quant.shape
@@ -230,7 +241,7 @@
         grad = grad.astype(BF16)
         low[here, :] = grad
         act[8 + r : 8 + r + step, :] = grad.astype(F32)
-    weight_grads(me, sent, kept, low, act3, cot, mid, own, depth)
+    weight_grads(me_ref, near, (g0, g1, g2, g3), low, act3, cot, mid, own, depth)
     taps_into(act, act3, prev_ok, next_ok, rows, depth)
     for r in range(0, rows, step):
         here = slice(r, r + step)
@@ -240,8 +251,8 @@
 
 
 def quantize_back_kernel(
-    group_ref, grad_ref, prob_ref, first_ref, second_ref, books, turned, usage,
-    out_ref, table_ref, total, columns, *, own, levels,
+    group_ref, grad_ref, prob_ref, first_ref, second_ref, books, usage,
+    out_ref, kept_ref, sent_ref, mark_ref, total, columns, *, own, levels,
 ):
     step = pl.program_id(0)
     rows = grad_ref.shape[0]
@@ -276,22 +287,30 @@
 
     @pl.when(step == pl.num_programs(0) - 1)
     def _():
-        depth = turned.shape[2]
-        for level in range(levels):
-            table_ref[level, 0:depth, :] = (
-                total[level] - scale * columns[level] * turned[0, level].astype(F32)
-            ).astype(BF16)
-            row = lax.broadcasted_iota(jnp.int32, (16, total.shape[2]), 0)
-            table_ref[level, depth : depth + 16, :] = jnp.where(
-                row == 0, usage[0, level], 0.0
-            ).astype(BF16)
-
-
-def encoder_grad_kernel(
+        depth = books.shape[3]
+        row = lax.broadcasted_iota(jnp.int32, (16, kept_ref.shape[2]), 0)
+        for j, table in enumerate((kept_ref, sent_ref)):
+            level = group_ref[1] ^ j
+            codes = table.shape[2]
+            turned = books[0, level].astype(F32).T
+            for k in range(table.shape[0]):
+                here = slice(k * codes, k * codes + codes)
+                part = group_ref[2] ^ k
+                table[part, 0:depth, :] = (
+                    total[level, :, here] - scale * columns[level, :, here] * turned[:, here]
+                ).astype(BF16)
+                table[part, depth : depth + 16, :] = jnp.where(
+                    row == 0, usage[0, level, :, here], 0.0
+                ).astype(BF16)
+        mark_ref[...] = jnp.zeros_like(mark_ref)
+
+
+def encoder_weight_grad_kernel(
     me_ref, grad_mine, grad_other, hidden, mid, f0, f1, f2, f3,
     w0, w1, w2a, w2b, w3a, w3b, prev_ok, next_ok,
-    sent, kept, o0, o1, o2, o3, feat, weight, act, act3, low, grad_latent,
+    g0, g1, g2, g3, low, grad_latent, mark, feat, weight, act, act3, *, near,
 ):
+    mark[...] = jnp.zeros_like(mark)
     me = me_ref[0]
     rows, depth = hidden.shape
     own = rows - 2 * HALO
@@ -312,10 +331,22 @@
     for r in range(0, rows, step):
         here = slice(r, r + step)
         grad = dot_nt(grad_latent[here, :], weight[3 * depth : 4 * depth, :])
-        grad = (grad * elu_slope(hidden[here, :])).astype(BF16)
-        low[here, :] = grad
-        act[8 + r : 8 + r + step, :] = grad.astype(F32)
-    weight_grads(me, sent, kept, low, act3, grad_latent, mid, own, depth)
+        low[here, :] = (grad * elu_slope(hidden[here, :])).astype(BF16)
+    weight_grads(me_ref, near, (g0, g1, g2, g3), low, act3, grad_latent, mid, own, depth)
+
+
+def encoder_input_grad_kernel(
+    me_ref, low, grad_latent, f0, f1, f2, f3, w0, w1, w2a, w2b, w3a, w3b, prev_ok, next_ok,
+    o0, o1, o2, o3, feat, weight, act, act3,
+):
+    me = me_ref[0]
+    rows, depth = low.shape
+    own = rows - 2 * HALO
+    assemble(me, feat, (f0, f1, f2, f3))
+    assemble_halves(me, me_ref[1], weight, w0, w1, (w2a, w2b, w3a, w3b))
+    act[8 : 8 + rows, :] = low[...].astype(F32)
+    act[0:8, :] = jnp.zeros((8, depth), F32)
+    act[8 + rows : 16 + rows, :] = jnp.zeros((8, depth), F32)
     taps_into(act, act3, prev_ok, next_ok, rows, depth)
     for r in range(HALO, HALO + own, own // 4):
         here = slice(r, r + own // 4)
@@ -379,40 +410,83 @@
     rows = own + 2 * HALO
     depth = cols * width
     side, level_side = me % 2, me // 2
-    dp_bits = bits_of(n_dp)
-    where_row = jnp.stack([me, place % 2, side])
-
-    def pack(conv3, conv1, biases):
-        rows32 = jnp.pad(jnp.stack(biases), ((0, 32 - len(biases)), (0, 0)))
-        return jnp.concatenate([conv3.reshape(3 * depth, cols), conv1, rows32], 0)
-
-    enc_own = pack(enc_conv3, enc_conv1, [enc_bias3, enc_bias1])
-    half_rows = enc_own.shape[0] // 2
-    enc_half = lax.dynamic_slice_in_dim(enc_own, (place % 2) * half_rows, half_rows, 0)
+    near = 2 if n_dp % 2 == 0 else n_dp
+    near_at = place % near
+    far_bits = [near << i for i in range((n_dp // near).bit_length() - 1)]
+    where_row = jnp.stack([me, place % near, side])
+
+    def pack(row, conv3, conv1, biases, half):
+        total = conv3.shape[0] * conv3.shape[1] + conv1.shape[0] + 32
+        shapes = [shaped((total, cols), BF16)] + [shaped((total // 2, cols), BF16)] * half
+        return pl.pallas_call(
+            functools.partial(pack_kernel, count=len(biases)),
+            out_shape=shapes,
+            in_specs=whole(3 + len(biases), True),
+            out_specs=whole(len(shapes)),
+            compiler_params=PARAMS,
+            cost_estimate=cost(0, 1e6),
+        )(
+            row,
+            conv3.reshape(3 * depth, cols),
+            conv1,
+            *[bias.reshape(1, cols) for bias in biases],
+        )
+
+    def frames_out(row, values):
+        return pl.pallas_call(
+            frames_kernel,
+            out_shape=[shaped((rows, cols), BF16)] * 4,
+            in_specs=whole(2, True),
+            out_specs=whole(4),
+            compiler_params=PARAMS,
+            cost_estimate=cost(0, 2e6),
+        )(row, values)
+
+    enc_own, enc_half = pack(where_row, enc_conv3, enc_conv1, [enc_bias3, enc_bias1], 1)
     enc_2a = swap(enc_half, "mp", 2)
-    frames_of = frames_out(after(features, enc_half), me, own)
-    feat = [frames_of[0]] + [swap(frames_of[k], "mp", k) for k in (1, 2, 3)]
+    feat = list(frames_out(after(where_row, enc_half), features))
+    feat[2], feat[3] = swap(feat[2], "mp", 2), swap(feat[3], "mp", 3)
+    feat[1] = swap(feat[1], "mp", 1)
     enc_1 = swap(enc_own, "mp", 1)
     enc_2b = swap(enc_2a, "dp", 1)
     enc_3a = swap(enc_2a, "mp", 1)
     enc_3b = swap(enc_2b, "mp", 1)
     enc = (enc_own, enc_1, enc_2a, enc_2b, enc_3a, enc_3b)
 
-    dec_own = pack(dec_conv3, dec_conv1, [dec_bias3])
-    dec_1 = swap(after(dec_own, enc_2a), "mp", 1)
-    dec_2 = swap(after(dec_own, feat[2], feat[3]), "mp", 2)
-
     clip_ends = jnp.cumsum(lengths[0])
     starts = clip_ends - lengths[0]
-    positions = me * own - HALO + jnp.arange(rows + 1, dtype=jnp.int32)
-    is_start = jnp.any(positions[:, None] == starts[None, :], axis=1) | (positions == frames)
-    ok = jnp.where(is_start, 0.0, 1.0).astype(F32)[:, None]
-    prev_ok, next_ok = ok[:-1], ok[1:]
-
+
+    def ok_at(shift):
+        at = me * own - HALO + shift + jnp.arange(rows, dtype=jnp.int32)
+        is_start = jnp.any(at[:, None] == starts[None, :], axis=1) | (at == frames)
+        return jnp.where(is_start, 0.0, 1.0).astype(F32)[:, None]
+
+    prev_ok, next_ok = ok_at(0), ok_at(1)
     books_f = codebooks.astype(F32)
     norms = jnp.sum(books_f * books_f, axis=3) * (LOG2E / SOFTMAX_WARMTH)
     norms = norms[:, :, None, :]
-    turned = codebooks.transpose(0, 1, 3, 2)
+
+    codes = num_codes // near
+    first = near_at * codes
+
+    def own_codes(array):
+        start = (side, level_side, first) + (jnp.int32(0),) * (array.ndim - 3)
+        return lax.dynamic_slice(array, start, (1, 1, codes) + array.shape[3:])[0, 0]
+
+    index = own_codes(buffer_index)
+    one_hot = index[:, None] == jnp.arange(code_buffer.shape[0], dtype=jnp.int32)[None, :]
+    buffer_half = lax.dynamic_slice_in_dim(code_buffer, side * group_dim, group_dim, 1)
+    chosen = dot_nn(one_hot.astype(BF16), buffer_half)
+    books_own = own_codes(codebooks).astype(F32)
+
+    at = jnp.arange(cols, dtype=jnp.int32)
+    turn = ((at[:, None] ^ (near_at * (cols // near))) == at[None, :]).astype(BF16)
+    early_row = after(where_row, chosen, books_own, turn, norms, prev_ok, next_ok)
+
+    (dec_own,) = pack(early_row, dec_conv3, dec_conv1, [dec_bias3], 0)
+    cot = list(frames_out(early_row, out_cotangent))
+    dec_1 = swap(dec_own, "mp", 1)
+    dec_2 = swap(after(dec_own, feat[2], feat[3]), "mp", 2)
 
     hidden_enc, act_mid, latent = pl.pallas_call(
         encoder_kernel,
@@ -431,12 +505,12 @@
         ],
         compiler_params=PARAMS,
         cost_estimate=cost(8 * rows * depth * depth, 12e6),
-    )(where_row, *feat, *enc, prev_ok, next_ok)
+    )(after(where_row, cot[0], dec_own), *feat, *enc, prev_ok, next_ok)
 
     dec_3 = swap(after(dec_2, latent), "mp", 1)
     dec = (dec_own, dec_1, dec_2, dec_3)
-    frames_of = frames_out(after(out_cotangent, dec_2), me, own)
-    cot = [frames_of[0]] + [swap(frames_of[k], "mp", k) for k in (1, 2, 3)]
+    cot[2], cot[3], _ = lax.optimization_barrier((cot[2], cot[3], dec_2))
+    cot = [cot[0]] + [swap(cot[k], "mp", k) for k in (1, 2, 3)]
 
     step = rows // 3
     quant, usage, prob, second = pl.pallas_call(
@@ -464,15 +538,14 @@
     )(latent, codebooks, norms)
 
     packed = 4 * depth + LANES
-    grad_quant, dec_sent, dec_kept = pl.pallas_call(
-        decoder_kernel,
-        out_shape=(
-            shaped((rows, depth), F32),
-            shaped((2, cols, packed), BF16),
-            shaped((2, cols, packed), F32),
-        ),
+    grads_shape = tuple(
+        shaped((cols, packed), dtype) for dtype in (F32, BF16, F32, BF16)
+    )
+    grad_quant, *dec_grads = pl.pallas_call(
+        functools.partial(decoder_kernel, near=near),
+        out_shape=(shaped((rows, depth), F32),) + grads_shape,
         in_specs=whole(12, True),
-        out_specs=tuple(whole(3)),
+        out_specs=tuple(whole(5)),
         scratch_shapes=[
             pltpu.VMEM((rows, depth), BF16),
             pltpu.VMEM((4 * depth + 32, depth), BF16),
@@ -485,7 +558,9 @@
         cost_estimate=cost(24 * rows * depth * depth, 20e6),
     )(where_row, quant, *cot, *dec, prev_ok, next_ok)
 
-    def quantize_back(group, grads):
+    table_shape = (near, group_dim + 16, num_codes // near)
+
+    def quantize_back(group):
         return pl.pallas_call(
             functools.partial(quantize_back_kernel, own=own, levels=levels),
             grid_spec=pltpu.PrefetchScalarGridSpec(
@@ -497,12 +572,13 @@
                     pl.BlockSpec((step, group_dim), lambda i, g: (i, g[0])),
                     pl.BlockSpec((levels - 1, step, group_dim), lambda i, g: (0, i, g[0])),
                     pl.BlockSpec((1, levels, num_codes, group_dim), lambda i, g: (g[0], 0, 0, 0)),
-                    pl.BlockSpec((1, levels, group_dim, num_codes), lambda i, g: (g[0], 0, 0, 0)),
                     pl.BlockSpec((1, levels, 1, num_codes), lambda i, g: (g[0], 0, 0, 0)),
                 ],
                 out_specs=(
                     pl.BlockSpec((step, group_dim), lambda i, g: (i, 0)),
-                    pl.BlockSpec((levels, group_dim + 16, num_codes), lambda i, g: (0, 0, 0)),
+                    pl.BlockSpec(table_shape, lambda i, g: (0, 0, 0)),
+                    pl.BlockSpec(table_shape, lambda i, g: (0, 0, 0)),
+                    pl.BlockSpec((8, LANES), lambda i, g: (0, 0)),
                 ),
                 scratch_shapes=[
                     pltpu.VMEM((levels, group_dim, num_codes), F32),
@@ -511,86 +587,126 @@
             ),
             out_shape=(
                 shaped((rows, group_dim), BF16),
-                shaped((levels, group_dim + 16, num_codes), BF16),
+                shaped(table_shape, BF16),
+                shaped(table_shape, BF16),
+                shaped((8, LANES), F32),
             ),
             compiler_params=PARAMS,
             cost_estimate=cost(16 * rows * num_codes * group_dim, 15e6),
-        )(group.reshape(1), grads, prob, latent, second, codebooks, turned, usage)
-
-    grad_other, table_other = quantize_back(1 - side, grad_quant)
-    dec_got = swap(dec_sent, "mp", 1)
-    dec_held = dec_kept + after(dec_got, table_other).astype(F32)
-    dec_x = swap(dec_held[1].astype(BF16), "mp", 2)
-    table_got = swap(table_other, "mp", 1)
-    grad_mine, table_mine = quantize_back(side, after(grad_quant, dec_held))
-    dec_x, table_got, grad_mine, table_mine = lax.optimization_barrier(
-        (dec_x, table_got, grad_mine, table_mine)
-    )
-    dec_held = dec_held[0] + dec_x.astype(F32)
-    tables = table_mine.astype(F32) + table_got.astype(F32)
-    book_held = lax.dynamic_index_in_dim(tables, level_side, 0, keepdims=False)
-    sent = lax.dynamic_index_in_dim(tables, 1 - level_side, 0, keepdims=False)
-    sent = sent.astype(BF16)
-    dec_mine, dec_y = halves(dec_held, place, dp_bits[0], 0)
-    grad_mine = after(grad_mine, sent, dec_y)
-    book_x = swap(sent, "mp", 2)
-    dec_y = swap(dec_y, "dp", dp_bits[0])
-
-    enc_sent, enc_kept, *outs = pl.pallas_call(
-        encoder_grad_kernel,
-        out_shape=(
-            shaped((2, cols, packed), BF16),
-            shaped((2, cols, packed), F32),
-        )
-        + (shaped((own, cols), BF16),) * 4,
+        )(jnp.stack([group, level_side, near_at]), grad_quant, prob, latent, second, codebooks, usage)
+
+    def gather_near(block):
+        return jnp.concatenate([block] + [swap(block, "dp", k) for k in range(1, near)], 0)
+
+    def stage(*groups):
+        flat = lax.optimization_barrier(tuple(x for group in groups for x in group))
+        out = []
+        for group in groups:
+            out.append(list(flat[: len(group)]))
+            flat = flat[len(group) :]
+        return out
+
+    grad_other, kept_other, sent_other, mark = quantize_back(1 - side)
+    dec_1g, dec_3g = swap(dec_grads[1], "mp", 1), swap(dec_grads[3], "mp", 1)
+    dec_send = low_sum(dec_grads[2], dec_3g).astype(BF16)
+
+    (mine, _), (dec_send,) = stage([side, mark], [dec_send])
+    dec_x = swap(dec_send, "mp", 2)
+    kept_got, sent_got = swap(kept_other, "mp", 1), swap(sent_other, "mp", 1)
+    grad_mine, kept_mine, sent_mine, mark = quantize_back(mine)
+    book_send = low_sum(sent_mine, sent_got).astype(BF16)
+    dec_mine, *dec_send = parts_of(low_sum(dec_grads[0], dec_1g, dec_x), near)
+    dec_send = [piece.astype(BF16) for piece in dec_send]
+
+    (row, _), (book_send,), dec_send = stage([where_row, mark], [book_send], dec_send)
+    book_x = swap(book_send, "mp", 2)
+    dec_got = [swap(piece, "dp", k + 1) for k, piece in enumerate(dec_send)]
+    *enc_grads, low, grad_latent, mark = pl.pallas_call(
+        functools.partial(encoder_weight_grad_kernel, near=near),
+        out_shape=grads_shape + (shaped((rows, depth), BF16),) * 2 + (shaped((8, LANES), F32),),
         in_specs=whole(17, True),
-        out_specs=tuple(whole(6)),
+        out_specs=tuple(whole(7)),
         scratch_shapes=[
             pltpu.VMEM((rows, depth), BF16),
             pltpu.VMEM((4 * depth + 32, depth), BF16),
             pltpu.VMEM((rows + 16, depth), F32),
             pltpu.VMEM((rows, 3 * depth), BF16),
-            pltpu.VMEM((rows, depth), BF16),
-            pltpu.VMEM((rows, depth), BF16),
         ],
         compiler_params=PARAMS,
-        cost_estimate=cost(16 * rows * depth * depth, 20e6),
-    )(where_row, grad_mine, grad_other, hidden_enc, act_mid, *feat, *enc, prev_ok, next_ok)
-
-    enc_sent, book_x, dec_y = lax.optimization_barrier((enc_sent, book_x, dec_y))
-    enc_got = swap(enc_sent, "mp", 1)
-    book_held = book_held + book_x.astype(F32)
-    dec_held = dec_mine + dec_y.astype(F32)
-    enc_held = enc_kept + enc_got.astype(F32)
-    enc_held = enc_held[0] + swap(enc_held[1].astype(BF16), "mp", 2).astype(F32)
-    for bit in dp_bits:
-        book_held = scatter_step(book_held, place, bit, 1)
-    for bit in dp_bits[1:]:
-        dec_held = scatter_step(dec_held, place, bit, 0)
-    for bit in dp_bits:
-        enc_held = scatter_step(enc_held, place, bit, 0)
-
-    codes = book_held.shape[1]
-    first = first_of(place, num_codes, dp_bits)
-
-    def own_codes(array):
-        start = (side, level_side, first) + (jnp.int32(0),) * (array.ndim - 3)
-        return lax.dynamic_slice(array, start, (1, 1, codes) + array.shape[3:])[0, 0]
-
-    index = own_codes(buffer_index)
-    one_hot = index[:, None] == jnp.arange(code_buffer.shape[0], dtype=jnp.int32)[None, :]
-    buffer_half = lax.dynamic_slice_in_dim(code_buffer, side * group_dim, group_dim, 1)
-    chosen = dot_nn(one_hot.astype(BF16), buffer_half)
+        cost_estimate=cost(12 * rows * depth * depth, 20e6),
+    )(row, grad_mine, grad_other, hidden_enc, act_mid, *feat, *enc, prev_ok, next_ok)
+
+    def book_sum(k):
+        return low_sum(kept_mine[k], kept_got[k], book_x[k])
+
+    def pair_sum(held, sent, bit):
+        return held + swap(sent, "dp", bit).astype(F32)
+
+    dec_held = low_sum(dec_mine, *dec_got)
+    enc_1g, enc_3g = swap(enc_grads[1], "mp", 1), swap(enc_grads[3], "mp", 1)
+    book_send, (dec_send, _) = stage(
+        [book_sum(k).astype(BF16) for k in range(1, near)], [dec_held.astype(BF16), mark]
+    )
+    book_got = [swap(piece, "dp", k + 1) for k, piece in enumerate(book_send)]
+    dec_held = pair_sum(dec_held, dec_send, far_bits[0])
+    enc_mine, *enc_near = parts_of(low_sum(enc_grads[0], enc_1g), near)
+    enc_near = [piece.astype(BF16) for piece in enc_near]
+    enc_far = parts_of(low_sum(enc_grads[2], enc_3g).astype(BF16), near)
+    book_held = low_sum(book_sum(0), *book_got)
+
+    (row,), enc_near, enc_far, (book_send, dec_send) = stage(
+        [where_row], enc_near, enc_far, [book_held.astype(BF16), dec_held.astype(BF16)]
+    )
+    enc_got = [swap(piece, "dp", k + 1) for k, piece in enumerate(enc_near)] + [
+        swap_both(piece, k, 2) for k, piece in enumerate(enc_far)
+    ]
+    book_held = pair_sum(book_held, book_send, far_bits[0])
+    dec_held = pair_sum(dec_held, dec_send, far_bits[1])
+    for bit in far_bits[2:]:
+        dec_held = pair_sum(dec_held, dec_held.astype(BF16), bit)
+    outs = pl.pallas_call(
+        encoder_input_grad_kernel,
+        out_shape=(shaped((own, cols), BF16),) * 4,
+        in_specs=whole(15, True),
+        out_specs=tuple(whole(4)),
+        scratch_shapes=[
+            pltpu.VMEM((rows, depth), BF16),
+            pltpu.VMEM((4 * depth + 32, depth), BF16),
+            pltpu.VMEM((rows + 16, depth), F32),
+            pltpu.VMEM((rows, 3 * depth), BF16),
+        ],
+        compiler_params=PARAMS,
+        cost_estimate=cost(6 * rows * depth * depth, 10e6),
+    )(row, low, grad_latent, *feat, *enc, prev_ok, next_ok)
+
+    enc_held = low_sum(enc_mine, *enc_got)
+    (book_send, dec_send, enc_send), outs_send = stage(
+        [book_held.astype(BF16), dec_held.astype(BF16), enc_held.astype(BF16)], outs[1:]
+    )
+    book_held = pair_sum(book_held, book_send, far_bits[1])
+    enc_held = pair_sum(enc_held, enc_send, far_bits[0])
+    outs = [outs[0]] + [swap(piece, "mp", k + 1) for k, piece in enumerate(outs_send)]
+    dec_held = gather_near(dec_send)
+    for bit in far_bits[2:]:
+        book_held = pair_sum(book_held, book_held.astype(BF16), bit)
+
     share = num_codes / (frames * n_dp)
     book_held = book_held.T
     ratio = book_held[:, group_dim : group_dim + 1] * share
     refresh = jax.nn.sigmoid(SHARPNESS * (THRESHOLD - ratio))
-    stepped = own_codes(codebooks).astype(F32) - (STEP_SCALE * share) * book_held[:, :group_dim]
+    stepped = books_own - (STEP_SCALE * share) * book_held[:, :group_dim]
     fresh = ((1.0 - refresh) * stepped + refresh * chosen).astype(BF16)
-    for bit in reversed(dp_bits):
-        fresh = gather_step(fresh, "dp", bit)
-    fresh = gather_step(fresh, "mp", 2)
-    fresh_other = swap(fresh, "mp", 1)
+
+    (fresh, enc_send), _ = stage([fresh, enc_held.astype(BF16)], [])
+    enc_held = pair_sum(enc_held, enc_send, far_bits[1])
+    for bit in far_bits[2:]:
+        enc_held = pair_sum(enc_held, enc_held.astype(BF16), bit)
+    fresh = [
+        swap_both(fresh, k, bits) if k or bits else fresh for bits in (0, 2) for k in range(near)
+    ]
+    enc_turn = enc_held.astype(BF16)
+    enc_held = gather_near(enc_turn)
+    fresh = fresh + [swap(part, "mp", 1) for part in fresh]
 
     def put(mask, block, total, *pieces):
         return pl.pallas_call(
@@ -603,16 +719,9 @@
         )(mask.reshape(1), *pieces)
 
     mask = (side * levels + level_side) * num_codes + first
-    new_codebooks = put(mask, codes, groups * levels * num_codes, fresh, fresh_other)
-
-    turn = jnp.arange(cols, dtype=jnp.int32)
-    turn = (turn[:, None] ^ first_of(place, cols, dp_bits)) == turn[None, :]
-    turn = turn.astype(BF16)
+    new_codebooks = put(mask, codes, groups * levels * num_codes, *fresh)
 
     def unpack(held):
-        held = held.astype(BF16)
-        for bit in reversed(dp_bits):
-            held = gather_step(held, "dp", bit)
         biases = dot_tn(held[:, 4 * depth :], turn)
         return (
             dot_tn(held[:, : 3 * depth], turn).reshape(3, depth, cols),
@@ -621,8 +730,7 @@
             biases[1],
         )
 
-    outs = [outs[0]] + [swap(outs[k], "mp", k) for k in (1, 2, 3)]
-    grad_features = put(me * own, own, frames, *outs)
+    grad_features = put(after(me * own, enc_turn), own, frames, *outs)
 
     return (
         grad_features,

time: 246 us -> 229 us (0.931)
  waiting for transfers between devices: 82.2 us -> 47.4 us
  Pallas kernels: 77.3 us -> 105 us
  local copies, waits for them, and re-layouts: 35.3 us -> 15.5 us
  other arithmetic: 13.3 us -> 19.1 us
  starting transfers between devices: 32 us -> 34.5 us
    ppermute x43 -> x40, waiting for transfers between devices: 82.2 us -> 40.1 us  [swap(): return lax.ppermute(values, axis, [(i, i ^ bits) for i in range(size)])]
    pallas_call x2, Pallas kernels: 24.4 us -> 38.4 us  [quantize_back(): pl.pallas_call(functools.partial(quantize_back_kernel, own=own, levels=le...]
    pallas_call x2 -> x7, Pallas kernels: 25.2 us -> 38.9 us  [the longest x1 13 us: body(): pl.pallas_call(functools.partial(decoder_kernel, near=near), out_shape=(s...]
    unnamed x56 -> x89, local copies, waits for them, and re-layouts: 20.4 us -> 8.13 us
    convert_element_type x2 -> x13, other arithmetic: 0.03 us -> 11.1 us  [the longest x3 3.79 us: body(): dec_held.astype(BF16)]
    ppermute x0 -> x5, waiting for transfers between devices: none -> 7.24 us  [swap_both(): return lax.ppermute(values, ('dp', 'mp'), pairs)]
    ppermute x0 -> x5, starting transfers between devices: none -> 6.74 us  [swap_both(): return lax.ppermute(values, ('dp', 'mp'), pairs)]
    dynamic_slice x5 -> x1, local copies, waits for them, and re-layouts: 6.36 us -> 0.76 us  [own_codes(): lax.dynamic_slice(array, start, (1, 1, codes) + array.shape[3:])[0, 0]]
  transfers between devices with their start and end apart: 43 -> 45, of which waited for: 22 -> 10; matrix products, arithmetic and copies ran while one was open for 17% -> 13% of each run, Pallas kernels for 26% -> 39%
where the time goes in v4:
time: 229 us
  Pallas kernels  105 us (46%)
  waiting for transfers between devices  47.4 us (21%)
  starting transfers between devices  34.5 us (15%)
  other arithmetic  19.1 us (8%)
  local copies, waits for them, and re-layouts  15.5 us (7%)
  matrix products  6.05 us (3%)
    ppermute x40, waiting for transfers between devices, swap(): return lax.ppermute(values, axis, [(i, i ^ bits) for i in range(size)])  40.1 us
    pallas_call x2, Pallas kernels, quantize_back(): pl.pallas_call(functools.partial(quantize_back_kernel, own=own, levels=le...  38.4 us
    ppermute x40, starting transfers between devices, swap(): return lax.ppermute(values, axis, [(i, i ^ bits) for i in range(size)])  27.8 us
    pallas_call x1, Pallas kernels, body(): pl.pallas_call(functools.partial(quantize_kernel, own=own), grid=(3,), ou...  13.1 us
    pallas_call x1, Pallas kernels, body(): pl.pallas_call(functools.partial(decoder_kernel, near=near), out_shape=(s...  13 us
    pallas_call x1, Pallas kernels, body(): pl.pallas_call(functools.partial(encoder_weight_grad_kernel, near=near),...  10.6 us
    pallas_call x1, Pallas kernels, body(): pl.pallas_call(encoder_kernel, out_shape=(shaped((rows, depth), F32), sha...  8.2 us
    unnamed x89, local copies, waits for them, and re-layouts  8.13 us
  transfers between devices with their start and end apart: 45, of which 10 were waited for; matrix products, arithmetic and copies ran while one was open for 13% of the time, Pallas kernels for 39%

profile of v4, /device:TPU:0, one launch (start us, length us, event | category | flops | bytes accessed | tf_op | source)
XLA Modules:
  0.0 229.1 jit_solution(18312677481875449022)
XLA Ops:
  1.3 2.0 shard_map.206
  3.3 2.9 %collective-permute-start.4 = (bf16[1040,128]{1,0:T(8,128)(2,1)}, bf16[1040,128]{1,0:T(8,128)(2,1)}, u32[]{:S(2)}, u32[]{:S(2)}) collective-permute-start(bf16[1040,128]{1,0:T(8,128)(2,1)} %get-tuple-element.80), channel_id=1, source_target_pairs={{0,2},{1,3},{2,0},{3,1},{4,6},{5,7},{6,4},{7,5},{8,10},{9,11},{10,... | collective-permute-start | bytes 798728 | tf_op jit(solution)/shard_map/ppermute | solution.py:45
  6.2 2.3 shard_map.207
  14.4 1.5 collective-permute-start.5
  17.2 1.9 shard_map.205.w0
  19.4 4.3 %collective-permute-done.2.f3 = bf16[1056,128]{1,0:T(8,128)(2,1)} collective-permute-done((bf16[1056,128]{1,0:T(8,128)(2,1)}, bf16[1056,128]{1,0:T(8,128)(2,1)}, u32[]{:S(2)}, u32[]{:S(2)}) %collective-permute-start.2) | collective-permute-done | bytes 270368 | tf_op jit(solution)/shard_map/ppermute | solution.py:45
  26.3 2.3 shard_map.204
  29.6 8.2 %shard_map.208 = (f32[1056,512]{1,0:T(8,128)}, bf16[1056,512]{1,0:T(8,128)(2,1)}, bf16[1056,512]{1,0:T(8,128)(2,1)}) custom-call(s32[3]{0:T(128)} %pad_add_fusion.where_ref.me_ref, bf16[1056,128]{1,0:T(8,128)(2,1)} %get-tuple-element.82.f0, bf16[1056,128]{1,0:T(8,128)(2,1)} %copy-done.14, bf16[1056,128]{1,0:T(8,128)(2,1)} %copy-done.13, ...), custom_call_target="tpu_custom_call" | custom-call | flops 2214592512 | bytes 12000000 | tf_op jit(solution)/shard_map/pallas_call | solution.py:491
  39.1 1.7 collective-permute-start.10
  40.8 13.1 %shard_map.209 = (bf16[1056,512]{1,0:T(8,128)(2,1)}, f32[2,2,1,1024]{3,2,1,0:T(1,128)}, bf16[2,2,1056,1024]{3,2,1,0:T(8,128)(2,1)}, bf16[1,1056,512]{2,1,0:T(8,128)(2,1)}) custom-call(bf16[1056,512]{1,0:T(8,128)(2,1)} %get-tuple-element.87.latent_ref.first_ref, bf16[2,2,1024,256]{3,2,1,0:T(8,128)(2,1)} %books.5, f32[2,2,1,1024]{3,2,1,0:T(1,128)} %mul.83.norms), custom_call_target="tpu_custom_call" | custom-call | flops 4429185024 | bytes 30000000 | tf_op jit(solution)/shard_map/pallas_call | solution.py:516
  55.2 13.0 %shard_map.210 = (f32[1056,512]{1,0:T(8,128)}, f32[128,2176]{1,0:T(8,128)}, bf16[128,2176]{1,0:T(8,128)(2,1)}, f32[128,2176]{1,0:T(8,128)}, bf16[128,2176]{1,0:T(8,128)(2,1)}) custom-call(s32[3]{0:T(128)} %pad_add_fusion.where_ref.me_ref, bf16[1056,512]{1,0:T(8,128)(2,1)} %get-tuple-element.88.quant, bf16[1056,128]{1,0:T(8,128)(2,1)} %get-tuple-element.78.c0, ...), custom_call_target="tpu_custom_call" | custom-call | flops 6643777536 | bytes 20000000 | tf_op jit(solution)/shard_map/pallas_call | solution.py:544
  69.4 25.7 %shard_map.212 = (bf16[1056,256]{1,0:T(8,128)(2,1)}, bf16[2,272,512]{2,1,0:T(8,128)(2,1)}, bf16[2,272,512]{2,1,0:T(8,128)(2,1)}, f32[8,128]{1,0:T(8,128)}) custom-call(s32[3]{0:T(128)} %add_add_fusion.1.group_ref, f32[1056,512]{1,0:T(8,128)} %get-tuple-element.99.grad_ref, bf16[2,2,1056,1024]{3,2,1,0:T(8,128)(2,1)} %get-tuple-element.100.prob_ref, ...), custom_call_target="tpu_custom_call" | custom-call | flops 4429185024 | bytes 15000000 | tf_op jit(solution)/shard_map/pallas_call | solution.py:564
  96.6 1.7 collective-permute-start.17
  98.9 12.6 %shard_map.211 = (bf16[1056,256]{1,0:T(8,128)(2,1)}, bf16[2,272,512]{2,1,0:T(8,128)(2,1)}, bf16[2,272,512]{2,1,0:T(8,128)(2,1)}, f32[8,128]{1,0:T(8,128)}) custom-call(s32[3]{0:T(128)} %add_add_fusion.group_ref, f32[1056,512]{1,0:T(8,128)} %get-tuple-element.99.grad_ref, bf16[2,2,1056,1024]{3,2,1,0:T(8,128)(2,1)} %get-tuple-element.100.prob_ref, ...), custom_call_target="tpu_custom_call" | custom-call | flops 4429185024 | bytes 15000000 | tf_op jit(solution)/shard_map/pallas_call | solution.py:564
  117.0 1.6 collective-permute-start.22
  119.2 10.6 %shard_map.213 = (f32[128,2176]{1,0:T(8,128)}, bf16[128,2176]{1,0:T(8,128)(2,1)}, f32[128,2176]{1,0:T(8,128)}, bf16[128,2176]{1,0:T(8,128)(2,1)}, bf16[1056,512]...) custom-call(s32[3]{0:T(128)} %pad_add_fusion.where_ref.me_ref, ...), custom_call_target="tpu_custom_call" | custom-call | flops 3321888768 | bytes 20000000 | tf_op jit(solution)/shard_map/pallas_call | solution.py:624
  135.9 1.6 collective-permute-start.24
  139.4 2.1 convert_add_fusion
  143.6 1.8 slice.197
  145.4 1.8 fusion.20
  148.4 2.6 %collective-permute-start.29 = (bf16[64,2176]{1,0:T(8,128)(2,1)}, bf16[64,2176]{1,0:T(8,128)(2,1)}, u32[]{:S(2)}, u32[]{:S(2)}) collective-permute-start(bf16[64,2176]{1,0:T(8,128)(2,1)} %fusion.20), channel_id=1, source_target_pairs={{0,16},{4,20},{8,24},{12,28},{16,0},{20,4},{24,8},{28,12},{1,17},{... | collective-permute-start | bytes 835592 | tf_op jit(solution)/shard_map/ppermute | solution.py:45
  152.9 1.6 collective-permute-start.27
  155.0 6.7 %shard_map.214 = (bf16[1024,128]{1,0:T(8,128)(2,1)}, bf16[1024,128]{1,0:T(8,128)(2,1)}, bf16[1024,128]{1,0:T(8,128)(2,1)}, bf16[1024,128]{1,0:T(8,128)(2,1)}) custom-call(s32[3]{0:T(128)} %pad_add_fusion.where_ref.me_ref, bf16[1056,512]{1,0:T(8,128)(2,1)} %get-tuple-element.129.low, bf16[1056,512]{1,0:T(8,128)(2,1)} %get-tuple-element.130.grad_latent, ...), custom_call_target="tpu_custom_call" | custom-call | flops 1660944384 | bytes 10000000 | tf_op jit(solution)/shard_map/pallas_call | solution.py:667
  163.6 5.1 %collective-permute-done.28 = bf16[272,512]{0,1:T(8,128)(2,1)S(1)} collective-permute-done((bf16[272,512]{0,1:T(8,128)(2,1)}, bf16[272,512]{0,1:T(8,128)(2,1)S(1)}, u32[]{:S(2)}, u32[]{:S(2)}) %collective-permute-start.28) | collective-permute-done | bytes 278560 | tf_op jit(solution)/shard_map/ppermute | solution.py:45
  171.1 1.5 collective-permute-start.34
  172.6 15.5 %collective-permute-done.31 = bf16[272,512]{0,1:T(8,128)(2,1)S(1)} collective-permute-done((bf16[272,512]{0,1:T(8,128)(2,1)S(1)}, bf16[272,512]{0,1:T(8,128)(2,1)S(1)}, u32[]{:S(2)}, u32[]{:S(2)}) %collective-permute-start.31) | collective-permute-done | bytes 278560 | tf_op jit(solution)/shard_map/ppermute | solution.py:45
  190.6 1.6 collective-permute-start.38
  193.4 1.8 collective-permute-start.39
  195.2 11.8 %collective-permute-done.32 = bf16[64,2176]{1,0:T(8,128)(2,1)S(1)} collective-permute-done((bf16[64,2176]{1,0:T(8,128)(2,1)S(1)}, bf16[64,2176]{1,0:T(8,128)(2,1)S(1)}, u32[]{:S(2)}, u32[]{:S(2)}) %collective-permute-start.32) | collective-permute-done | bytes 278560 | tf_op jit(solution)/shard_map/ppermute | solution.py:45
  209.0 7.2 %collective-permute-done.40.refs_3_ = bf16[512,256]{1,0:T(8,128)(2,1)S(1)} collective-permute-done((bf16[512,256]{1,0:T(8,128)(2,1)S(1)}, bf16[512,256]{1,0:T(8,128)(2,1)S(1)}, u32[]{:S(2)}, u32[]{:S(2)}) %collective-permute-start.40) | collective-permute-done | bytes 262176 | tf_op jit(solution)/shard_map/ppermute | solution.py:61
  218.6 2.6 %shard_map.215 = f32[4096,128]{1,0:T(8,128)} custom-call(s32[1]{0:T(128)} %bitcast.18.mask_ref, bf16[1024,128]{1,0:T(8,128)(2,1)} %get-tuple-element.138.refs_0_, bf16[1024,128]{1,0:T(8,128)(2,1)} %copy-done.25, bf16[1024,128]{1,0:T(8,128)(2,1)} %copy-done.26, bf16[1024,128]{1,0:T(8,128)(2,1)} %copy-done.27), custom_call_target="tpu_custom_call" | custom-call | bytes 4194304 | tf_op jit(solution)/shard_map/pallas_call | solution.py:712
  222.2 3.8 %shard_map.216 = f32[4096,256]{1,0:T(8,128)} custom-call(s32[1]{0:T(128)} %bitcast.25.mask_ref, bf16[512,256]{1,0:T(8,128)(2,1)} %copy-done.10, bf16[512,256]{1,0:T(8,128)(2,1)} %copy-done.18, bf16[512,256]{1,0:T(8,128)(2,1)} %copy-done.19, bf16[512,256]{1,0:T(8,128)(2,1)} %copy-done.20, bf16[512,256]{1,0:T(8,128)(2,1)} %copy-done.21, ...), custom_call_target="tpu_custom_call" | custom-call | bytes 8388608 | tf_op jit(solution)/shard_map/pallas_call | solution.py:712
  (207 shorter events, 52.7 us)
Async XLA Ops:
  8.7 15.1 %collective-permute-start.2 = (bf16[1056,128]{1,0:T(8,128)(2,1)}, bf16[1056,128]{1,0:T(8,128)(2,1)}, u32[]{:S(2)}, u32[]{:S(2)}) collective-permute-start(bf16[1056,128]{1,0:T(8,128)(2,1)} %get-tuple-element.85), channel_id=1, source_target_pairs={{0,3},{1,2},{2,1},{3,0},{4,7},{5,6},{6,5},{7,4},{8,11},{9,10},{10,... | collective-permute-start | bytes 811016 | tf_op jit(solution)/shard_map/ppermute | solution.py:45
  9.4 19.4 %collective-permute-start.3 = (bf16[2080,128]{1,0:T(8,128)(2,1)}, bf16[2080,128]{1,0:T(8,128)(2,1)}, u32[]{:S(2)}, u32[]{:S(2)}) collective-permute-start(bf16[2080,128]{1,0:T(8,128)(2,1)} %get-tuple-element.86.w0), channel_id=1, source_target_pairs={{0,1},{1,0},{2,3},{3,2},{4,5},{5,4},{6,7},{7,6},{8,9},{9,8},{10,11... | collective-permute-start | bytes 1597448 | tf_op jit(solution)/shard_map/ppermute | solution.py:45
  23.8 14.8 %collective-permute-start.9 = (bf16[2080,128]{1,0:T(8,128)(2,1)}, bf16[2080,128]{1,0:T(8,128)(2,1)S(1)}, u32[]{:S(2)}, u32[]{:S(2)}) collective-permute-start(bf16[2080,128]{1,0:T(8,128)(2,1)} %shard_map.205.w0), channel_id=1, source_target_pairs={{0,2},{1,3},{2,0},{3,1},{4,6},{5,7},{6,4},{7,5},{8,10},{9,11},{10,... | collective-permute-start | bytes 1597448 | tf_op jit(solution)/shard_map/ppermute | solution.py:45
  28.6 25.4 %collective-permute-start.12 = (bf16[2080,128]{1,0:T(8,128)(2,1)}, bf16[2080,128]{1,0:T(8,128)(2,1)S(1)}, u32[]{:S(2)}, u32[]{:S(2)}) collective-permute-start(bf16[2080,128]{1,0:T(8,128)(2,1)} %shard_map.205.w0), channel_id=1, source_target_pairs={{0,1},{1,0},{2,3},{3,2},{4,5},{5,4},{6,7},{7,6},{8,9},{9,8},{10,11... | collective-permute-start | bytes 1597448 | tf_op jit(solution)/shard_map/ppermute | solution.py:45
  38.6 15.5 %collective-permute-start.13 = (bf16[2080,128]{1,0:T(8,128)(2,1)S(1)}, bf16[2080,128]{1,0:T(8,128)(2,1)S(1)}, u32[]{:S(2)}, u32[]{:S(2)}) collective-permute-start(bf16[2080,128]{1,0:T(8,128)(2,1)S(1)} %collective-permute-done.9.w2), channel_id=1, source_target_pairs={{0,1},{1,0},{2,3},{3,2},{4,5},{5,4},{6,7},{7,6},{8,9},{9,8},{10,11... | collective-permute-start | bytes 1597448 | tf_op jit(solution)/shard_map/ppermute | solution.py:45
  38.6 15.4 %collective-permute-start.8 = (bf16[1056,128]{1,0:T(8,128)(2,1)S(1)}, bf16[1056,128]{1,0:T(8,128)(2,1)S(1)}, u32[]{:S(2)}, u32[]{:S(2)}) collective-permute-start(bf16[1056,128]{1,0:T(8,128)(2,1)S(1)} %copy-done.34), channel_id=1, source_target_pairs={{0,1},{1,0},{2,3},{3,2},{4,5},{5,4},{6,7},{7,6},{8,9},{9,8},{10,11... | collective-permute-start | bytes 811016 | tf_op jit(solution)/shard_map/ppermute | solution.py:45
  39.1 14.9 %collective-permute-start.10 = (bf16[1056,128]{1,0:T(8,128)(2,1)S(1)}, bf16[1056,128]{1,0:T(8,128)(2,1)S(1)}, u32[]{:S(2)}, u32[]{:S(2)}) collective-permute-start(bf16[1056,128]{1,0:T(8,128)(2,1)S(1)} %copy-done.33), channel_id=1, source_target_pairs={{0,2},{1,3},{2,0},{3,1},{4,6},{5,7},{6,4},{7,5},{8,10},{9,11},{10,... | collective-permute-start | bytes 811016 | tf_op jit(solution)/shard_map/ppermute | solution.py:45
  40.8 13.2 %collective-permute-start.11 = (bf16[1056,128]{1,0:T(8,128)(2,1)S(1)}, bf16[1056,128]{1,0:T(8,128)(2,1)S(1)}, u32[]{:S(2)}, u32[]{:S(2)}) collective-permute-start(bf16[1056,128]{1,0:T(8,128)(2,1)S(1)} %copy-done.32), channel_id=1, source_target_pairs={{0,3},{1,2},{2,1},{3,0},{4,7},{5,6},{6,5},{7,4},{8,11},{9,10},{10,... | collective-permute-start | bytes 811016 | tf_op jit(solution)/shard_map/ppermute | solution.py:45
  68.3 27.4 %collective-permute-start.14 = (bf16[128,2176]{1,0:T(8,128)(2,1)}, bf16[128,2176]{1,0:T(8,128)(2,1)S(1)}, u32[]{:S(2)}, u32[]{:S(2)}) collective-permute-start(bf16[128,2176]{1,0:T(8,128)(2,1)} %get-tuple-element.97), channel_id=1, source_target_pairs={{0,1},{1,0},{2,3},{3,2},{4,5},{5,4},{6,7},{7,6},{8,9},{9,8},{10,11... | collective-permute-start | bytes 1671176 | tf_op jit(solution)/shard_map/ppermute | solution.py:45
  69.2 45.7 %collective-permute-start.16 = (bf16[128,2176]{1,0:T(8,128)(2,1)}, bf16[128,2176]{1,0:T(8,128)(2,1)S(1)}, u32[]{:S(2)}, u32[]{:S(2)}) collective-permute-start(bf16[128,2176]{1,0:T(8,128)(2,1)} %get-tuple-element.106), channel_id=1, source_target_pairs={{0,1},{1,0},{2,3},{3,2},{4,5},{5,4},{6,7},{7,6},{8,9},{9,8},{10,11... | collective-permute-start | bytes 1671176 | tf_op jit(solution)/shard_map/ppermute | solution.py:45
  95.1 18.3 %collective-permute-start.15 = (bf16[2,272,512]{2,1,0:T(8,128)(2,1)}, bf16[2,272,512]{2,1,0:T(8,128)(2,1)}, u32[]{:S(2)}, u32[]{:S(2)}) collective-permute-start(bf16[2,272,512]{2,1,0:T(8,128)(2,1)} %get-tuple-element.104), channel_id=1, source_target_pairs={{0,1},{1,0},{2,3},{3,2},{4,5},{5,4},{6,7},{7,6},{8,9},{9,8},{10,11... | collective-permute-start | bytes 1671176 | tf_op jit(solution)/shard_map/ppermute | solution.py:45
  95.6 17.4 %collective-permute-start.20 = (bf16[2,272,512]{2,1,0:T(8,128)(2,1)}, bf16[2,272,512]{2,1,0:T(8,128)(2,1)S(1)}, u32[]{:S(2)}, u32[]{:S(2)}) collective-permute-start(bf16[2,272,512]{2,1,0:T(8,128)(2,1)} %get-tuple-element.118), channel_id=1, source_target_pairs={{0,1},{1,0},{2,3},{3,2},{4,5},{5,4},{6,7},{7,6},{8,9},{9,8},{10,11... | collective-permute-start | bytes 1671176 | tf_op jit(solution)/shard_map/ppermute | solution.py:45
  96.6 18.3 %collective-permute-start.17 = (bf16[128,2176]{1,0:T(8,128)(2,1)}, bf16[128,2176]{1,0:T(8,128)(2,1)S(1)}, u32[]{:S(2)}, u32[]{:S(2)}) collective-permute-start(bf16[128,2176]{1,0:T(8,128)(2,1)} %add_convert_fusion.2), channel_id=1, source_target_pairs={{0,2},{1,3},{2,0},{3,1},{4,6},{5,7},{6,4},{7,5},{8,10},{9,11},{10,... | collective-permute-start | bytes 1671176 | tf_op jit(solution)/shard_map/ppermute | solution.py:45
  117.0 13.4 %collective-permute-start.22 = (bf16[64,2176]{1,0:T(8,128)(2,1)S(1)}, bf16[64,2176]{1,0:T(8,128)(2,1)S(1)}, u32[]{:S(2)}, u32[]{:S(2)}) collective-permute-start(bf16[64,2176]{1,0:T(8,128)(2,1)S(1)} %slice.198), channel_id=1, source_target_pairs={{0,4},{4,0},{8,12},{12,8},{16,20},{20,16},{24,28},{28,24},{1,5},{5... | collective-permute-start | bytes 835592 | tf_op jit(solution)/shard_map/ppermute | solution.py:45
  118.6 14.4 %collective-permute-start.21 = (bf16[2,272,512]{2,1,0:T(8,128)(2,1)S(1)}, bf16[2,272,512]{2,1,0:T(8,128)(2,1)S(1)}, u32[]{:S(2)}, u32[]{:S(2)}) collective-permute-start(bf16[2,272,512]{2,1,0:T(8,128)(2,1)S(1)} %add_convert_fusion.1), channel_id=1, source_target_pairs={{0,2},{1,3},{2,0},{3,1},{4,6},{5,7},{6,4},{7,5},{8,10},{9,11},{10,... | collective-permute-start | bytes 1671176 | tf_op jit(solution)/shard_map/ppermute | solution.py:45
  148.4 14.0 %collective-permute-start.29 = (bf16[64,2176]{1,0:T(8,128)(2,1)}, bf16[64,2176]{1,0:T(8,128)(2,1)}, u32[]{:S(2)}, u32[]{:S(2)}) collective-permute-start(bf16[64,2176]{1,0:T(8,128)(2,1)} %fusion.20), channel_id=1, source_target_pairs={{0,16},{4,20},{8,24},{12,28},{16,0},{20,4},{24,8},{28,12},{1,17},{... | collective-permute-start | bytes 835592 | tf_op jit(solution)/shard_map/ppermute | solution.py:45
  151.0 18.3 %collective-permute-start.25 = (bf16[64,2176]{1,0:T(8,128)(2,1)}, bf16[64,2176]{1,0:T(8,128)(2,1)S(1)}, u32[]{:S(2)}, u32[]{:S(2)}) collective-permute-start(bf16[64,2176]{1,0:T(8,128)(2,1)} %slice.197), channel_id=1, source_target_pairs={{0,4},{4,0},{8,12},{12,8},{16,20},{20,16},{24,28},{28,24},{1,5},{5... | collective-permute-start | bytes 835592 | tf_op jit(solution)/shard_map/ppermute | solution.py:45
  152.3 17.0 %collective-permute-start.26 = (bf16[64,2176]{1,0:T(8,128)(2,1)}, bf16[64,2176]{1,0:T(8,128)(2,1)S(1)}, u32[]{:S(2)}, u32[]{:S(2)}) collective-permute-start(bf16[64,2176]{1,0:T(8,128)(2,1)} %get-tuple-element.124), channel_id=1, source_target_pairs={{0,2},{1,3},{2,0},{3,1},{4,6},{5,7},{6,4},{7,5},{8,10},{9,11},{10,... | collective-permute-start | bytes 835592 | tf_op jit(solution)/shard_map/ppermute | solution.py:61
  152.9 16.4 %collective-permute-start.27 = (bf16[64,2176]{1,0:T(8,128)(2,1)}, bf16[64,2176]{1,0:T(8,128)(2,1)S(1)}, u32[]{:S(2)}, u32[]{:S(2)}) collective-permute-start(bf16[64,2176]{1,0:T(8,128)(2,1)} %get-tuple-element.125), channel_id=1, source_target_pairs={{0,6},{1,7},{2,4},{3,5},{4,2},{5,3},{6,0},{7,1},{8,14},{9,15},{10,... | collective-permute-start | bytes 835592 | tf_op jit(solution)/shard_map/ppermute | solution.py:61
  154.5 14.3 %collective-permute-start.28 = (bf16[272,512]{0,1:T(8,128)(2,1)}, bf16[272,512]{0,1:T(8,128)(2,1)S(1)}, u32[]{:S(2)}, u32[]{:S(2)}) collective-permute-start(bf16[272,512]{0,1:T(8,128)(2,1)} %fusion.49), channel_id=1, source_target_pairs={{0,8},{4,12},{8,0},{12,4},{16,24},{20,28},{24,16},{28,20},{1,9},{5... | collective-permute-start | bytes 835592 | tf_op jit(solution)/shard_map/ppermute | solution.py:45
  169.4 19.0 %collective-permute-start.30 = (bf16[64,2176]{1,0:T(8,128)(2,1)S(1)}, bf16[64,2176]{1,0:T(8,128)(2,1)S(1)}, u32[]{:S(2)}, u32[]{:S(2)}) collective-permute-start(bf16[64,2176]{1,0:T(8,128)(2,1)S(1)} %get-tuple-element.134), channel_id=1, source_target_pairs={{0,8},{4,12},{8,0},{12,4},{16,24},{20,28},{24,16},{28,20},{1,9},{5... | collective-permute-start | bytes 835592 | tf_op jit(solution)/shard_map/ppermute | solution.py:45
  169.5 18.6 %collective-permute-start.31 = (bf16[272,512]{0,1:T(8,128)(2,1)S(1)}, bf16[272,512]{0,1:T(8,128)(2,1)S(1)}, u32[]{:S(2)}, u32[]{:S(2)}) collective-permute-start(bf16[272,512]{0,1:T(8,128)(2,1)S(1)} %fusion.4), channel_id=1, source_target_pairs={{0,16},{4,20},{8,24},{12,28},{16,0},{20,4},{24,8},{28,12},{1,17},{... | collective-permute-start | bytes 835592 | tf_op jit(solution)/shard_map/ppermute | solution.py:45
  169.6 22.6 %collective-permute-start.37 = (bf16[64,2176]{1,0:T(8,128)(2,1)S(1)}, bf16[64,2176]{1,0:T(8,128)(2,1)S(1)}, u32[]{:S(2)}, u32[]{:S(2)}) collective-permute-start(bf16[64,2176]{1,0:T(8,128)(2,1)S(1)} %add_convert_fusion.5), channel_id=1, source_target_pairs={{0,4},{4,0},{8,12},{12,8},{16,20},{20,16},{24,28},{28,24},{1,5},{5... | collective-permute-start | bytes 835592 | tf_op jit(solution)/shard_map/ppermute | solution.py:45
  171.1 22.3 %collective-permute-start.33 = (bf16[1024,128]{1,0:T(8,128)(2,1)S(1)}, bf16[1024,128]{1,0:T(8,128)(2,1)S(1)}, u32[]{:S(2)}, u32[]{:S(2)}) collective-permute-start(bf16[1024,128]{1,0:T(8,128)(2,1)S(1)} %copy-done.40), channel_id=1, source_target_pairs={{0,1},{1,0},{2,3},{3,2},{4,5},{5,4},{6,7},{7,6},{8,9},{9,8},{10,11... | collective-permute-start | bytes 786440 | tf_op jit(solution)/shard_map/ppermute | solution.py:45
  171.1 37.2 %collective-permute-start.34 = (bf16[1024,128]{1,0:T(8,128)(2,1)S(1)}, bf16[1024,128]{1,0:T(8,128)(2,1)S(1)}, u32[]{:S(2)}, u32[]{:S(2)}) collective-permute-start(bf16[1024,128]{1,0:T(8,128)(2,1)S(1)} %copy-done.39), channel_id=1, source_target_pairs={{0,2},{1,3},{2,0},{3,1},{4,6},{5,7},{6,4},{7,5},{8,10},{9,11},{10,... | collective-permute-start | bytes 786440 | tf_op jit(solution)/shard_map/ppermute | solution.py:45
  188.1 28.1 %collective-permute-start.35 = (bf16[1024,128]{1,0:T(8,128)(2,1)S(1)}, bf16[1024,128]{1,0:T(8,128)(2,1)S(1)}, u32[]{:S(2)}, u32[]{:S(2)}) collective-permute-start(bf16[1024,128]{1,0:T(8,128)(2,1)S(1)} %copy-done.38), channel_id=1, source_target_pairs={{0,3},{1,2},{2,1},{3,0},{4,7},{5,6},{6,5},{7,4},{8,11},{9,10},{10,... | collective-permute-start | bytes 786440 | tf_op jit(solution)/shard_map/ppermute | solution.py:45
  190.6 17.8 %collective-permute-start.38 = (bf16[512,256]{1,0:T(8,128)(2,1)S(1)}, bf16[512,256]{1,0:T(8,128)(2,1)S(1)}, u32[]{:S(2)}, u32[]{:S(2)}) collective-permute-start(bf16[512,256]{1,0:T(8,128)(2,1)S(1)} %fusion.12.refs_0_), channel_id=1, source_target_pairs={{0,4},{1,5},{2,6},{3,7},{4,0},{5,1},{6,2},{7,3},{8,12},{9,13},{10,... | collective-permute-start | bytes 786440 | tf_op jit(solution)/shard_map/ppermute | solution.py:61
  192.2 14.8 %collective-permute-start.32 = (bf16[64,2176]{1,0:T(8,128)(2,1)S(1)}, bf16[64,2176]{1,0:T(8,128)(2,1)S(1)}, u32[]{:S(2)}, u32[]{:S(2)}) collective-permute-start(bf16[64,2176]{1,0:T(8,128)(2,1)S(1)} %fusion.21), channel_id=1, source_target_pairs={{0,16},{4,20},{8,24},{12,28},{16,0},{20,4},{24,8},{28,12},{1,17},{... | collective-permute-start | bytes 835592 | tf_op jit(solution)/shard_map/ppermute | solution.py:45
  193.4 15.5 %collective-permute-start.39 = (bf16[512,256]{1,0:T(8,128)(2,1)S(1)}, bf16[512,256]{1,0:T(8,128)(2,1)S(1)}, u32[]{:S(2)}, u32[]{:S(2)}) collective-permute-start(bf16[512,256]{1,0:T(8,128)(2,1)S(1)} %fusion.12.refs_0_), channel_id=1, source_target_pairs={{0,2},{1,3},{2,0},{3,1},{4,6},{5,7},{6,4},{7,5},{8,10},{9,11},{10,... | collective-permute-start | bytes 786440 | tf_op jit(solution)/shard_map/ppermute | solution.py:61
  208.3 12.9 %collective-permute-start.41 = (bf16[512,256]{1,0:T(8,128)(2,1)S(1)}, bf16[512,256]{1,0:T(8,128)(2,1)S(1)}, u32[]{:S(2)}, u32[]{:S(2)}) collective-permute-start(bf16[512,256]{1,0:T(8,128)(2,1)S(1)} %fusion.12.refs_0_), channel_id=1, source_target_pairs={{0,1},{1,0},{2,3},{3,2},{4,5},{5,4},{6,7},{7,6},{8,9},{9,8},{10,11... | collective-permute-start | bytes 786440 | tf_op jit(solution)/shard_map/ppermute | solution.py:45
  208.4 12.8 %collective-permute-start.42 = (bf16[512,256]{1,0:T(8,128)(2,1)S(1)}, bf16[512,256]{1,0:T(8,128)(2,1)S(1)}, u32[]{:S(2)}, u32[]{:S(2)}) collective-permute-start(bf16[512,256]{1,0:T(8,128)(2,1)S(1)} %collective-permute-done.38.refs_1_), channel_id=1, source_target_pairs={{0,1},{1,0},{2,3},{3,2},{4,5},{5,4},{6,7},{7,6},{8,9},{9,8},{10,11... | collective-permute-start | bytes 786440 | tf_op jit(solution)/shard_map/ppermute | solution.py:45
  208.9 12.4 %collective-permute-start.43 = (bf16[512,256]{1,0:T(8,128)(2,1)S(1)}, bf16[512,256]{1,0:T(8,128)(2,1)S(1)}, u32[]{:S(2)}, u32[]{:S(2)}) collective-permute-start(bf16[512,256]{1,0:T(8,128)(2,1)S(1)} %collective-permute-done.39.refs_2_), channel_id=1, source_target_pairs={{0,1},{1,0},{2,3},{3,2},{4,5},{5,4},{6,7},{7,6},{8,9},{9,8},{10,11... | collective-permute-start | bytes 786440 | tf_op jit(solution)/shard_map/ppermute | solution.py:45
  (55 other events, 374.9 us)

commit v5 on v4

--- a/solution.py
+++ b/solution.py
@@ -191,20 +191,27 @@
     ones3 = jnp.where(lane == 0, 1.0, 0.0).astype(BF16)
     ones1 = jnp.where(lane == 1, 1.0, 0.0).astype(BF16)
     size = LANES // near
-    for k, target in enumerate(targets):
-        left = grad[here, columns_of(where_ref[0], k)]
-        left1 = grad1[here, columns_of(where_ref[0], k)]
-
-        def put(first, count, values, target=target):
+
+    def ordered(values):
+        return jnp.concatenate(
+            [values[here, columns_of(where_ref[0], k)] for k in range(len(targets))], 1
+        )
+
+    def put(first, values):
+        count = values.shape[1]
+        for k, target in enumerate(targets):
             for j in range(near):
                 start = pl.multiple_of((where_ref[1] ^ j) * size, size)
+                row = k * LANES + j * size
                 target[pl.ds(start, size), first : first + count] = values[
-                    j * size : j * size + size, :
+                    row : row + size, :
                 ].astype(target.dtype)
 
-        put(0, 3 * depth, dot_tn(left, deep[here, :]))
-        put(3 * depth, depth, dot_tn(left1, deep1[here, :]))
-        put(4 * depth, LANES, dot_tn(left, ones3) + dot_tn(left1, ones1))
+    left, left1 = ordered(grad), ordered(grad1)
+    for first in range(0, 3 * depth, depth):
+        put(first, dot_tn(left, deep[here, first : first + depth]))
+    put(3 * depth, dot_tn(left1, deep1[here, :]))
+    put(4 * depth, dot_tn(left, ones3) + dot_tn(left1, ones1))
 
 
 def input_grad(taps, weight, here, depth):
@@ -217,7 +224,7 @@
 
 def decoder_kernel(
     me_ref, quant, c0, c1, c2, c3, w0, w1, w2, w3, prev_ok, next_ok,
-    grad_ref, g0, g1, g2, g3, cot, weight, act, act3, low, mid, *, near,
+    grad_ref, g0, g2, sent, cot, weight, act, act3, low, mid, *, near,
 ):
     me = me_ref[0]
     rows, depth = quant.shape
@@ -241,7 +248,8 @@
         grad = grad.astype(BF16)
         low[here, :] = grad
         act[8 + r : 8 + r + step, :] = grad.astype(F32)
-    weight_grads(me_ref, near, (g0, g1, g2, g3), low, act3, cot, mid, own, depth)
+    targets = (g0, sent.at[0], g2, sent.at[1])
+    weight_grads(me_ref, near, targets, low, act3, cot, mid, own, depth)
     taps_into(act, act3, prev_ok, next_ok, rows, depth)
     for r in range(0, rows, step):
         here = slice(r, r + step)
@@ -252,7 +260,7 @@
 
 def quantize_back_kernel(
     group_ref, grad_ref, prob_ref, first_ref, second_ref, books, usage,
-    out_ref, kept_ref, sent_ref, mark_ref, total, columns, *, own, levels,
+    out_ref, table_ref, mark_ref, total, columns, *, own, levels,
 ):
     step = pl.program_id(0)
     rows = grad_ref.shape[0]
@@ -279,17 +287,17 @@
         grad_scores = (prob * (grad_prob - inner)).astype(BF16)
         through = dot_nn(grad_scores, book) * scale
         grad_remain = through if grad_remain is None else grad_remain + through
-        total[level] += dot_tn(picked * mine_low, low) + dot_tn(
-            current * (mine_low * scale), grad_scores
-        )
+        left = jnp.concatenate([picked * mine_low, current * (mine_low * scale)], 0)
+        total[level] += dot_tn(left, jnp.concatenate([low, grad_scores], 0))
         columns[level] += jnp.sum(grad_scores.astype(F32) * mine, axis=0, keepdims=True)
     out_ref[...] = grad_remain.astype(BF16)
 
     @pl.when(step == pl.num_programs(0) - 1)
     def _():
         depth = books.shape[3]
-        row = lax.broadcasted_iota(jnp.int32, (16, kept_ref.shape[2]), 0)
-        for j, table in enumerate((kept_ref, sent_ref)):
+        row = lax.broadcasted_iota(jnp.int32, (16, table_ref.shape[3]), 0)
+        for j in range(levels):
+            table = table_ref.at[j]
             level = group_ref[1] ^ j
             codes = table.shape[2]
             turned = books[0, level].astype(F32).T
@@ -308,7 +316,7 @@
 def encoder_weight_grad_kernel(
     me_ref, grad_mine, grad_other, hidden, mid, f0, f1, f2, f3,
     w0, w1, w2a, w2b, w3a, w3b, prev_ok, next_ok,
-    g0, g1, g2, g3, low, grad_latent, mark, feat, weight, act, act3, *, near,
+    g0, g2, sent, low, grad_latent, mark, feat, weight, act, act3, *, near,
 ):
     mark[...] = jnp.zeros_like(mark)
     me = me_ref[0]
@@ -332,13 +340,15 @@
         here = slice(r, r + step)
         grad = dot_nt(grad_latent[here, :], weight[3 * depth : 4 * depth, :])
         low[here, :] = (grad * elu_slope(hidden[here, :])).astype(BF16)
-    weight_grads(me_ref, near, (g0, g1, g2, g3), low, act3, grad_latent, mid, own, depth)
+    targets = (g0, sent.at[0], g2, sent.at[1])
+    weight_grads(me_ref, near, targets, low, act3, grad_latent, mid, own, depth)
 
 
 def encoder_input_grad_kernel(
     me_ref, low, grad_latent, f0, f1, f2, f3, w0, w1, w2a, w2b, w3a, w3b, prev_ok, next_ok,
-    o0, o1, o2, o3, feat, weight, act, act3,
+    o0, o1, o2, o3, mark, feat, weight, act, act3,
 ):
+    mark[...] = jnp.zeros_like(mark)
     me = me_ref[0]
     rows, depth = low.shape
     own = rows - 2 * HALO
@@ -367,6 +377,94 @@
         first += ref.shape[0]
 
 
+def sum_of(*refs):
+    return functools.reduce(lambda x, y: x + y, [ref[...].astype(F32) for ref in refs])
+
+
+def halve_kernel(where_ref, d0, d1, dx, t0, t1, mine, sent, book_sent, mark):
+    half = mine.shape[0]
+    total = sum_of(d0, d1.at[0], dx)
+    mine[...] = total[:half]
+    sent[...] = total[half:].astype(BF16)
+    book_sent[...] = sum_of(t0.at[1], t1.at[1]).astype(BF16)
+    mark[...] = jnp.zeros_like(mark)
+
+
+def near_kernel(
+    where_ref, t0, t1, bx, d0, d1, core, book_mine, book_sent, dec_mine, dec_sent, passed
+):
+    passed[...] = core[...]
+    for k, out in enumerate((book_mine, book_sent)):
+        out[...] = sum_of(t0.at[0, k], t1.at[0, k], bx.at[k]).astype(out.dtype)
+    total = sum_of(d0, d1)
+    dec_mine[...] = total
+    dec_sent[...] = total.astype(BF16)
+
+
+def spread_kernel(
+    where_ref, b0, b1, e0, e2, core, d0, d1,
+    book_mine, book_sent, enc_mine, enc_near, enc_x, enc_both, dec_mine, dec_sent, mark,
+):
+    half = enc_mine.shape[0]
+    total = sum_of(e0, core.at[0])
+    enc_mine[...] = total[:half]
+    enc_near[...] = total[half:].astype(BF16)
+    total = sum_of(e2, core.at[1])
+    enc_x[...] = total[:half].astype(BF16)
+    enc_both[...] = total[half:].astype(BF16)
+    for mine, sent, total in (
+        (book_mine, book_sent, sum_of(b0, b1)),
+        (dec_mine, dec_sent, sum_of(d0, d1)),
+    ):
+        mine[...] = total
+        sent[...] = total.astype(BF16)
+    mark[...] = jnp.zeros_like(mark)
+
+
+def sum_kernel(
+    where_ref, b0, b1, e0, e1, e2, e3, d0, d1, book_mine, book_sent, enc_mine, enc_sent, dec_sent
+):
+    for mine, sent, total in (
+        (book_mine, book_sent, sum_of(b0, b1)),
+        (enc_mine, enc_sent, sum_of(e0, e1, e2, e3)),
+    ):
+        mine[...] = total
+        sent[...] = total.astype(BF16)
+    dec_sent[...] = sum_of(d0, d1).astype(BF16)
+
+
+def refresh_kernel(where_ref, b0, b1, books, chosen, e0, e1, fresh, enc_mine, enc_sent, *, share):
+    held = sum_of(b0, b1)
+    depth = books.shape[0]
+    ratio = held[depth : depth + 1, :] * share
+    refresh = jax.nn.sigmoid(SHARPNESS * (THRESHOLD - ratio))
+    stepped = books[...] - (STEP_SCALE * share) * held[:depth, :]
+    fresh[...] = ((1.0 - refresh) * stepped + refresh * chosen[...]).T.astype(BF16)
+    total = sum_of(e0, e1)
+    enc_mine[...] = total
+    enc_sent[...] = total.astype(BF16)
+
+
+def join_kernel(where_ref, e0, e1, enc):
+    enc[...] = sum_of(e0, e1).astype(BF16)
+
+
+def unpack_kernel(mask_ref, *refs, block):
+    *parts, conv3, conv1, bias3, bias1, held = refs
+    first = 0
+    for part in parts:
+        for r in range(0, part.shape[0], block):
+            start = pl.multiple_of((first + r) ^ mask_ref[0], block)
+            held[pl.ds(start, block), :] = part[r : r + block, :].astype(F32)
+        first += part.shape[0]
+    count3, count1 = conv3.shape[0], conv1.shape[0]
+    conv3[...] = held[:, 0:count3].T
+    conv1[...] = held[:, count3 : count3 + count1].T
+    biases = held[:, count3 + count1 :].T
+    bias3[...] = biases[0:1, :]
+    bias1[...] = biases[1:2, :]
+
+
 def whole(count, smem_first=False):
     specs = [pl.BlockSpec(memory_space=pltpu.VMEM)] * count
     if smem_first:
@@ -383,6 +481,26 @@
 
 
 PARAMS = pltpu.CompilerParams(vmem_limit_bytes=VMEM_LIMIT)
+LIGHT = pltpu.CompilerParams(vmem_limit_bytes=14 * 1024 * 1024)
+
+
+def tied(kernel, first, count):
+    def without(*refs):
+        kernel(*refs[:first], *refs[first + count :])
+
+    return without
+
+
+def call(kernel, row, inputs, outs, scratch=(), ties=(), price=None, params=None):
+    return pl.pallas_call(
+        tied(kernel, 1 + len(inputs), len(ties)),
+        out_shape=[shaped(*out) for out in outs],
+        in_specs=whole(1 + len(inputs), True) + [pl.BlockSpec(memory_space=pl.ANY)] * len(ties),
+        out_specs=whole(len(outs)),
+        scratch_shapes=[pltpu.VMEM(*buffer) for buffer in scratch],
+        compiler_params=params or LIGHT,
+        cost_estimate=price or cost(0, 2e6),
+    )(row, *inputs, *ties)
 
 
 def body(
@@ -413,7 +531,8 @@
     near = 2 if n_dp % 2 == 0 else n_dp
     near_at = place % near
     far_bits = [near << i for i in range((n_dp // near).bit_length() - 1)]
-    where_row = jnp.stack([me, place % near, side])
+    where_row = jnp.stack([me, near_at, side, place // near])
+    quad = near == 2 and n_dp == 8
 
     def pack(row, conv3, conv1, biases, half):
         total = conv3.shape[0] * conv3.shape[1] + conv1.shape[0] + 32
@@ -423,7 +542,7 @@
             out_shape=shapes,
             in_specs=whole(3 + len(biases), True),
             out_specs=whole(len(shapes)),
-            compiler_params=PARAMS,
+            compiler_params=LIGHT,
             cost_estimate=cost(0, 1e6),
         )(
             row,
@@ -438,7 +557,7 @@
             out_shape=[shaped((rows, cols), BF16)] * 4,
             in_specs=whole(2, True),
             out_specs=whole(4),
-            compiler_params=PARAMS,
+            compiler_params=LIGHT,
             cost_estimate=cost(0, 2e6),
         )(row, values)
 
@@ -478,6 +597,8 @@
     buffer_half = lax.dynamic_slice_in_dim(code_buffer, side * group_dim, group_dim, 1)
     chosen = dot_nn(one_hot.astype(BF16), buffer_half)
     books_own = own_codes(codebooks).astype(F32)
+    if quad:
+        chosen, books_own = chosen.T, books_own.T
 
     at = jnp.arange(cols, dtype=jnp.int32)
     turn = ((at[:, None] ^ (near_at * (cols // near))) == at[None, :]).astype(BF16)
@@ -538,14 +659,16 @@
     )(latent, codebooks, norms)
 
     packed = 4 * depth + LANES
-    grads_shape = tuple(
-        shaped((cols, packed), dtype) for dtype in (F32, BF16, F32, BF16)
+    grads_shape = (
+        shaped((cols, packed), F32),
+        shaped((cols, packed), F32),
+        shaped((2, cols, packed), BF16),
     )
     grad_quant, *dec_grads = pl.pallas_call(
         functools.partial(decoder_kernel, near=near),
         out_shape=(shaped((rows, depth), F32),) + grads_shape,
         in_specs=whole(12, True),
-        out_specs=tuple(whole(5)),
+        out_specs=tuple(whole(4)),
         scratch_shapes=[
             pltpu.VMEM((rows, depth), BF16),
             pltpu.VMEM((4 * depth + 32, depth), BF16),
@@ -558,11 +681,11 @@
         cost_estimate=cost(24 * rows * depth * depth, 20e6),
     )(where_row, quant, *cot, *dec, prev_ok, next_ok)
 
-    table_shape = (near, group_dim + 16, num_codes // near)
-
-    def quantize_back(group):
+    table_shape = (levels, near, group_dim + 16, num_codes // near)
+
+    def quantize_back(group, *ties):
         return pl.pallas_call(
-            functools.partial(quantize_back_kernel, own=own, levels=levels),
+            tied(functools.partial(quantize_back_kernel, own=own, levels=levels), 7, len(ties)),
             grid_spec=pltpu.PrefetchScalarGridSpec(
                 num_scalar_prefetch=1,
                 grid=(3,),
@@ -573,11 +696,11 @@
                     pl.BlockSpec((levels - 1, step, group_dim), lambda i, g: (0, i, g[0])),
                     pl.BlockSpec((1, levels, num_codes, group_dim), lambda i, g: (g[0], 0, 0, 0)),
                     pl.BlockSpec((1, levels, 1, num_codes), lambda i, g: (g[0], 0, 0, 0)),
-                ],
+                ]
+                + [pl.BlockSpec(memory_space=pl.ANY)] * len(ties),
                 out_specs=(
                     pl.BlockSpec((step, group_dim), lambda i, g: (i, 0)),
-                    pl.BlockSpec(table_shape, lambda i, g: (0, 0, 0)),
-                    pl.BlockSpec(table_shape, lambda i, g: (0, 0, 0)),
+                    pl.BlockSpec(table_shape, lambda i, g: (0, 0, 0, 0)),
                     pl.BlockSpec((8, LANES), lambda i, g: (0, 0)),
                 ),
                 scratch_shapes=[
@@ -588,12 +711,52 @@
             out_shape=(
                 shaped((rows, group_dim), BF16),
                 shaped(table_shape, BF16),
-                shaped(table_shape, BF16),
                 shaped((8, LANES), F32),
             ),
             compiler_params=PARAMS,
             cost_estimate=cost(16 * rows * num_codes * group_dim, 15e6),
-        )(jnp.stack([group, level_side, near_at]), grad_quant, prob, latent, second, codebooks, usage)
+        )(
+            jnp.stack([group, level_side, near_at]),
+            grad_quant, prob, latent, second, codebooks, usage, *ties,
+        )
+
+    taken = [((rows, depth), BF16), ((4 * depth + 32, depth), BF16)]
+    taken += [((rows + 16, depth), F32), ((rows, 3 * depth), BF16)]
+
+    def encoder_weight_grads(*ties):
+        return call(
+            functools.partial(encoder_weight_grad_kernel, near=near),
+            where_row,
+            [grad_mine, grad_other, hidden_enc, act_mid, *feat, *enc, prev_ok, next_ok],
+            [(out.shape, out.dtype) for out in grads_shape]
+            + [((rows, depth), BF16)] * 2 + [((8, LANES), F32)],
+            taken,
+            ties,
+            cost(12 * rows * depth * depth, 20e6),
+            PARAMS,
+        )
+
+    def encoder_input_grads(low, grad_latent, *ties):
+        return call(
+            encoder_input_grad_kernel,
+            where_row,
+            [low, grad_latent, *feat, *enc, prev_ok, next_ok],
+            [((own, cols), BF16)] * 4 + [((8, LANES), F32)],
+            taken,
+            ties,
+            cost(6 * rows * depth * depth, 10e6),
+            PARAMS,
+        )
+
+    def put(mask, block, total, pieces, ties=()):
+        return call(
+            functools.partial(place_kernel, block=block),
+            mask.reshape(1),
+            pieces,
+            [((total, pieces[0].shape[1]), F32)],
+            ties=ties,
+            price=cost(0, 8 * total * pieces[0].shape[1]),
+        )[0]
 
     def gather_near(block):
         return jnp.concatenate([block] + [swap(block, "dp", k) for k in range(1, near)], 0)
@@ -606,56 +769,118 @@
             flat = flat[len(group) :]
         return out
 
-    grad_other, kept_other, sent_other, mark = quantize_back(1 - side)
-    dec_1g, dec_3g = swap(dec_grads[1], "mp", 1), swap(dec_grads[3], "mp", 1)
-    dec_send = low_sum(dec_grads[2], dec_3g).astype(BF16)
-
-    (mine, _), (dec_send,) = stage([side, mark], [dec_send])
+    grad_other, table_other, mark = quantize_back(1 - side)
+    dec_0, dec_2, dec_send = dec_grads
+    dec_core = swap(dec_send, "mp", 1)
+    dec_send = low_sum(dec_2, dec_core[1]).astype(BF16)
     dec_x = swap(dec_send, "mp", 2)
-    kept_got, sent_got = swap(kept_other, "mp", 1), swap(sent_other, "mp", 1)
-    grad_mine, kept_mine, sent_mine, mark = quantize_back(mine)
-    book_send = low_sum(sent_mine, sent_got).astype(BF16)
-    dec_mine, *dec_send = parts_of(low_sum(dec_grads[0], dec_1g, dec_x), near)
+    table_got = swap(table_other, "mp", 1)
+    grad_mine, table_mine, mark = quantize_back(side, mark, dec_send)
+
+    if quad:
+        packed_half, table = (cols // 2, packed), table_shape[2:]
+        mark_shape = ((8, LANES), F32)
+        dec_mine, dec_send, book_send, mark = call(
+            halve_kernel,
+            where_row,
+            [dec_0, dec_core, dec_x, table_mine, table_got],
+            [(packed_half, F32), (packed_half, BF16), (table_shape[1:], BF16), mark_shape],
+        )
+        book_x, dec_got = swap(book_send, "mp", 2), swap(dec_send, "dp", 1)
+        enc_0, enc_2, enc_send, low, grad_latent, mark = encoder_weight_grads(mark)
+        book_mine, book_send, dec_mine, dec_send, enc_send = call(
+            near_kernel,
+            where_row,
+            [table_mine, table_got, book_x, dec_mine, dec_got, enc_send],
+            [(table, F32), (table, BF16), (packed_half, F32), (packed_half, BF16)]
+            + [((2, cols, packed), BF16)],
+            ties=[mark],
+        )
+        enc_core = swap(enc_send, "mp", 1)
+        book_got, dec_got = swap(book_send, "dp", 1), swap(dec_send, "dp", 2)
+        book_mine, book_send, enc_mine, enc_near, enc_x, enc_both, dec_mine, dec_send, mark = call(
+            spread_kernel,
+            where_row,
+            [book_mine, book_got, enc_0, enc_2, enc_core, dec_mine, dec_got],
+            [(table, F32), (table, BF16), (packed_half, F32)] + [(packed_half, BF16)] * 3
+            + [(packed_half, F32), (packed_half, BF16), mark_shape],
+        )
+        enc_got = [swap(enc_near, "dp", 1), swap(enc_x, "mp", 2), swap_both(enc_both, 1, 2)]
+        book_got, dec_got = swap(book_send, "dp", 2), swap(dec_send, "dp", 4)
+        *outs, mark = encoder_input_grads(low, grad_latent, mark)
+        book_mine, book_send, enc_mine, enc_send, dec_send = call(
+            sum_kernel,
+            where_row,
+            [book_mine, book_got, enc_mine, *enc_got, dec_mine, dec_got],
+            [(table, F32), (table, BF16), (packed_half, F32)] + [(packed_half, BF16)] * 2,
+            ties=[mark],
+        )
+        book_got, enc_got = swap(book_send, "dp", 4), swap(enc_send, "dp", 2)
+        dec_got = swap(dec_send, "dp", 1)
+        outs = [outs[0]] + [swap(outs[k], "mp", k) for k in (1, 2, 3)]
+        grad_features = put(me * own, own, frames, outs)
+        fresh, enc_mine, enc_send = call(
+            functools.partial(refresh_kernel, share=num_codes / (frames * n_dp)),
+            where_row,
+            [book_mine, book_got, books_own, chosen, enc_mine, enc_got],
+            [((codes, group_dim), BF16), (packed_half, F32), (packed_half, BF16)],
+            ties=[grad_features],
+        )
+        fresh = [fresh, swap(fresh, "dp", 1), swap(fresh, "mp", 2), swap_both(fresh, 1, 2)]
+        enc_got = swap(enc_send, "dp", 4)
+        (enc_send,) = call(join_kernel, where_row, [enc_mine, enc_got], [(packed_half, BF16)])
+        enc_got = swap(enc_send, "dp", 1)
+        fresh = fresh + [swap(piece, "mp", 1) for piece in fresh]
+        mask = (side * levels + level_side) * num_codes + first
+        new_codebooks = put(mask, codes, groups * levels * num_codes, fresh)
+
+        def unpack(mask, *parts):
+            conv3, conv1, bias3, bias1 = call(
+                functools.partial(unpack_kernel, block=cols // 2),
+                mask.reshape(1),
+                parts,
+                [((3 * depth, cols), F32), ((depth, cols), F32)] + [((1, cols), F32)] * 2,
+                [((cols, packed), F32)],
+            )
+            return (conv3.reshape(3, depth, cols), bias3[0], conv1, bias1[0])
+
+        half = near_at * (cols // 2)
+        return (
+            grad_features,
+            *unpack(half, enc_send, enc_got),
+            *unpack(half, dec_send, dec_got),
+            new_codebooks.reshape(codebooks.shape),
+        )
+
+    book_send = low_sum(table_mine[1], table_got[1]).astype(BF16)
+    dec_mine, *dec_send = parts_of(low_sum(dec_0, dec_core[0], dec_x), near)
     dec_send = [piece.astype(BF16) for piece in dec_send]
 
-    (row, _), (book_send,), dec_send = stage([where_row, mark], [book_send], dec_send)
+    (mark,), (book_send,), dec_send = stage([mark], [book_send], dec_send)
     book_x = swap(book_send, "mp", 2)
     dec_got = [swap(piece, "dp", k + 1) for k, piece in enumerate(dec_send)]
-    *enc_grads, low, grad_latent, mark = pl.pallas_call(
-        functools.partial(encoder_weight_grad_kernel, near=near),
-        out_shape=grads_shape + (shaped((rows, depth), BF16),) * 2 + (shaped((8, LANES), F32),),
-        in_specs=whole(17, True),
-        out_specs=tuple(whole(7)),
-        scratch_shapes=[
-            pltpu.VMEM((rows, depth), BF16),
-            pltpu.VMEM((4 * depth + 32, depth), BF16),
-            pltpu.VMEM((rows + 16, depth), F32),
-            pltpu.VMEM((rows, 3 * depth), BF16),
-        ],
-        compiler_params=PARAMS,
-        cost_estimate=cost(12 * rows * depth * depth, 20e6),
-    )(row, grad_mine, grad_other, hidden_enc, act_mid, *feat, *enc, prev_ok, next_ok)
+    enc_0, enc_2, enc_send, low, grad_latent, mark = encoder_weight_grads(mark)
 
     def book_sum(k):
-        return low_sum(kept_mine[k], kept_got[k], book_x[k])
+        return low_sum(table_mine[0, k], table_got[0, k], book_x[k])
 
     def pair_sum(held, sent, bit):
         return held + swap(sent, "dp", bit).astype(F32)
 
     dec_held = low_sum(dec_mine, *dec_got)
-    enc_1g, enc_3g = swap(enc_grads[1], "mp", 1), swap(enc_grads[3], "mp", 1)
+    enc_core = swap(enc_send, "mp", 1)
     book_send, (dec_send, _) = stage(
         [book_sum(k).astype(BF16) for k in range(1, near)], [dec_held.astype(BF16), mark]
     )
     book_got = [swap(piece, "dp", k + 1) for k, piece in enumerate(book_send)]
     dec_held = pair_sum(dec_held, dec_send, far_bits[0])
-    enc_mine, *enc_near = parts_of(low_sum(enc_grads[0], enc_1g), near)
+    enc_mine, *enc_near = parts_of(low_sum(enc_0, enc_core[0]), near)
     enc_near = [piece.astype(BF16) for piece in enc_near]
-    enc_far = parts_of(low_sum(enc_grads[2], enc_3g).astype(BF16), near)
+    enc_far = parts_of(low_sum(enc_2, enc_core[1]).astype(BF16), near)
     book_held = low_sum(book_sum(0), *book_got)
 
-    (row,), enc_near, enc_far, (book_send, dec_send) = stage(
-        [where_row], enc_near, enc_far, [book_held.astype(BF16), dec_held.astype(BF16)]
+    (mark,), enc_near, enc_far, (book_send, dec_send) = stage(
+        [mark], enc_near, enc_far, [book_held.astype(BF16), dec_held.astype(BF16)]
     )
     enc_got = [swap(piece, "dp", k + 1) for k, piece in enumerate(enc_near)] + [
         swap_both(piece, k, 2) for k, piece in enumerate(enc_far)
@@ -664,20 +889,7 @@
     dec_held = pair_sum(dec_held, dec_send, far_bits[1])
     for bit in far_bits[2:]:
         dec_held = pair_sum(dec_held, dec_held.astype(BF16), bit)
-    outs = pl.pallas_call(
-        encoder_input_grad_kernel,
-        out_shape=(shaped((own, cols), BF16),) * 4,
-        in_specs=whole(15, True),
-        out_specs=tuple(whole(4)),
-        scratch_shapes=[
-            pltpu.VMEM((rows, depth), BF16),
-            pltpu.VMEM((4 * depth + 32, depth), BF16),
-            pltpu.VMEM((rows + 16, depth), F32),
-            pltpu.VMEM((rows, 3 * depth), BF16),
-        ],
-        compiler_params=PARAMS,
-        cost_estimate=cost(6 * rows * depth * depth, 10e6),
-    )(row, low, grad_latent, *feat, *enc, prev_ok, next_ok)
+    *outs, _ = encoder_input_grads(low, grad_latent, mark)
 
     enc_held = low_sum(enc_mine, *enc_got)
     (book_send, dec_send, enc_send), outs_send = stage(
@@ -697,29 +909,18 @@
     stepped = books_own - (STEP_SCALE * share) * book_held[:, :group_dim]
     fresh = ((1.0 - refresh) * stepped + refresh * chosen).astype(BF16)
 
-    (fresh, enc_send), _ = stage([fresh, enc_held.astype(BF16)], [])
+    ((fresh, enc_send),) = stage([fresh, enc_held.astype(BF16)])
     enc_held = pair_sum(enc_held, enc_send, far_bits[1])
     for bit in far_bits[2:]:
         enc_held = pair_sum(enc_held, enc_held.astype(BF16), bit)
     fresh = [
         swap_both(fresh, k, bits) if k or bits else fresh for bits in (0, 2) for k in range(near)
     ]
-    enc_turn = enc_held.astype(BF16)
-    enc_held = gather_near(enc_turn)
+    enc_held = gather_near(enc_held.astype(BF16))
     fresh = fresh + [swap(part, "mp", 1) for part in fresh]
 
-    def put(mask, block, total, *pieces):
-        return pl.pallas_call(
-            functools.partial(place_kernel, block=block),
-            out_shape=shaped((total, pieces[0].shape[1]), F32),
-            in_specs=whole(1 + len(pieces), True),
-            out_specs=whole(1)[0],
-            compiler_params=PARAMS,
-            cost_estimate=cost(0, 8 * total * pieces[0].shape[1]),
-        )(mask.reshape(1), *pieces)
-
     mask = (side * levels + level_side) * num_codes + first
-    new_codebooks = put(mask, codes, groups * levels * num_codes, *fresh)
+    new_codebooks = put(mask, codes, groups * levels * num_codes, fresh)
 
     def unpack(held):
         biases = dot_tn(held[:, 4 * depth :], turn)
@@ -730,7 +931,7 @@
             biases[1],
         )
 
-    grad_features = put(after(me * own, enc_turn), own, frames, *outs)
+    grad_features = put(me * own, own, frames, outs)
 
     return (
         grad_features,

time: 229 us -> 209 us (0.913)
  other arithmetic: 19.1 us -> 5.29 us
  matrix products: 6.05 us -> 0.68 us
  Pallas kernels: 105 us -> 101 us
  starting transfers between devices: 34.5 us -> 36.8 us
    convert_element_type x13 -> x1, other arithmetic: 11.1 us -> 0.1 us  [body(): dec_send = low_sum(dec_2, dec_core[1]).astype(BF16)]
    unnamed x89 -> x99, local copies, waits for them, and re-layouts: 8.13 us -> 14.5 us
    ppermute x5 -> x2, waiting for transfers between devices: 7.24 us -> 2 us  [swap_both(): return lax.ppermute(values, ('dp', 'mp'), pairs)]
    ppermute x40, starting transfers between devices: 27.8 us -> 33 us  [swap(): return lax.ppermute(values, axis, [(i, i ^ bits) for i in range(size)])]
    dot_general x6 -> x0, matrix products: 4.75 us -> none  [dot_tn(): lax.dot_general(left, right, (((0,), (0,)), ((), ())), preferred_element_...]
    ppermute x40, waiting for transfers between devices: 40.1 us -> 44.8 us  [swap(): return lax.ppermute(values, axis, [(i, i ^ bits) for i in range(size)])]
    slice x5 -> x0, local copies, waits for them, and re-layouts: 3.55 us -> none  [the longest x3 2.67 us: parts_of(): return [total[k * size:k * size + size] for k in range(count)]]
    add x2 -> x0, other arithmetic: 3.36 us -> none  [low_sum(): return functools.reduce(lambda x, y: x + y, [t.astype(F32) for t in terms])]
  transfers between devices with their start and end apart: 45 -> 42, of which waited for: 10 -> 15; matrix products, arithmetic and copies ran while one was open for 13% -> 4% of each run, Pallas kernels for 39% -> 40%
where the time goes in v5:
time: 209 us
  Pallas kernels  101 us (48%)
  waiting for transfers between devices  46.8 us (22%)
  starting transfers between devices  36.8 us (18%)
  local copies, waits for them, and re-layouts  16.9 us (8%)
  other arithmetic  5.29 us (3%)
    ppermute x40, waiting for transfers between devices, swap(): return lax.ppermute(values, axis, [(i, i ^ bits) for i in range(size)])  44.8 us
    pallas_call x2, Pallas kernels, quantize_back(): pl.pallas_call(tied(functools.partial(quantize_back_kernel, own=own, leve...  36.3 us
    ppermute x40, starting transfers between devices, swap(): return lax.ppermute(values, axis, [(i, i ^ bits) for i in range(size)])  33 us
    pallas_call x12, Pallas kernels, call(): pl.pallas_call(tied(kernel, 1 + len(inputs), len(ties)), out_shape=[shape...  28.5 us
    unnamed x99, local copies, waits for them, and re-layouts  14.5 us
    pallas_call x1, Pallas kernels, body(): pl.pallas_call(functools.partial(quantize_kernel, own=own), grid=(3,), ou...  13.1 us
    pallas_call x1, Pallas kernels, body(): pl.pallas_call(functools.partial(decoder_kernel, near=near), out_shape=(s...  12.3 us
    pallas_call x1, Pallas kernels, body(): pl.pallas_call(encoder_kernel, out_shape=(shaped((rows, depth), F32), sha...  8.12 us
  transfers between devices with their start and end apart: 42, of which 15 were waited for; matrix products, arithmetic and copies ran while one was open for 4% of the time, Pallas kernels for 40%

profile of v5, /device:TPU:0, one launch (start us, length us, event | category | flops | bytes accessed | tf_op | source)
XLA Modules:
  0.0 209.4 jit_solution(7557275318928106953)
XLA Ops:
  4.6 3.0 %collective-permute-start.4 = (bf16[1040,128]{1,0:T(8,128)(2,1)S(1)}, bf16[1040,128]{1,0:T(8,128)(2,1)}, u32[]{:S(2)}, u32[]{:S(2)}) collective-permute-start(bf16[1040,128]{1,0:T(8,128)(2,1)S(1)} %get-tuple-element.91), channel_id=1, source_target_pairs={{0,2},{1,3},{2,0},{3,1},{4,6},{5,7},{6,4},{7,5},{8,10},{9,11},{10,... | collective-permute-start | bytes 798728 | tf_op jit(solution)/shard_map/ppermute | solution.py:45
  11.1 1.7 collective-permute-start.2
  15.7 2.2 %multiply_reduce_fusion = f32[2,2,1024]{2,1,0:T(2,128)S(1)} fusion(bf16[2,2,1024,256]{3,2,1,0:T(8,128)(2,1)} %refs_5_.3), kind=kLoop, calls=%fused_computation | loop fusion | flops 3141632 | bytes 2113536 | tf_op jit(solution)/shard_map/reduce_sum | solution.py:585
  19.4 1.5 collective-permute-start.5
  22.3 3.3 %collective-permute-done.2.f3.refs_8_.refs_6_ = bf16[1056,128]{1,0:T(8,128)(2,1)} collective-permute-done((bf16[1056,128]{1,0:T(8,128)(2,1)}, bf16[1056,128]{1,0:T(8,128)(2,1)}, u32[]{:S(2)}, u32[]{:S(2)}) %collective-permute-start.2) | collective-permute-done | bytes 270368 | tf_op jit(solution)/shard_map/ppermute | solution.py:45
  30.5 8.1 %shard_map.208 = (f32[1056,512]{1,0:T(8,128)}, bf16[1056,512]{1,0:T(8,128)(2,1)}, bf16[1056,512]{1,0:T(8,128)(2,1)}) custom-call(s32[4]{0:T(128)} %copy-done.21, bf16[1056,128]{1,0:T(8,128)(2,1)} %copy-done.15, bf16[1056,128]{1,0:T(8,128)(2,1)} %copy-done.35, bf16[1056,128]{1,0:T(8,128)(2,1)} %collective-permute-done.1.f2.refs_7_.refs_5_, ...), custom_call_target="tpu_custom_call" | custom-call | flops 2214592512 | bytes 12000000 | tf_op jit(solution)/shard_map/pallas_call | solution.py:612
  41.9 13.1 %shard_map.209 = (bf16[1056,512]{1,0:T(8,128)(2,1)}, f32[2,2,1,1024]{3,2,1,0:T(1,128)}, bf16[2,2,1056,1024]{3,2,1,0:T(8,128)(2,1)}, bf16[1,1056,512]{2,1,0:T(8,128)(2,1)}) custom-call(bf16[1056,512]{1,0:T(8,128)(2,1)} %get-tuple-element.98.latent_ref.refs_3_, bf16[2,2,1024,256]{3,2,1,0:T(8,128)(2,1)} %refs_5_.3, f32[2,2,1,1024]{3,2,1,0:T(1,128)} %mul.46.norms), custom_call_target="tpu_custom_call" | custom-call | flops 4429185024 | bytes 30000000 | tf_op jit(solution)/shard_map/pallas_call | solution.py:637
  56.3 12.3 %shard_map.210 = (f32[1056,512]{1,0:T(8,128)}, f32[128,2176]{1,0:T(8,128)}, f32[128,2176]{1,0:T(8,128)}, bf16[2,128,2176]{2,1,0:T(8,128)(2,1)}) custom-call(s32[4]{0:T(128)} %copy-done.21, bf16[1056,512]{1,0:T(8,128)(2,1)} %get-tuple-element.99.quant, bf16[1056,128]{1,0:T(8,128)(2,1)} %copy-done.31, bf16[1056,128]{1,0:T(8,128)(2,1)} %copy-done.42, ...), custom_call_target="tpu_custom_call" | custom-call | flops 6643777536 | bytes 20000000 | tf_op jit(solution)/shard_map/pallas_call | solution.py:667
  70.0 24.5 %shard_map.211 = (bf16[1056,256]{1,0:T(8,128)(2,1)}, bf16[2,2,272,512]{3,2,1,0:T(8,128)(2,1)}, f32[8,128]{1,0:T(8,128)}) custom-call(s32[3]{0:T(128)} %add_add_fusion.1.refs_0_, f32[1056,512]{1,0:T(8,128)} %get-tuple-element.107.refs_1_, bf16[2,2,1056,1024]{3,2,1,0:T(8,128)(2,1)} %get-tuple-element.108.refs_2_, ...), custom_call_target="tpu_custom_call" | custom-call | flops 4429185024 | bytes 15000000 | tf_op jit(solution)/shard_map/pallas_call | solution.py:687
  96.5 11.8 %shard_map.212 = (bf16[1056,256]{1,0:T(8,128)(2,1)}, bf16[2,2,272,512]{3,2,1,0:T(8,128)(2,1)}, f32[8,128]{1,0:T(8,128)}) custom-call(s32[3]{0:T(128)} %add_add_fusion.refs_0_, f32[1056,512]{1,0:T(8,128)} %get-tuple-element.107.refs_1_, bf16[2,2,1056,1024]{3,2,1,0:T(8,128)(2,1)} %get-tuple-element.108.refs_2_, ...), custom_call_target="tpu_custom_call" | custom-call | flops 4429185024 | bytes 15000000 | tf_op jit(solution)/shard_map/pallas_call | solution.py:687
  108.2 1.6 collective-permute-done.15.refs_3_
  113.0 1.9 collective-permute-start.18
  115.0 10.6 %shard_map.214 = (f32[128,2176]{1,0:T(8,128)}, f32[128,2176]{1,0:T(8,128)}, bf16[2,128,2176]{2,1,0:T(8,128)(2,1)}, bf16[1056,512]{1,0:T(8,128)(2,1)}, bf16[1056,512]{1,0:T(8,128)(2,1)}, /*index=5*/f32[8,128]{1,0:T(8,128)}) custom-call(s32[4]{0:T(128)} %copy-done.21, bf16[1056,256]{1,0:T(8,128)(2,1)} %get-tuple-element.114.refs_1_, ...), custom_call_target="tpu_custom_call" | custom-call | flops 3321888768 | bytes 20000000 | tf_op jit(solution)/shard_map/pallas_call | solution.py:495
  129.1 1.6 collective-permute-start.19
  130.7 1.6 collective-permute-start.21
  132.3 5.9 %collective-permute-done.19.refs_2_ = bf16[272,512]{1,0:T(8,128)(2,1)S(1)} collective-permute-done((bf16[272,512]{1,0:T(8,128)(2,1)S(1)}, bf16[272,512]{1,0:T(8,128)(2,1)S(1)}, u32[]{:S(2)}, u32[]{:S(2)}) %collective-permute-start.19) | collective-permute-done | bytes 278560 | tf_op jit(solution)/shard_map/ppermute | solution.py:45
  140.3 1.6 collective-permute-start.25
  143.9 1.5 collective-permute-start.28
  145.5 2.6 %collective-permute-start.29 = (bf16[64,2176]{1,0:T(8,128)(2,1)S(1)}, bf16[64,2176]{1,0:T(8,128)(2,1)S(1)}, u32[]{:S(2)}, u32[]{:S(2)}) collective-permute-start(bf16[64,2176]{1,0:T(8,128)(2,1)S(1)} %get-tuple-element.148), channel_id=1, source_target_pairs={{0,16},{4,20},{8,24},{12,28},{16,0},{20,4},{24,8},{28,12},{1,17},{... | collective-permute-start | bytes 835592 | tf_op jit(solution)/shard_map/ppermute | solution.py:45
  148.1 6.7 %shard_map.217 = (bf16[1024,128]{1,0:T(8,128)(2,1)}, bf16[1024,128]{1,0:T(8,128)(2,1)}, bf16[1024,128]{1,0:T(8,128)(2,1)}, bf16[1024,128]{1,0:T(8,128)(2,1)}, f32[8,128]{1,0:T(8,128)}) custom-call(s32[4]{0:T(128)} %copy-done.21, bf16[1056,512]{1,0:T(8,128)(2,1)} %get-tuple-element.122.refs_1_, bf16[1056,512]{1,0:T(8,128)(2,1)} %get-tuple-element.123.refs_2_, ...), custom_call_target="tpu_custom_call" | custom-call | flops 1660944384 | bytes 10000000 | tf_op jit(solution)/shard_map/pallas_call | solution.py:495
  154.8 2.0 collective-permute-done.28.refs_6_
  156.8 2.4 %collective-permute-done.29.refs_8_ = bf16[64,2176]{1,0:T(8,128)(2,1)S(1)} collective-permute-done((bf16[64,2176]{1,0:T(8,128)(2,1)S(1)}, bf16[64,2176]{1,0:T(8,128)(2,1)S(1)}, u32[]{:S(2)}, u32[]{:S(2)}) %collective-permute-start.29) | collective-permute-done | bytes 278560 | tf_op jit(solution)/shard_map/ppermute | solution.py:45
  160.9 2.9 %collective-permute-start.31 = (bf16[64,2176]{1,0:T(8,128)(2,1)S(1)}, bf16[64,2176]{1,0:T(8,128)(2,1)S(1)}, u32[]{:S(2)}, u32[]{:S(2)}) collective-permute-start(bf16[64,2176]{1,0:T(8,128)(2,1)S(1)} %get-tuple-element.153), channel_id=1, source_target_pairs={{0,8},{4,12},{8,0},{12,4},{16,24},{20,28},{24,16},{28,20},{1,9},{5... | collective-permute-start | bytes 835592 | tf_op jit(solution)/shard_map/ppermute | solution.py:45
  163.8 1.5 collective-permute-start.23
  165.7 7.3 %collective-permute-done.23.refs_3_ = bf16[1024,128]{1,0:T(8,128)(2,1)S(1)} collective-permute-done((bf16[1024,128]{1,0:T(8,128)(2,1)S(1)}, bf16[1024,128]{1,0:T(8,128)(2,1)S(1)}, u32[]{:S(2)}, u32[]{:S(2)}) %collective-permute-start.23) | collective-permute-done | bytes 262176 | tf_op jit(solution)/shard_map/ppermute | solution.py:45
  173.0 4.7 %collective-permute-done.24.refs_4_ = bf16[1024,128]{1,0:T(8,128)(2,1)S(1)} collective-permute-done((bf16[1024,128]{1,0:T(8,128)(2,1)S(1)}, bf16[1024,128]{1,0:T(8,128)(2,1)S(1)}, u32[]{:S(2)}, u32[]{:S(2)}) %collective-permute-start.24) | collective-permute-done | bytes 262176 | tf_op jit(solution)/shard_map/ppermute | solution.py:45
  177.7 1.5 shard_map.218.refs_7_
  179.1 1.6 copy-done.2
  182.3 2.3 %collective-permute-start.37 = (bf16[512,256]{1,0:T(8,128)(2,1)S(1)}, bf16[512,256]{1,0:T(8,128)(2,1)S(1)}, u32[]{:S(2)}, u32[]{:S(2)}) collective-permute-start(bf16[512,256]{1,0:T(8,128)(2,1)S(1)} %get-tuple-element.165.refs_1_), channel_id=1, source_target_pairs={{0,6},{1,7},{2,4},{3,5},{4,2},{5,3},{6,0},{7,1},{8,14},{9,15},{10,... | collective-permute-start | bytes 786440 | tf_op jit(solution)/shard_map/ppermute | solution.py:61
  185.8 11.0 %collective-permute-done.32.refs_2_ = bf16[64,2176]{1,0:T(8,128)(2,1)S(1)} collective-permute-done((bf16[64,2176]{1,0:T(8,128)(2,1)S(1)}, bf16[64,2176]{1,0:T(8,128)(2,1)S(1)}, u32[]{:S(2)}, u32[]{:S(2)}) %collective-permute-start.32) | collective-permute-done | bytes 278560 | tf_op jit(solution)/shard_map/ppermute | solution.py:45
  198.7 3.7 %collective-permute-done.35.refs_2_ = bf16[512,256]{1,0:T(8,128)(2,1)S(1)} collective-permute-done((bf16[512,256]{1,0:T(8,128)(2,1)S(1)}, bf16[512,256]{1,0:T(8,128)(2,1)S(1)}, u32[]{:S(2)}, u32[]{:S(2)}) %collective-permute-start.35) | collective-permute-done | bytes 262176 | tf_op jit(solution)/shard_map/ppermute | solution.py:45
  205.6 2.3 %shard_map.224 = f32[4096,256]{1,0:T(8,128)} custom-call(s32[1]{0:T(128)} %bitcast.25.refs_0_, bf16[512,256]{1,0:T(8,128)(2,1)S(1)} %get-tuple-element.165.refs_1_, bf16[512,256]{1,0:T(8,128)(2,1)S(1)} %collective-permute-done.35.refs_2_, bf16[512,256]{1,0:T(8,128)(2,1)S(1)} %collective-permute-done.36.refs_3_, ...), custom_call_target="tpu_custom_call" | custom-call | bytes 8388608 | tf_op jit(solution)/shard_map/pallas_call | solution.py:495
  (189 shorter events, 47.7 us)
Async XLA Ops:
  4.6 14.8 %collective-permute-start.4 = (bf16[1040,128]{1,0:T(8,128)(2,1)S(1)}, bf16[1040,128]{1,0:T(8,128)(2,1)}, u32[]{:S(2)}, u32[]{:S(2)}) collective-permute-start(bf16[1040,128]{1,0:T(8,128)(2,1)S(1)} %get-tuple-element.91), channel_id=1, source_target_pairs={{0,2},{1,3},{2,0},{3,1},{4,6},{5,7},{6,4},{7,5},{8,10},{9,11},{10,... | collective-permute-start | bytes 798728 | tf_op jit(solution)/shard_map/ppermute | solution.py:45
  7.6 21.8 %collective-permute-start.3 = (bf16[2080,128]{1,0:T(8,128)(2,1)S(1)}, bf16[2080,128]{1,0:T(8,128)(2,1)}, u32[]{:S(2)}, u32[]{:S(2)}) collective-permute-start(bf16[2080,128]{1,0:T(8,128)(2,1)S(1)} %get-tuple-element.97.w0.refs_9_.refs_7_), channel_id=1, source_target_pairs={{0,1},{1,0},{2,3},{3,2},{4,5},{5,4},{6,7},{7,6},{8,9},{9,8},{10,11... | collective-permute-start | bytes 1597448 | tf_op jit(solution)/shard_map/ppermute | solution.py:45
  11.0 11.3 %collective-permute-start.1 = (bf16[1056,128]{1,0:T(8,128)(2,1)}, bf16[1056,128]{1,0:T(8,128)(2,1)}, u32[]{:S(2)}, u32[]{:S(2)}) collective-permute-start(bf16[1056,128]{1,0:T(8,128)(2,1)} %get-tuple-element.95), channel_id=1, source_target_pairs={{0,2},{1,3},{2,0},{3,1},{4,6},{5,7},{6,4},{7,5},{8,10},{9,11},{10,... | collective-permute-start | bytes 811016 | tf_op jit(solution)/shard_map/ppermute | solution.py:45
  11.1 14.5 %collective-permute-start.2 = (bf16[1056,128]{1,0:T(8,128)(2,1)}, bf16[1056,128]{1,0:T(8,128)(2,1)}, u32[]{:S(2)}, u32[]{:S(2)}) collective-permute-start(bf16[1056,128]{1,0:T(8,128)(2,1)} %get-tuple-element.96), channel_id=1, source_target_pairs={{0,3},{1,2},{2,1},{3,0},{4,7},{5,6},{6,5},{7,4},{8,11},{9,10},{10,... | collective-permute-start | bytes 811016 | tf_op jit(solution)/shard_map/ppermute | solution.py:45
  25.6 14.4 %collective-permute-start.9 = (bf16[2080,128]{1,0:T(8,128)(2,1)S(1)}, bf16[2080,128]{1,0:T(8,128)(2,1)S(1)}, u32[]{:S(2)}, u32[]{:S(2)}) collective-permute-start(bf16[2080,128]{1,0:T(8,128)(2,1)S(1)} %shard_map.205.w0), channel_id=1, source_target_pairs={{0,2},{1,3},{2,0},{3,1},{4,6},{5,7},{6,4},{7,5},{8,10},{9,11},{10,... | collective-permute-start | bytes 1597448 | tf_op jit(solution)/shard_map/ppermute | solution.py:45
  28.9 26.1 %collective-permute-start.12 = (bf16[2080,128]{1,0:T(8,128)(2,1)S(1)}, bf16[2080,128]{1,0:T(8,128)(2,1)S(1)}, u32[]{:S(2)}, u32[]{:S(2)}) collective-permute-start(bf16[2080,128]{1,0:T(8,128)(2,1)S(1)} %shard_map.205.w0), channel_id=1, source_target_pairs={{0,1},{1,0},{2,3},{3,2},{4,5},{5,4},{6,7},{7,6},{8,9},{9,8},{10,11... | collective-permute-start | bytes 1597448 | tf_op jit(solution)/shard_map/ppermute | solution.py:45
  40.0 15.1 %collective-permute-start.13 = (bf16[2080,128]{1,0:T(8,128)(2,1)S(1)}, bf16[2080,128]{1,0:T(8,128)(2,1)S(1)}, u32[]{:S(2)}, u32[]{:S(2)}) collective-permute-start(bf16[2080,128]{1,0:T(8,128)(2,1)S(1)} %collective-permute-done.9.w2), channel_id=1, source_target_pairs={{0,1},{1,0},{2,3},{3,2},{4,5},{5,4},{6,7},{7,6},{8,9},{9,8},{10,11... | collective-permute-start | bytes 1597448 | tf_op jit(solution)/shard_map/ppermute | solution.py:45
  40.0 15.0 %collective-permute-start.8 = (bf16[1056,128]{1,0:T(8,128)(2,1)S(1)}, bf16[1056,128]{1,0:T(8,128)(2,1)S(1)}, u32[]{:S(2)}, u32[]{:S(2)}) collective-permute-start(bf16[1056,128]{1,0:T(8,128)(2,1)S(1)} %get-tuple-element.100), channel_id=1, source_target_pairs={{0,1},{1,0},{2,3},{3,2},{4,5},{5,4},{6,7},{7,6},{8,9},{9,8},{10,11... | collective-permute-start | bytes 811016 | tf_op jit(solution)/shard_map/ppermute | solution.py:45
  40.5 14.5 %collective-permute-start.10 = (bf16[1056,128]{1,0:T(8,128)(2,1)S(1)}, bf16[1056,128]{1,0:T(8,128)(2,1)S(1)}, u32[]{:S(2)}, u32[]{:S(2)}) collective-permute-start(bf16[1056,128]{1,0:T(8,128)(2,1)S(1)} %get-tuple-element.104), channel_id=1, source_target_pairs={{0,2},{1,3},{2,0},{3,1},{4,6},{5,7},{6,4},{7,5},{8,10},{9,11},{10,... | collective-permute-start | bytes 811016 | tf_op jit(solution)/shard_map/ppermute | solution.py:45
  41.6 13.5 %collective-permute-start.11 = (bf16[1056,128]{1,0:T(8,128)(2,1)S(1)}, bf16[1056,128]{1,0:T(8,128)(2,1)S(1)}, u32[]{:S(2)}, u32[]{:S(2)}) collective-permute-start(bf16[1056,128]{1,0:T(8,128)(2,1)S(1)} %get-tuple-element.105), channel_id=1, source_target_pairs={{0,3},{1,2},{2,1},{3,0},{4,7},{5,6},{6,5},{7,4},{8,11},{9,10},{10,... | collective-permute-start | bytes 811016 | tf_op jit(solution)/shard_map/ppermute | solution.py:45
  68.6 26.0 %collective-permute-start.14 = (bf16[2,128,2176]{2,1,0:T(8,128)(2,1)}, bf16[2,128,2176]{2,1,0:T(8,128)(2,1)S(1)}, u32[]{:S(2)}, u32[]{:S(2)}) collective-permute-start(bf16[2,128,2176]{2,1,0:T(8,128)(2,1)} %get-tuple-element.113), channel_id=1, source_target_pairs={{0,1},{1,0},{2,3},{3,2},{4,5},{5,4},{6,7},{7,6},{8,9},{9,8},{10,11... | collective-permute-start | bytes 3342344 | tf_op jit(solution)/shard_map/ppermute | solution.py:45
  94.5 13.7 %collective-permute-start.16 = (bf16[2,2,272,512]{3,2,1,0:T(8,128)(2,1)}, bf16[2,2,272,512]{3,2,1,0:T(8,128)(2,1)S(1)}, u32[]{:S(2)}, u32[]{:S(2)}) collective-permute-start(bf16[2,2,272,512]{3,2,1,0:T(8,128)(2,1)} %get-tuple-element.120), channel_id=1, source_target_pairs={{0,1},{1,0},{2,3},{3,2},{4,5},{5,4},{6,7},{7,6},{8,9},{9,8},{10,11... | collective-permute-start | bytes 3342344 | tf_op jit(solution)/shard_map/ppermute | solution.py:45
  94.7 15.1 %collective-permute-start.15 = (bf16[128,2176]{1,0:T(8,128)(2,1)S(1)}, bf16[128,2176]{1,0:T(8,128)(2,1)S(1)}, u32[]{:S(2)}, u32[]{:S(2)}) collective-permute-start(bf16[128,2176]{1,0:T(8,128)(2,1)S(1)} %fusion.1.refs_8_), channel_id=1, source_target_pairs={{0,2},{1,3},{2,0},{3,1},{4,6},{5,7},{6,4},{7,5},{8,10},{9,11},{10,... | collective-permute-start | bytes 1671176 | tf_op jit(solution)/shard_map/ppermute | solution.py:45
  111.9 14.3 %collective-permute-start.17 = (bf16[2,272,512]{2,1,0:T(8,128)(2,1)S(1)}, bf16[2,272,512]{2,1,0:T(8,128)(2,1)S(1)}, u32[]{:S(2)}, u32[]{:S(2)}) collective-permute-start(bf16[2,272,512]{2,1,0:T(8,128)(2,1)S(1)} %get-tuple-element.124), channel_id=1, source_target_pairs={{0,2},{1,3},{2,0},{3,1},{4,6},{5,7},{6,4},{7,5},{8,10},{9,11},{10,... | collective-permute-start | bytes 1671176 | tf_op jit(solution)/shard_map/ppermute | solution.py:45
  113.0 12.6 %collective-permute-start.18 = (bf16[64,2176]{1,0:T(8,128)(2,1)S(1)}, bf16[64,2176]{1,0:T(8,128)(2,1)S(1)}, u32[]{:S(2)}, u32[]{:S(2)}) collective-permute-start(bf16[64,2176]{1,0:T(8,128)(2,1)S(1)} %get-tuple-element.126), channel_id=1, source_target_pairs={{0,4},{4,0},{8,12},{12,8},{16,20},{20,16},{24,28},{28,24},{1,5},{5... | collective-permute-start | bytes 835592 | tf_op jit(solution)/shard_map/ppermute | solution.py:45
  129.0 10.4 %collective-permute-start.20 = (bf16[2,128,2176]{2,1,0:T(8,128)(2,1)S(1)}, bf16[2,128,2176]{2,1,0:T(8,128)(2,1)S(1)}, u32[]{:S(2)}, u32[]{:S(2)}) collective-permute-start(bf16[2,128,2176]{2,1,0:T(8,128)(2,1)S(1)} %get-tuple-element.133), channel_id=1, source_target_pairs={{0,1},{1,0},{2,3},{3,2},{4,5},{5,4},{6,7},{7,6},{8,9},{9,8},{10,11... | collective-permute-start | bytes 3342344 | tf_op jit(solution)/shard_map/ppermute | solution.py:45
  129.1 9.1 %collective-permute-start.19 = (bf16[272,512]{1,0:T(8,128)(2,1)S(1)}, bf16[272,512]{1,0:T(8,128)(2,1)S(1)}, u32[]{:S(2)}, u32[]{:S(2)}) collective-permute-start(bf16[272,512]{1,0:T(8,128)(2,1)S(1)} %get-tuple-element.130), channel_id=1, source_target_pairs={{0,4},{4,0},{8,12},{12,8},{16,20},{20,16},{24,28},{28,24},{1,5},{5... | collective-permute-start | bytes 835592 | tf_op jit(solution)/shard_map/ppermute | solution.py:45
  140.3 14.4 %collective-permute-start.25 = (bf16[272,512]{1,0:T(8,128)(2,1)S(1)}, bf16[272,512]{1,0:T(8,128)(2,1)S(1)}, u32[]{:S(2)}, u32[]{:S(2)}) collective-permute-start(bf16[272,512]{1,0:T(8,128)(2,1)S(1)} %get-tuple-element.142), channel_id=1, source_target_pairs={{0,8},{4,12},{8,0},{12,4},{16,24},{20,28},{24,16},{28,20},{1,9},{5... | collective-permute-start | bytes 835592 | tf_op jit(solution)/shard_map/ppermute | solution.py:45
  142.0 12.8 %collective-permute-start.26 = (bf16[64,2176]{1,0:T(8,128)(2,1)S(1)}, bf16[64,2176]{1,0:T(8,128)(2,1)S(1)}, u32[]{:S(2)}, u32[]{:S(2)}) collective-permute-start(bf16[64,2176]{1,0:T(8,128)(2,1)S(1)} %get-tuple-element.144), channel_id=1, source_target_pairs={{0,4},{4,0},{8,12},{12,8},{16,20},{20,16},{24,28},{28,24},{1,5},{5... | collective-permute-start | bytes 835592 | tf_op jit(solution)/shard_map/ppermute | solution.py:45
  142.5 12.3 %collective-permute-start.27 = (bf16[64,2176]{1,0:T(8,128)(2,1)S(1)}, bf16[64,2176]{1,0:T(8,128)(2,1)S(1)}, u32[]{:S(2)}, u32[]{:S(2)}) collective-permute-start(bf16[64,2176]{1,0:T(8,128)(2,1)S(1)} %get-tuple-element.145), channel_id=1, source_target_pairs={{0,2},{1,3},{2,0},{3,1},{4,6},{5,7},{6,4},{7,5},{8,10},{9,11},{10,... | collective-permute-start | bytes 835592 | tf_op jit(solution)/shard_map/ppermute | solution.py:45
  143.9 12.8 %collective-permute-start.28 = (bf16[64,2176]{1,0:T(8,128)(2,1)S(1)}, bf16[64,2176]{1,0:T(8,128)(2,1)S(1)}, u32[]{:S(2)}, u32[]{:S(2)}) collective-permute-start(bf16[64,2176]{1,0:T(8,128)(2,1)S(1)} %get-tuple-element.146), channel_id=1, source_target_pairs={{0,6},{1,7},{2,4},{3,5},{4,2},{5,3},{6,0},{7,1},{8,14},{9,15},{10,... | collective-permute-start | bytes 835592 | tf_op jit(solution)/shard_map/ppermute | solution.py:61
  145.5 13.7 %collective-permute-start.29 = (bf16[64,2176]{1,0:T(8,128)(2,1)S(1)}, bf16[64,2176]{1,0:T(8,128)(2,1)S(1)}, u32[]{:S(2)}, u32[]{:S(2)}) collective-permute-start(bf16[64,2176]{1,0:T(8,128)(2,1)S(1)} %get-tuple-element.148), channel_id=1, source_target_pairs={{0,16},{4,20},{8,24},{12,28},{16,0},{20,4},{24,8},{28,12},{1,17},{... | collective-permute-start | bytes 835592 | tf_op jit(solution)/shard_map/ppermute | solution.py:45
  160.7 18.4 %collective-permute-start.30 = (bf16[272,512]{1,0:T(8,128)(2,1)S(1)}, bf16[272,512]{1,0:T(8,128)(2,1)S(1)}, u32[]{:S(2)}, u32[]{:S(2)}) collective-permute-start(bf16[272,512]{1,0:T(8,128)(2,1)S(1)} %get-tuple-element.151), channel_id=1, source_target_pairs={{0,16},{4,20},{8,24},{12,28},{16,0},{20,4},{24,8},{28,12},{1,17},{... | collective-permute-start | bytes 835592 | tf_op jit(solution)/shard_map/ppermute | solution.py:45
  160.9 18.2 %collective-permute-start.31 = (bf16[64,2176]{1,0:T(8,128)(2,1)S(1)}, bf16[64,2176]{1,0:T(8,128)(2,1)S(1)}, u32[]{:S(2)}, u32[]{:S(2)}) collective-permute-start(bf16[64,2176]{1,0:T(8,128)(2,1)S(1)} %get-tuple-element.153), channel_id=1, source_target_pairs={{0,8},{4,12},{8,0},{12,4},{16,24},{20,28},{24,16},{28,20},{1,9},{5... | collective-permute-start | bytes 835592 | tf_op jit(solution)/shard_map/ppermute | solution.py:45
  163.8 9.2 %collective-permute-start.23 = (bf16[1024,128]{1,0:T(8,128)(2,1)S(1)}, bf16[1024,128]{1,0:T(8,128)(2,1)S(1)}, u32[]{:S(2)}, u32[]{:S(2)}) collective-permute-start(bf16[1024,128]{1,0:T(8,128)(2,1)S(1)} %copy-done.46), channel_id=1, source_target_pairs={{0,2},{1,3},{2,0},{3,1},{4,6},{5,7},{6,4},{7,5},{8,10},{9,11},{10,... | collective-permute-start | bytes 786440 | tf_op jit(solution)/shard_map/ppermute | solution.py:45
  165.3 12.4 %collective-permute-start.24 = (bf16[1024,128]{1,0:T(8,128)(2,1)S(1)}, bf16[1024,128]{1,0:T(8,128)(2,1)S(1)}, u32[]{:S(2)}, u32[]{:S(2)}) collective-permute-start(bf16[1024,128]{1,0:T(8,128)(2,1)S(1)} %copy-done.45), channel_id=1, source_target_pairs={{0,3},{1,2},{2,1},{3,0},{4,7},{5,6},{6,5},{7,4},{8,11},{9,10},{10,... | collective-permute-start | bytes 786440 | tf_op jit(solution)/shard_map/ppermute | solution.py:45
  181.6 15.2 %collective-permute-start.32 = (bf16[64,2176]{1,0:T(8,128)(2,1)S(1)}, bf16[64,2176]{1,0:T(8,128)(2,1)S(1)}, u32[]{:S(2)}, u32[]{:S(2)}) collective-permute-start(bf16[64,2176]{1,0:T(8,128)(2,1)S(1)} %get-tuple-element.155), channel_id=1, source_target_pairs={{0,16},{4,20},{8,24},{12,28},{16,0},{20,4},{24,8},{28,12},{1,17},{... | collective-permute-start | bytes 835592 | tf_op jit(solution)/shard_map/ppermute | solution.py:45
  181.7 16.4 %collective-permute-start.34 = (bf16[64,2176]{1,0:T(8,128)(2,1)S(1)}, bf16[64,2176]{1,0:T(8,128)(2,1)S(1)}, u32[]{:S(2)}, u32[]{:S(2)}) collective-permute-start(bf16[64,2176]{1,0:T(8,128)(2,1)S(1)} %get-tuple-element.160.refs_1_), channel_id=1, source_target_pairs={{0,4},{4,0},{8,12},{12,8},{16,20},{20,16},{24,28},{28,24},{1,5},{5... | collective-permute-start | bytes 835592 | tf_op jit(solution)/shard_map/ppermute | solution.py:45
  182.3 15.8 %collective-permute-start.37 = (bf16[512,256]{1,0:T(8,128)(2,1)S(1)}, bf16[512,256]{1,0:T(8,128)(2,1)S(1)}, u32[]{:S(2)}, u32[]{:S(2)}) collective-permute-start(bf16[512,256]{1,0:T(8,128)(2,1)S(1)} %get-tuple-element.165.refs_1_), channel_id=1, source_target_pairs={{0,6},{1,7},{2,4},{3,5},{4,2},{5,3},{6,0},{7,1},{8,14},{9,15},{10,... | collective-permute-start | bytes 786440 | tf_op jit(solution)/shard_map/ppermute | solution.py:61
  184.6 14.0 %collective-permute-start.36 = (bf16[512,256]{1,0:T(8,128)(2,1)S(1)}, bf16[512,256]{1,0:T(8,128)(2,1)S(1)}, u32[]{:S(2)}, u32[]{:S(2)}) collective-permute-start(bf16[512,256]{1,0:T(8,128)(2,1)S(1)} %get-tuple-element.165.refs_1_), channel_id=1, source_target_pairs={{0,2},{1,3},{2,0},{3,1},{4,6},{5,7},{6,4},{7,5},{8,10},{9,11},{10,... | collective-permute-start | bytes 786440 | tf_op jit(solution)/shard_map/ppermute | solution.py:45
  185.2 17.2 %collective-permute-start.35 = (bf16[512,256]{1,0:T(8,128)(2,1)S(1)}, bf16[512,256]{1,0:T(8,128)(2,1)S(1)}, u32[]{:S(2)}, u32[]{:S(2)}) collective-permute-start(bf16[512,256]{1,0:T(8,128)(2,1)S(1)} %get-tuple-element.165.refs_1_), channel_id=1, source_target_pairs={{0,4},{4,0},{8,12},{12,8},{16,20},{20,16},{24,28},{28,24},{1,5},{5... | collective-permute-start | bytes 786440 | tf_op jit(solution)/shard_map/ppermute | solution.py:45
  197.4 10.5 %collective-permute-start.33 = (bf16[64,2176]{1,0:T(8,128)(2,1)S(1)}, bf16[64,2176]{1,0:T(8,128)(2,1)S(1)}, u32[]{:S(2)}, u32[]{:S(2)}) collective-permute-start(bf16[64,2176]{1,0:T(8,128)(2,1)S(1)} %shard_map.221.refs_1_), channel_id=1, source_target_pairs={{0,4},{4,0},{8,12},{12,8},{16,20},{20,16},{24,28},{28,24},{1,5},{5... | collective-permute-start | bytes 835592 | tf_op jit(solution)/shard_map/ppermute | solution.py:45
  (59 other events, 348.7 us)
